TPU v7x, 32 devices: a whole 2x2x4 slice. The times are simulated.
32 devices in a mesh: rep: 4 (over y, core), fsdp: 8 (over z, x).
Axes of the slice: x: 2, y: 2, z: 4, core: 2. Of those that a mesh axis runs over, the one named last changes fastest.
Arguments:
- grads: bfloat16 [4, 2, 512, 8192], P('rep', None, 'fsdp'), may hold values from -0.29882812 to 0.29882812
- left_stat: float32 [32, 512, 512], P(('rep', 'fsdp')), may hold values from -6 to 6
- right_stat: float32 [32, 512, 512], P(('rep', 'fsdp')), may hold values from -6 to 6
- left_root: bfloat16 [32, 512, 512], P(('rep', 'fsdp')), may hold values from -1 to 3
- right_root: bfloat16 [32, 512, 512], P(('rep', 'fsdp')), may hold values from -1 to 3
- accum: float32 [32, 512, 512], P(('rep', 'fsdp')), may hold values from 0.01 to 1
Outputs:
- update: bfloat16 [2, 512, 8192], P(None, 'fsdp', 'rep')
- left_new: float32 [32, 512, 512], P(('rep', 'fsdp'))
- right_new: float32 [32, 512, 512], P(('rep', 'fsdp'))
- accum_new: float32 [32, 512, 512], P(('rep', 'fsdp'))
All inputs are finite; a program needn't handle non-finite values.
Results may differ from a plain program's by a relative error of at most 0.02.
Values may be sent and summed in bfloat16 or wider, within the bound.
No kernel may reach another device: no remote copies, remote signals or barrier semaphores. Data moves between devices by JAX's collectives and lax.ppermute only.
A program may use at most 64 MiB of HBM per device.

v0:
```python
import jax
import jax.numpy as jnp
from jax import lax
from jax.sharding import PartitionSpec as P


def body(grads, left_stat, right_stat, left_root, right_root, accum):
    rep_count = lax.axis_size("rep")
    fsdp_count = lax.axis_size("fsdp")
    slabs = grads.shape[1]
    rows_local = grads.shape[2]
    width = grads.shape[3]
    block = rows_local * fsdp_count
    bcols = width // block
    owned = left_stat.shape[0]
    pieces = grads.reshape(slabs, rows_local, bcols, block).transpose(2, 0, 1, 3)
    pieces = pieces.reshape(rep_count, fsdp_count * owned, rows_local, block)
    moved = lax.all_to_all(pieces, "fsdp", split_axis=1, concat_axis=2, tiled=True)
    summed = lax.psum_scatter(
        moved.astype(jnp.float32).astype(jnp.bfloat16), "rep", scatter_dimension=0, tiled=True
    ).astype(jnp.float32)
    blocks = summed.reshape(owned, block, block)
    left_new = left_stat + jnp.einsum(
        "kij,klj->kil", blocks, blocks, precision=lax.Precision.HIGHEST
    )
    right_new = right_stat + jnp.einsum(
        "kji,kjl->kil", blocks, blocks, precision=lax.Precision.HIGHEST
    )
    accum_new = accum + blocks * blocks
    adagrad = blocks / jnp.sqrt(accum_new)
    blocks_low = blocks.astype(jnp.bfloat16)
    half = jnp.einsum(
        "kij,kjl->kil", left_root, blocks_low, preferred_element_type=jnp.float32
    ).astype(jnp.bfloat16)
    precond = jnp.einsum("kij,kjl->kil", half, right_root, preferred_element_type=jnp.float32)
    ada_sq = jnp.sum(adagrad * adagrad, axis=(1, 2), keepdims=True)
    pre_sq = jnp.sum(precond * precond, axis=(1, 2), keepdims=True)
    ratio = jnp.sqrt(ada_sq) / jnp.sqrt(pre_sq + 1e-06)
    scaled = (ratio * precond).astype(jnp.bfloat16)
    returned = lax.all_to_all(scaled, "fsdp", split_axis=1, concat_axis=0, tiled=True)
    local_cols = bcols // rep_count
    update = returned.reshape(local_cols, slabs, rows_local, block).transpose(1, 2, 0, 3)
    update = update.reshape(slabs, rows_local, local_cols * block)
    return (update, left_new, right_new, accum_new)


def solution(mesh):
    return jax.shard_map(
        body,
        mesh=mesh,
        in_specs=(
            P("rep", None, "fsdp", None),
            P(("rep", "fsdp"), None, None),
            P(("rep", "fsdp"), None, None),
            P(("rep", "fsdp"), None, None),
            P(("rep", "fsdp"), None, None),
            P(("rep", "fsdp"), None, None),
        ),
        out_specs=(
            P(None, "fsdp", "rep"),
            P(("rep", "fsdp"), None, None),
            P(("rep", "fsdp"), None, None),
            P(("rep", "fsdp"), None, None),
        ),
        check_vma=False,
    )
```

profile of v0, /device:TPU:0, one launch (start us, length us, event | category | flops | bytes accessed | tf_op | source)
XLA Modules:
  0.0 139.6 jit_solution(13782685533890265779)
XLA Ops:
  7.2 0.0 copy-start
  7.2 0.0 reduce-scatter.2.cloned.1.call-start
  7.2 2.5 %copy.24 = bf16[16,8,16,512]{3,2,1,0:T(8,128)(2,1)S(1)} copy(bf16[16,8,16,512]{3,1,2,0:T(8,128)(2,1)} %bitcast.62) | data formatting | bytes 4194304
  9.7 0.2 bitcast_bitcast_fusion
  9.9 1.2 copy.17
  11.1 0.2 copy.18
  11.3 55.3 %all_to_all.21 = bf16[4,8,64,512]{3,2,0,1:T(8,128)(2,1)S(1)} all-to-all(bf16[4,8,64,512]{3,2,0,1:T(8,128)(2,1)S(1)} %copy.18), channel_id=1, replica_groups=mesh['rep'=4,'fsdp'=8] {'fsdp'}, dimensions={1} | all-to-all | bytes 4194304 | tf_op jit(solution)/shard_map/all_to_all | solution.py:18
  66.6 1.6 %copy.19 = bf16[4,8,64,512]{3,2,1,0:T(8,128)(2,1)} copy(bf16[4,8,64,512]{3,2,0,1:T(8,128)(2,1)S(1)} %all_to_all.21) | data formatting | bytes 4194304 | tf_op jit(solution)/shard_map/all_to_all | solution.py:18
  68.1 0.0 copy-start.2
  68.1 0.0 reduce-scatter.2.cloned.1.call-update
  68.2 30.6 %reduce-scatter.2.cloned.1.call-done = bf16[1,1,512,512]{3,2,0,1:T(8,128)(2,1)} async-done(((bf16[4,1,512,512]{3,2,0,1:T(8,128)(2,1)}), bf16[1,1,512,512]{3,2,0,1:T(8,128)(2,1)}) %reduce-scatter.2.cloned.1.call-update) | async-done | bytes 524304 | tf_op jit(solution)/shard_map/reduce_scatter | solution.py:19
  98.8 0.0 copy-done
  98.8 0.0 copy-start.1
  98.8 2.7 %multiply_reduce_fusion = (f32[]{:T(128)}, f32[512,512]{1,0:T(8,128)S(1)}) fusion(bf16[1,512,512]{2,1,0:T(8,128)(2,1)S(1)} %copy-done, bf16[1,1,512,512]{3,2,0,1:T(8,128)(2,1)} %reduce-scatter.2.cloned.1.call-done, bf16[1,512,512]{2,1,0:T(8,128)(2,1)} %param.9), kind=kOutput, calls=%fused_computation.13 | convolution fusion | flops 537657344 | bytes 2621444 | tf_op jit(solution)/shard_map/kij,kjl->kil/dot_general | solution.py:35
  102.2 0.0 copy-done.2
  102.2 0.0 copy-done.1
  102.2 1.8 %fusion.5 = (f32[]{:T(128)}, f32[1,512,512]{2,1,0:T(8,128)}) fusion(bf16[1,1,512,512]{3,2,0,1:T(8,128)(2,1)S(1)} %copy-done.1, f32[1,512,512]{2,1,0:T(8,128)S(1)} %copy-done.2), kind=kLoop, calls=%fused_computation.11 | loop fusion | flops 1572863 | bytes 2621444 | tf_op jit(solution)/shard_map/reduce_sum | solution.py:36
  104.7 0.1 fusion.6
  104.8 0.8 copy.26
  105.6 0.5 broadcast.3
  106.1 3.8 %reduce.3 = bf16[512,512]{1,0:T(8,128)(2,1)S(1)} reduce(bf16[512,1,512]{2,1,0:T(2,128)(2,1)S(1)} %bitcast.60, bf16[]{:T(256)} %broadcast.3), dimensions={1}, to_apply=%bitcast.54.reduce_sub_computation | reduce | bytes 1048578
  110.0 1.2 reshape.97
  111.1 0.0 copy-start.3
  111.1 5.7 %all-to-all-start.1 = ((bf16[8,2,16384]{2,1,0:T(2,128)(2,1)}), bf16[8,2,16384]{2,1,0:T(2,128)(2,1)S(1)}, u32[]{:S(2)}, u32[]{:S(2)}) async-start(bf16[8,2,16384]{2,1,0:T(2,128)(2,1)} %reshape.97), calls=%async_computation.2 | async-start | bytes 1048576 | tf_op jit(solution)/shard_map/all_to_all | solution.py:40
  116.8 2.7 %fusion = f32[1,512,512]{2,1,0:T(8,128)} fusion(f32[1,512,512]{2,1,0:T(8,128)} %param.7, bf16[1,1,512,512]{3,2,0,1:T(8,128)(2,1)S(1)} %copy-done.1), kind=kOutput, calls=%fused_computation.5 | convolution fusion | flops 268697600 | bytes 2621440 | tf_op jit(solution)/shard_map/kij,klj->kil/dot_general | solution.py:23
  119.5 0.0 copy-done.3
  119.5 1.4 %fusion.1 = f32[1,512,512]{2,1,0:T(8,128)} fusion(f32[1,512,512]{2,1,0:T(8,128)S(1)} %copy-done.3, bf16[1,1,512,512]{3,2,0,1:T(8,128)(2,1)S(1)} %copy-done.1), kind=kOutput, calls=%fused_computation.6 | convolution fusion | flops 268697600 | bytes 2621440 | tf_op jit(solution)/shard_map/kji,kjl->kil/dot_general | solution.py:26
  120.9 10.4 %all-to-all-done.1 = bf16[8,2,16384]{2,1,0:T(2,128)(2,1)S(1)} async-done(((bf16[8,2,16384]{2,1,0:T(2,128)(2,1)}), bf16[8,2,16384]{2,1,0:T(2,128)(2,1)S(1)}, u32[]{:S(2)}, u32[]{:S(2)}) %all-to-all-start.1) | async-done | bytes 524320 | tf_op jit(solution)/shard_map/all_to_all | solution.py:40
  131.3 0.5 reshape.98
  131.8 0.1 copy.22
  131.9 0.9 copy.23
Async XLA Ops:
  7.2 91.6 %copy-start = (bf16[1,512,512]{2,1,0:T(8,128)(2,1)S(1)}, bf16[1,512,512]{2,1,0:T(8,128)(2,1)}, u32[]{:S(2)}) copy-start(bf16[1,512,512]{2,1,0:T(8,128)(2,1)} %param.10) | copy-start | bytes 1572868
  7.2 91.6 %reduce-scatter.2.cloned.1.call-start = ((), (), s32[]{:S(2)}) async-start(), calls=%async_computation.3 | async-start | bytes 2621440 | tf_op jit(solution)/shard_map/reduce_scatter | solution.py:19
  68.1 34.0 %copy-start.2 = (f32[1,512,512]{2,1,0:T(8,128)S(1)}, f32[1,512,512]{2,1,0:T(8,128)}, u32[]{:S(2)}) copy-start(f32[1,512,512]{2,1,0:T(8,128)} %param.11) | copy-start | bytes 3145732
  98.8 3.4 %copy-start.1 = (bf16[1,1,512,512]{3,2,0,1:T(8,128)(2,1)S(1)}, bf16[1,1,512,512]{3,2,0,1:T(8,128)(2,1)}, u32[]{:S(2)}) copy-start(bf16[1,1,512,512]{3,2,0,1:T(8,128)(2,1)} %reduce-scatter.2.cloned.1.call-done) | copy-start | bytes 1572868
  111.1 8.3 %copy-start.3 = (f32[1,512,512]{2,1,0:T(8,128)S(1)}, f32[1,512,512]{2,1,0:T(8,128)}, u32[]{:S(2)}) copy-start(f32[1,512,512]{2,1,0:T(8,128)} %param.8) | copy-start | bytes 3145732
  111.1 20.1 %all-to-all-start.1 = ((bf16[8,2,16384]{2,1,0:T(2,128)(2,1)}), bf16[8,2,16384]{2,1,0:T(2,128)(2,1)S(1)}, u32[]{:S(2)}, u32[]{:S(2)}) async-start(bf16[8,2,16384]{2,1,0:T(2,128)(2,1)} %reshape.97), calls=%async_computation.2 | async-start | bytes 1048576 | tf_op jit(solution)/shard_map/all_to_all | solution.py:40
Sparse Core Ops, SparseCore 0:
  68.3 30.4 reduce-scatter.1
where the time goes:
time: 140 us
  blocking collectives  55.3 us (40%)
  waiting for transfers between devices  41 us (29%)
  between operations  15.5 us (11%)
  local copies, waits for them, and re-layouts  9.61 us (7%)
  matrix products  6.81 us (5%)
  other arithmetic  5.74 us (4%)
  starting transfers between devices  5.69 us (4%)
    all_to_all x1, blocking collectives, body(): lax.all_to_all(pieces, 'fsdp', split_axis=1, concat_axis=2, tiled=True)  55.3 us
    reduce_scatter x1, waiting for transfers between devices, body(): lax.psum_scatter(moved.astype(jnp.float32).astype(jnp.bfloat16), 'rep', s...  30.6 us
    all_to_all x1, waiting for transfers between devices, body(): lax.all_to_all(scaled, 'fsdp', split_axis=1, concat_axis=0, tiled=True)  10.4 us
    all_to_all x1, starting transfers between devices, body(): lax.all_to_all(scaled, 'fsdp', split_axis=1, concat_axis=0, tiled=True)  5.65 us
    unnamed x13, local copies, waits for them, and re-layouts  4.82 us
    unnamed x1, other arithmetic  3.82 us
  transfers between devices with their start and end apart: 2, of which 2 were waited for; matrix products, arithmetic and copies ran while one was open for 3% of the time, Pallas kernels for 0%

commit v1 on v0

v1 whole, which is shorter than its diff:
```python
import functools

import jax
import jax.numpy as jnp
from jax import lax
from jax.experimental import pallas as pl
from jax.experimental.pallas import tpu as pltpu
from jax.sharding import PartitionSpec as P

MIB = 1024 * 1024
ANY = pl.BlockSpec(memory_space=pl.ANY)
VMEM = pl.BlockSpec(memory_space=pltpu.VMEM)


def swap(x, axis, bit):
    n = lax.axis_size(axis)
    return lax.ppermute(x, axis, [(i, i ^ bit) for i in range(n)])


def pick_kernel(fsdp_count, other, grads, half0, half1, sem):
    slabs, width = grads.shape[1], grads.shape[3]
    groups, _, _, cols = half0.shape
    block = 2 * cols
    low = lax.rem(lax.axis_index("rep"), 2)
    low = 1 - low if other else low
    copies = []
    for h, out in enumerate((half0, half1)):
        for g in range(groups):
            for f in range(fsdp_count):
                column = (2 * g + low) * (fsdp_count // slabs) + f // slabs
                start = pl.multiple_of(column * block + h * cols, cols)
                copies.append(
                    pltpu.make_async_copy(
                        grads.at[0, f % slabs, :, pl.ds(start, cols)], out.at[g, f], sem
                    )
                )
    for copy in copies:
        copy.start()
    for copy in copies:
        copy.wait()


def pick(grads, other, rep_count, fsdp_count):
    _, slabs, rows, width = grads.shape
    block = rows * fsdp_count
    shape = jax.ShapeDtypeStruct((rep_count // 2, fsdp_count, rows, block // 2), grads.dtype)
    return pl.pallas_call(
        functools.partial(pick_kernel, fsdp_count, other),
        out_shape=(shape, shape),
        in_specs=[ANY],
        out_specs=(ANY, ANY),
        scratch_shapes=[pltpu.SemaphoreType.DMA],
        compiler_params=pltpu.CompilerParams(vmem_limit_bytes=4 * MIB),
        cost_estimate=pl.CostEstimate(flops=0, bytes_accessed=2 * MIB, transcendentals=0),
        name="pick_other" if other else "pick_own",
    )(grads)


def place(z, x, k, other, rows):
    at = 2 * jnp.bitwise_xor(z, k) + (1 - x if other else x)
    return pl.ds(pl.multiple_of(at * rows, rows), rows)


def main_kernel(peers, *refs):
    firsts = refs[:peers]
    crossed = refs[peers]
    seconds = refs[peers + 1 : 2 * peers + 1]
    left_root, right_root, accum = refs[2 * peers + 1 : 2 * peers + 4]
    outs = refs[2 * peers + 4 :]
    sends, own0, away1, own1, block_out = outs[: peers - 1], *outs[peers - 1 : peers + 3]
    block, lroot, rroot, acc, sems = outs[peers + 3 :]
    rows, cols = firsts[0].shape[1:]
    me = lax.axis_index("fsdp")
    z, x = me // 2, lax.rem(me, 2)

    lcopy = pltpu.make_async_copy(left_root.at[0], lroot, sems.at[1])
    rcopy = pltpu.make_async_copy(right_root.at[0], rroot, sems.at[2])
    acopy = pltpu.make_async_copy(accum.at[0], acc, sems.at[3])
    copies = []
    for k in range(peers):
        here, there = place(z, x, k, False, rows), place(z, x, k, True, rows)
        for src, to, h in (
            (firsts[k].at[x], here, 0),
            (crossed.at[k], there, 0),
            (seconds[k].at[0], here, 1),
            (seconds[k].at[1], there, 1),
        ):
            copies.append(
                pltpu.make_async_copy(src, block.at[to, pl.ds(h * cols, cols)], sems.at[0])
            )
    lcopy.start()
    for copy in copies:
        copy.start()
    rcopy.start()
    acopy.start()
    lcopy.wait()
    for copy in copies:
        copy.wait()
    b = block[...]
    half = jnp.dot(lroot[...], b, preferred_element_type=jnp.float32).astype(jnp.bfloat16)
    rcopy.wait()
    precond = jnp.dot(half, rroot[...], preferred_element_type=jnp.float32)
    acopy.wait()
    wide = b.astype(jnp.float32)
    square = wide * wide
    ada_sq = jnp.sum(square / (acc[...] + square))
    pre_sq = jnp.sum(precond * precond)
    ratio = jnp.sqrt(ada_sq) / jnp.sqrt(pre_sq + 1e-06)
    block_out[...] = b
    lroot[...] = (ratio * precond).astype(jnp.bfloat16)
    lo, hi = pl.ds(0, cols), pl.ds(cols, cols)
    for k in range(peers):
        target = own0 if k == 0 else sends[k - 1]
        for xx in range(2):
            at = 2 * jnp.bitwise_xor(z, k) + xx
            target[xx] = lroot[pl.ds(pl.multiple_of(at * rows, rows), rows), lo]
    for zz in range(peers):
        at = pl.multiple_of((2 * zz + x) * rows, rows)
        own1[zz] = lroot[pl.ds(at, rows), hi]
        at = pl.multiple_of((2 * zz + 1 - x) * rows, rows)
        away1[zz] = lroot[pl.ds(at, rows), hi]


def precondition(firsts, crossed, seconds, left_root, right_root, accum):
    peers = len(firsts)
    side = left_root.shape[1]
    pair = jax.ShapeDtypeStruct(firsts[0].shape, jnp.bfloat16)
    line = jax.ShapeDtypeStruct(crossed.shape, jnp.bfloat16)
    outs = pl.pallas_call(
        functools.partial(main_kernel, peers),
        out_shape=(pair,) * peers + (line, line, jax.ShapeDtypeStruct((side, side), jnp.bfloat16)),
        in_specs=[ANY] * (2 * peers + 4),
        out_specs=(VMEM,) * (peers + 3),
        scratch_shapes=[
            pltpu.VMEM((side, side), jnp.bfloat16),
            pltpu.VMEM((side, side), jnp.bfloat16),
            pltpu.VMEM((side, side), jnp.bfloat16),
            pltpu.VMEM((side, side), jnp.float32),
            pltpu.SemaphoreType.DMA((4,)),
        ],
        compiler_params=pltpu.CompilerParams(vmem_limit_bytes=16 * MIB),
        cost_estimate=pl.CostEstimate(
            flops=4 * side**3, bytes_accessed=12 * side * side, transcendentals=0
        ),
        name="precondition",
    )(*firsts, crossed, *seconds, left_root, right_root, accum)
    return outs[: peers - 1], outs[peers - 1], outs[peers], outs[peers + 1], outs[peers + 2]


def stats_kernel(block, left, right, accum, left_out, right_out, accum_out):
    b = block[...]
    wide = b.astype(jnp.float32)
    accum_out[0] = accum[0] + wide * wide
    left_out[0] = left[0] + lax.dot_general(
        b, b, (((1,), (1,)), ((), ())), preferred_element_type=jnp.float32
    )
    right_out[0] = right[0] + lax.dot_general(
        b, b, (((0,), (0,)), ((), ())), preferred_element_type=jnp.float32
    )


def statistics(block, left, right, accum):
    shape = jax.ShapeDtypeStruct(left.shape, jnp.float32)
    side = left.shape[1]
    return pl.pallas_call(
        stats_kernel,
        out_shape=(shape,) * 3,
        in_specs=[VMEM] * 4,
        out_specs=(VMEM,) * 3,
        compiler_params=pltpu.CompilerParams(vmem_limit_bytes=20 * MIB),
        cost_estimate=pl.CostEstimate(
            flops=4 * side**3, bytes_accessed=26 * side * side, transcendentals=0
        ),
        name="statistics",
    )(block, left, right, accum)


def assemble_kernel(peers, *refs):
    firsts = refs[:peers]
    crossed = refs[peers]
    seconds = refs[peers + 1 : 2 * peers + 1]
    update, sem = refs[2 * peers + 1 :]
    slabs = update.shape[0]
    rows, cols = firsts[0].shape[1:]
    me = lax.axis_index("fsdp")
    z, x = me // 2, lax.rem(me, 2)
    copies = []
    for k in range(peers):
        for h, other, src in (
            (0, False, firsts[k].at[x]),
            (0, True, crossed.at[k]),
            (1, False, seconds[k].at[0]),
            (1, True, seconds[k].at[1]),
        ):
            owner = 2 * jnp.bitwise_xor(z, k) + (1 - x if other else x)
            start = pl.multiple_of((owner // slabs * 2 + h) * cols, cols)
            copies.append(
                pltpu.make_async_copy(
                    src, update.at[lax.rem(owner, slabs), :, pl.ds(start, cols)], sem
                )
            )
    for copy in copies:
        copy.start()
    for copy in copies:
        copy.wait()


def assemble(firsts, crossed, seconds, shape):
    peers = len(firsts)
    return pl.pallas_call(
        functools.partial(assemble_kernel, peers),
        out_shape=jax.ShapeDtypeStruct(shape, jnp.bfloat16),
        in_specs=[ANY] * (2 * peers + 1),
        out_specs=ANY,
        scratch_shapes=[pltpu.SemaphoreType.DMA],
        compiler_params=pltpu.CompilerParams(vmem_limit_bytes=4 * MIB),
        cost_estimate=pl.CostEstimate(flops=0, bytes_accessed=MIB, transcendentals=0),
        name="assemble",
    )(*firsts, crossed, *seconds)


def pick_one(x, index, axis=0):
    return lax.dynamic_index_in_dim(x, index, axis, keepdims=False)


def far_first(peers):
    return sorted(range(1, peers), reverse=True)


def body(grads, left_stat, right_stat, left_root, right_root, accum):
    rep_count, fsdp_count = lax.axis_size("rep"), lax.axis_size("fsdp")
    peers = fsdp_count // 2
    rep, fsdp = lax.axis_index("rep"), lax.axis_index("fsdp")
    z, x = fsdp // 2, fsdp % 2
    slabs, rows, width = grads.shape[1:]
    order = far_first(peers)

    away = pick(grads, True, rep_count, fsdp_count)
    mine = pick(grads, False, rep_count, fsdp_count)

    def add(a, b):
        return (a.astype(jnp.float32) + b.astype(jnp.float32)).astype(jnp.bfloat16)

    summed = []
    for h in range(2):
        part, kept, bit = swap(away[h], "rep", 1), mine[h], 1
        while 2 * bit < rep_count:
            bit *= 2
            side = (rep // bit) % 2
            part, kept = [
                a.reshape((a.shape[0] // 2, 2) + a.shape[1:]) for a in (part, kept)
            ]
            send = add(pick_one(part, 1 - side, 1), pick_one(kept, 1 - side, 1))
            kept = add(pick_one(part, side, 1), pick_one(kept, side, 1))
            part = swap(send, "rep", bit)
        summed.append((part[0], kept[0]))

    def piece(pair):
        return [a.reshape((peers, 2) + a.shape[1:]) for a in pair]

    part, kept = piece(summed[0])
    firsts = [None] * peers
    firsts[0] = add(pick_one(part, z), pick_one(kept, z))
    for k in order:
        send = add(pick_one(part, z ^ k), pick_one(kept, z ^ k))
        firsts[k] = swap(send, "fsdp", 2 * k)
    crossed = swap(jnp.stack([pick_one(a, 1 - x) for a in firsts]), "fsdp", 1)

    part, kept = piece(summed[1])
    stay = add(pick_one(part, x, 1), pick_one(kept, x, 1))
    come = swap(add(pick_one(part, 1 - x, 1), pick_one(kept, 1 - x, 1)), "fsdp", 1)
    seconds = [None] * peers
    for k in [0] + order:
        pair = jnp.stack([pick_one(stay, z ^ k), pick_one(come, z ^ k)])
        seconds[k] = pair if k == 0 else swap(pair, "fsdp", 2 * k)

    sends, own0, away1, own1, block = precondition(
        firsts, crossed, seconds, left_root, right_root, accum
    )

    firsts = [own0] + [None] * (peers - 1)
    for k in order:
        firsts[k] = swap(sends[k - 1], "fsdp", 2 * k)
    come = swap(away1, "fsdp", 1)
    crossed = swap(jnp.stack([pick_one(a, 1 - x) for a in firsts]), "fsdp", 1)
    seconds = [None] * peers
    for k in [0] + order:
        pair = jnp.stack([pick_one(own1, z ^ k), pick_one(come, z ^ k)])
        seconds[k] = pair if k == 0 else swap(pair, "fsdp", 2 * k)

    left_new, right_new, accum_new = statistics(block, left_stat, right_stat, accum)
    update = assemble(firsts, crossed, seconds, (slabs, rows, width // rep_count))
    return (update, left_new, right_new, accum_new)


def solution(mesh):
    owned = P(("rep", "fsdp"), None, None)
    return jax.shard_map(
        body,
        mesh=mesh,
        in_specs=(P("rep", None, "fsdp", None),) + (owned,) * 5,
        out_specs=(P(None, "fsdp", "rep"),) + (owned,) * 3,
        check_vma=False,
    )
```

time: 140 us -> 62.8 us (0.45)
  blocking collectives: 55.3 us -> 0 us
  starting transfers between devices: 5.69 us -> 27.8 us
  waiting for transfers between devices: 41 us -> 21.7 us
  between operations: 15.5 us -> 0.88 us
  local copies, waits for them, and re-layouts: 9.61 us -> 2.1 us
  matrix products: 6.81 us -> 0 us
  Pallas kernels: 0 us -> 5.97 us
  other arithmetic: 5.74 us -> 4.16 us
    all_to_all x1 -> x0, blocking collectives: 55.3 us -> none  [body(): lax.all_to_all(pieces, 'fsdp', split_axis=1, concat_axis=2, tiled=True)]
    reduce_scatter x1 -> x0, waiting for transfers between devices: 30.6 us -> none  [body(): lax.psum_scatter(moved.astype(jnp.float32).astype(jnp.bfloat16), 'rep', s...]
    ppermute x0 -> x20, starting transfers between devices: none -> 27.8 us  [swap(): return lax.ppermute(x, axis, [(i, i ^ bit) for i in range(n)])]
    ppermute x0 -> x20, waiting for transfers between devices: none -> 21.7 us  [swap(): return lax.ppermute(x, axis, [(i, i ^ bit) for i in range(n)])]
    all_to_all x1 -> x0, waiting for transfers between devices: 10.4 us -> none  [body(): lax.all_to_all(scaled, 'fsdp', split_axis=1, concat_axis=0, tiled=True)]
    dot_general x3 -> x0, matrix products: 6.81 us -> none  [the longest x1 2.71 us: body(): jnp.einsum('kij,kjl->kil', half, right_root, preferred_element_type=jnp.f...]
    pallas_call x0 -> x5, Pallas kernels: none -> 5.97 us  [the longest x1 2.15 us: statistics(): pl.pallas_call(stats_kernel, out_shape=(shape,) * 3, in_specs=[VMEM] * 4,...]
    all_to_all x1 -> x0, starting transfers between devices: 5.65 us -> none  [body(): lax.all_to_all(scaled, 'fsdp', split_axis=1, concat_axis=0, tiled=True)]
  transfers between devices with their start and end apart: 2 -> 20, of which waited for: 2 -> 9; matrix products, arithmetic and copies ran while one was open for 3% -> 7% of each run, Pallas kernels for 0% -> 4%
where the time goes in v1:
time: 62.8 us; the launch traced here: 62.6 us
  starting transfers between devices  27.8 us (44%)
  waiting for transfers between devices  21.7 us (35%)
  Pallas kernels  5.97 us (10%)
  other arithmetic  4.16 us (7%)
  local copies, waits for them, and re-layouts  2.1 us (3%)
  between operations  0.88 us (1%)
    ppermute x20, starting transfers between devices, swap(): return lax.ppermute(x, axis, [(i, i ^ bit) for i in range(n)])  27.8 us
    ppermute x20, waiting for transfers between devices, swap(): return lax.ppermute(x, axis, [(i, i ^ bit) for i in range(n)])  21.7 us
    convert_element_type x5, other arithmetic, add(): return (a.astype(jnp.float32) + b.astype(jnp.float32)).astype(jnp.bfloat16)  4.06 us
    pallas_call x1, Pallas kernels, statistics(): pl.pallas_call(stats_kernel, out_shape=(shape,) * 3, in_specs=[VMEM] * 4,...  2.15 us
    unnamed x14, local copies, waits for them, and re-layouts  2.01 us
    pallas_call x1, Pallas kernels, precondition(): pl.pallas_call(functools.partial(main_kernel, peers), out_shape=(pair,) *...  1.86 us
  transfers between devices with their start and end apart: 20, of which 9 were waited for; matrix products, arithmetic and copies ran while one was open for 7% of the time, Pallas kernels for 4%

profile of v1, /device:TPU:0, one launch (start us, length us, event | category | flops | bytes accessed | tf_op | source)
XLA Modules:
  0.0 62.6 jit_solution(7661242830976038242)
XLA Ops:
  0.6 1.6 %copy-done = bf16[1,2,64,8192]{3,2,1,0:T(8,128)(2,1)S(1)} copy-done((bf16[1,2,64,8192]{3,2,1,0:T(8,128)(2,1)S(1)}, bf16[1,2,64,8192]{3,2,1,0:T(8,128)(2,1)}, u32[]{:S(2)}) %copy-start) | copy-done | bytes 2097176
  2.2 0.9 %pick_other.1 = (bf16[2,8,64,256]{3,2,1,0:T(8,128)(2,1)}, bf16[2,8,64,256]{3,2,1,0:T(8,128)(2,1)}) custom-call(bf16[1,2,64,8192]{3,2,1,0:T(8,128)(2,1)S(1)} %copy-done), custom_call_target="tpu_custom_call" | custom-call | bytes 2097152 | tf_op jit(solution)/shard_map/pick_other/pallas_call | solution.py:47
  3.2 0.5 collective-permute-start
  3.7 0.1 collective-permute-start.6
  3.8 0.4 copy-done.1
  4.2 0.2 pick_own.1
  4.4 1.1 %collective-permute-done = bf16[2,8,64,256]{3,2,1,0:T(8,128)(2,1)} collective-permute-done((bf16[2,8,64,256]{3,2,1,0:T(8,128)(2,1)}, bf16[2,8,64,256]{3,2,1,0:T(8,128)(2,1)}, u32[]{:S(2)}, u32[]{:S(2)}) %collective-permute-start) | collective-permute-done | bytes 524320 | tf_op jit(solution)/shard_map/ppermute | solution.py:17
  5.6 1.9 %add_convert_fusion.3 = (bf16[1,8,64,256]{3,2,1,0:T(8,128)(2,1)}, bf16[1,8,64,256]{3,2,1,0:T(8,128)(2,1)S(1)}) fusion(bf16[2,8,64,256]{3,2,1,0:T(8,128)(2,1)S(1)} %get-tuple-element.19, s32[]{:T(128)S(6)} %select_n.88, bf16[2,8,64,256]{3,2,1,0:T(8,128)(2,1)} %collective-permute-done, s32[]{:T(128)S(6)} %select_n.91), kind=kLoop, calls=%fused_computation.3 | loop fusion | flops 1048576 | bytes 1572872 | tf_op jit(solution)/shard_map/convert_element_type | solution.py:242
  7.5 2.9 %collective-permute-start.1 = (bf16[1,8,64,256]{3,2,1,0:T(8,128)(2,1)}, bf16[1,8,64,256]{3,2,1,0:T(8,128)(2,1)S(1)}, u32[]{:S(2)}, u32[]{:S(2)}) collective-permute-start(bf16[1,8,64,256]{3,2,1,0:T(8,128)(2,1)} %get-tuple-element.34), channel_id=1, source_target_pairs={{0,16},{8,24},{16,0},{24,8},{1,17},{9,25},{17,1},{25,9},{2,18},{10... | collective-permute-start | bytes 786440 | tf_op jit(solution)/shard_map/ppermute | solution.py:17
  10.3 0.0 collective-permute-done.6
  10.4 2.0 %add_convert_fusion.1 = (bf16[1,8,64,256]{3,2,1,0:T(8,128)(2,1)}, bf16[1,8,64,256]{3,2,1,0:T(8,128)(2,1)S(1)}) fusion(bf16[2,8,64,256]{3,2,1,0:T(8,128)(2,1)S(1)} %get-tuple-element.21, s32[]{:T(128)S(6)} %select_n.88, bf16[2,8,64,256]{3,2,1,0:T(8,128)(2,1)} %collective-permute-done.6, s32[]{:T(128)S(6)} %select_n.91), kind=kLoop, calls=%fused_computation.1 | loop fusion | flops 1048576 | bytes 1572872 | tf_op jit(solution)/shard_map/convert_element_type | solution.py:242
  12.4 0.0 collective-permute-start.7
  12.4 5.2 %collective-permute-done.1 = bf16[1,8,64,256]{3,2,1,0:T(8,128)(2,1)S(1)} collective-permute-done((bf16[1,8,64,256]{3,2,1,0:T(8,128)(2,1)}, bf16[1,8,64,256]{3,2,1,0:T(8,128)(2,1)S(1)}, u32[]{:S(2)}, u32[]{:S(2)}) %collective-permute-start.1) | collective-permute-done | bytes 262176 | tf_op jit(solution)/shard_map/ppermute | solution.py:17
  17.6 0.1 fusion.3
  17.7 4.2 %collective-permute-start.4 = (bf16[2,64,256]{2,1,0:T(8,128)(2,1)S(1)}, bf16[2,64,256]{2,1,0:T(8,128)(2,1)S(1)}, u32[]{:S(2)}, u32[]{:S(2)}) collective-permute-start(bf16[2,64,256]{2,1,0:T(8,128)(2,1)S(1)} %get-tuple-element.36), channel_id=1, source_target_pairs={{0,6},{1,7},{2,4},{3,5},{4,2},{5,3},{6,0},{7,1},{8,14},{9,15},{10,... | collective-permute-start | bytes 196616 | tf_op jit(solution)/shard_map/ppermute | solution.py:17
  21.9 0.6 %collective-permute-start.2 = (bf16[2,64,256]{2,1,0:T(8,128)(2,1)S(1)}, bf16[2,64,256]{2,1,0:T(8,128)(2,1)S(1)}, u32[]{:S(2)}, u32[]{:S(2)}) collective-permute-start(bf16[2,64,256]{2,1,0:T(8,128)(2,1)S(1)} %get-tuple-element.38), channel_id=1, source_target_pairs={{0,2},{1,3},{2,0},{3,1},{4,6},{5,7},{6,4},{7,5},{8,10},{9,11},{10,... | collective-permute-start | bytes 196616 | tf_op jit(solution)/shard_map/ppermute | solution.py:17
  22.6 0.2 collective-permute-done.7
  22.9 1.8 %collective-permute-start.8 = (bf16[4,64,256]{2,1,0:T(8,128)(2,1)S(1)}, bf16[4,64,256]{2,1,0:T(8,128)(2,1)S(1)}, u32[]{:S(2)}, u32[]{:S(2)}) collective-permute-start(bf16[4,64,256]{2,1,0:T(8,128)(2,1)S(1)} %fusion), channel_id=1, source_target_pairs={{0,1},{1,0},{2,3},{3,2},{4,5},{5,4},{6,7},{7,6},{8,9},{9,8},{10,11... | collective-permute-start | bytes 393224 | tf_op jit(solution)/shard_map/ppermute | solution.py:17
  24.7 0.0 collective-permute-done.4.refs_3_
  24.7 2.4 %collective-permute-done.3.refs_2_ = bf16[2,64,256]{2,1,0:T(8,128)(2,1)S(1)} collective-permute-done((bf16[2,64,256]{2,1,0:T(8,128)(2,1)S(1)}, bf16[2,64,256]{2,1,0:T(8,128)(2,1)S(1)}, u32[]{:S(2)}, u32[]{:S(2)}) %collective-permute-start.3) | collective-permute-done | bytes 65568 | tf_op jit(solution)/shard_map/ppermute | solution.py:17
  27.1 0.0 collective-permute-done.2.refs_1_
  27.1 0.0 copy-start.3
  27.1 0.0 copy-start.4
  27.2 1.6 %collective-permute-start.5 = (bf16[4,64,256]{2,1,0:T(8,128)(2,1)S(1)}, bf16[4,64,256]{2,1,0:T(8,128)(2,1)S(1)}, u32[]{:S(2)}, u32[]{:S(2)}) collective-permute-start(bf16[4,64,256]{2,1,0:T(8,128)(2,1)S(1)} %pad_maximum_fusion), channel_id=1, source_target_pairs={{0,1},{1,0},{2,3},{3,2},{4,5},{5,4},{6,7},{7,6},{8,9},{9,8},{10,11... | collective-permute-start | bytes 393224 | tf_op jit(solution)/shard_map/ppermute | solution.py:17
  28.7 2.2 %collective-permute-start.9 = (bf16[2,64,256]{2,1,0:T(8,128)(2,1)S(1)}, bf16[2,64,256]{2,1,0:T(8,128)(2,1)S(1)}, u32[]{:S(2)}, u32[]{:S(2)}) collective-permute-start(bf16[2,64,256]{2,1,0:T(8,128)(2,1)S(1)} %pad_maximum_fusion.3), channel_id=1, source_target_pairs={{0,2},{1,3},{2,0},{3,1},{4,6},{5,7},{6,4},{7,5},{8,10},{9,11},{10,... | collective-permute-start | bytes 196616 | tf_op jit(solution)/shard_map/ppermute | solution.py:17
  31.0 2.6 %collective-permute-start.10 = (bf16[2,64,256]{2,1,0:T(8,128)(2,1)S(1)}, bf16[2,64,256]{2,1,0:T(8,128)(2,1)S(1)}, u32[]{:S(2)}, u32[]{:S(2)}) collective-permute-start(bf16[2,64,256]{2,1,0:T(8,128)(2,1)S(1)} %pad_maximum_fusion.4), channel_id=1, source_target_pairs={{0,4},{1,5},{2,6},{3,7},{4,0},{5,1},{6,2},{7,3},{8,12},{9,13},{10,... | collective-permute-start | bytes 196616 | tf_op jit(solution)/shard_map/ppermute | solution.py:17
  33.6 0.1 collective-permute-start.11
  33.7 0.0 collective-permute-done.5.refs_4_
  33.8 3.2 %collective-permute-done.10.refs_7_ = bf16[2,64,256]{2,1,0:T(8,128)(2,1)S(1)} collective-permute-done((bf16[2,64,256]{2,1,0:T(8,128)(2,1)S(1)}, bf16[2,64,256]{2,1,0:T(8,128)(2,1)S(1)}, u32[]{:S(2)}, u32[]{:S(2)}) %collective-permute-start.10) | collective-permute-done | bytes 65568 | tf_op jit(solution)/shard_map/ppermute | solution.py:17
  37.0 2.8 %collective-permute-done.11.refs_8_ = bf16[2,64,256]{2,1,0:T(8,128)(2,1)S(1)} collective-permute-done((bf16[2,64,256]{2,1,0:T(8,128)(2,1)S(1)}, bf16[2,64,256]{2,1,0:T(8,128)(2,1)S(1)}, u32[]{:S(2)}, u32[]{:S(2)}) %collective-permute-start.11) | collective-permute-done | bytes 65568 | tf_op jit(solution)/shard_map/ppermute | solution.py:17
  39.8 1.9 %precondition.1 = (bf16[2,64,256]{2,1,0:T(8,128)(2,1)S(1)}, bf16[2,64,256]{2,1,0:T(8,128)(2,1)S(1)}, bf16[2,64,256]{2,1,0:T(8,128)(2,1)S(1)}, bf16[2,64,256]{2,1...) custom-call(bf16[2,64,256]{2,1,0:T(8,128)(2,1)S(1)} %bitcast.27, ...), custom_call_target="tpu_custom_call" | custom-call | flops 536870912 | bytes 3145728 | tf_op jit(solution)/shard_map/precondition/pallas_call | solution.py:129
  41.6 0.1 collective-permute-start.12
  41.7 1.6 %collective-permute-start.14 = (bf16[2,64,256]{2,1,0:T(8,128)(2,1)S(1)}, bf16[2,64,256]{2,1,0:T(8,128)(2,1)S(1)}, u32[]{:S(2)}, u32[]{:S(2)}) collective-permute-start(bf16[2,64,256]{2,1,0:T(8,128)(2,1)S(1)} %get-tuple-element.25), channel_id=1, source_target_pairs={{0,6},{1,7},{2,4},{3,5},{4,2},{5,3},{6,0},{7,1},{8,14},{9,15},{10,... | collective-permute-start | bytes 196616 | tf_op jit(solution)/shard_map/ppermute | solution.py:17
  43.3 2.0 %collective-permute-start.13 = (bf16[2,64,256]{2,1,0:T(8,128)(2,1)S(1)}, bf16[2,64,256]{2,1,0:T(8,128)(2,1)S(1)}, u32[]{:S(2)}, u32[]{:S(2)}) collective-permute-start(bf16[2,64,256]{2,1,0:T(8,128)(2,1)S(1)} %get-tuple-element.24), channel_id=1, source_target_pairs={{0,4},{1,5},{2,6},{3,7},{4,0},{5,1},{6,2},{7,3},{8,12},{9,13},{10,... | collective-permute-start | bytes 196616 | tf_op jit(solution)/shard_map/ppermute | solution.py:17
  45.3 1.5 %collective-permute-start.16 = (bf16[4,64,256]{2,1,0:T(8,128)(2,1)S(1)}, bf16[4,64,256]{2,1,0:T(8,128)(2,1)S(1)}, u32[]{:S(2)}, u32[]{:S(2)}) collective-permute-start(bf16[4,64,256]{2,1,0:T(8,128)(2,1)S(1)} %get-tuple-element.27), channel_id=1, source_target_pairs={{0,1},{1,0},{2,3},{3,2},{4,5},{5,4},{6,7},{7,6},{8,9},{9,8},{10,11... | collective-permute-start | bytes 393224 | tf_op jit(solution)/shard_map/ppermute | solution.py:17
  46.8 2.2 %statistics.1 = (f32[1,512,512]{2,1,0:T(8,128)}, f32[1,512,512]{2,1,0:T(8,128)}, f32[1,512,512]{2,1,0:T(8,128)}) custom-call(bf16[512,512]{1,0:T(8,128)(2,1)S(1)} %get-tuple-element.28.block, f32[1,512,512]{2,1,0:T(8,128)S(1)} %copy-done.3, f32[1,512,512]{2,1,0:T(8,128)S(1)} %copy-done.4, f32[1,512,512]{2,1,0:T(8,128)S(1)} %copy-done.2), custom_call_target="tpu_custom_call" | custom-call | flops 536870912 | bytes 6815744 | tf_op jit(solution)/shard_map/statistics/pallas_call | solution.py:165
  49.0 0.0 collective-permute-done.12.refs_1_
  49.0 1.8 %collective-permute-done.13.refs_2_ = bf16[2,64,256]{2,1,0:T(8,128)(2,1)S(1)} collective-permute-done((bf16[2,64,256]{2,1,0:T(8,128)(2,1)S(1)}, bf16[2,64,256]{2,1,0:T(8,128)(2,1)S(1)}, u32[]{:S(2)}, u32[]{:S(2)}) %collective-permute-start.13) | collective-permute-done | bytes 65568 | tf_op jit(solution)/shard_map/ppermute | solution.py:17
  50.8 0.0 collective-permute-done.14.refs_3_
  50.8 1.5 %collective-permute-start.15 = (bf16[4,64,256]{2,1,0:T(8,128)(2,1)S(1)}, bf16[4,64,256]{2,1,0:T(8,128)(2,1)S(1)}, u32[]{:S(2)}, u32[]{:S(2)}) collective-permute-start(bf16[4,64,256]{2,1,0:T(8,128)(2,1)S(1)} %pad_maximum_fusion.1), channel_id=1, source_target_pairs={{0,1},{1,0},{2,3},{3,2},{4,5},{5,4},{6,7},{7,6},{8,9},{9,8},{10,11... | collective-permute-start | bytes 393224 | tf_op jit(solution)/shard_map/ppermute | solution.py:17
  52.3 0.0 collective-permute-done.16
  52.3 0.1 collective-permute-start.17
  52.4 3.3 %collective-permute-start.18 = (bf16[2,64,256]{2,1,0:T(8,128)(2,1)S(1)}, bf16[2,64,256]{2,1,0:T(8,128)(2,1)S(1)}, u32[]{:S(2)}, u32[]{:S(2)}) collective-permute-start(bf16[2,64,256]{2,1,0:T(8,128)(2,1)S(1)} %pad_maximum_fusion.8), channel_id=1, source_target_pairs={{0,4},{1,5},{2,6},{3,7},{4,0},{5,1},{6,2},{7,3},{8,12},{9,13},{10,... | collective-permute-start | bytes 196616 | tf_op jit(solution)/shard_map/ppermute | solution.py:17
  55.7 1.2 %collective-permute-start.19 = (bf16[2,64,256]{2,1,0:T(8,128)(2,1)S(1)}, bf16[2,64,256]{2,1,0:T(8,128)(2,1)S(1)}, u32[]{:S(2)}, u32[]{:S(2)}) collective-permute-start(bf16[2,64,256]{2,1,0:T(8,128)(2,1)S(1)} %pad_maximum_fusion.9), channel_id=1, source_target_pairs={{0,6},{1,7},{2,4},{3,5},{4,2},{5,3},{6,0},{7,1},{8,14},{9,15},{10,... | collective-permute-start | bytes 196616 | tf_op jit(solution)/shard_map/ppermute | solution.py:17
  56.9 0.0 collective-permute-done.17.refs_6_
  56.9 1.0 %collective-permute-done.18.refs_7_ = bf16[2,64,256]{2,1,0:T(8,128)(2,1)S(1)} collective-permute-done((bf16[2,64,256]{2,1,0:T(8,128)(2,1)S(1)}, bf16[2,64,256]{2,1,0:T(8,128)(2,1)S(1)}, u32[]{:S(2)}, u32[]{:S(2)}) %collective-permute-start.18) | collective-permute-done | bytes 65568 | tf_op jit(solution)/shard_map/ppermute | solution.py:17
  57.9 3.9 %collective-permute-done.19.refs_8_ = bf16[2,64,256]{2,1,0:T(8,128)(2,1)S(1)} collective-permute-done((bf16[2,64,256]{2,1,0:T(8,128)(2,1)S(1)}, bf16[2,64,256]{2,1,0:T(8,128)(2,1)S(1)}, u32[]{:S(2)}, u32[]{:S(2)}) %collective-permute-start.19) | collective-permute-done | bytes 65568 | tf_op jit(solution)/shard_map/ppermute | solution.py:17
  61.8 0.8 %assemble.1 = bf16[2,64,2048]{2,1,0:T(8,128)(2,1)} custom-call(bf16[2,64,256]{2,1,0:T(8,128)(2,1)S(1)} %get-tuple-element.22.refs_0_, bf16[2,64,256]{2,1,0:T(8,128)(2,1)S(1)} %collective-permute-done.12.refs_1_, bf16[2,64,256]{2,1,0:T(8,128)(2,1)S(1)} %collective-permute-done.13.refs_2_, bf16[2,64,256]{2,1,0:T(8,128)(2,1)S(1)} %collective-permute-done.14.refs_3_, ...), custom_call_target="tpu_custom_call" | custom-call | bytes 1048576 | tf_op jit(solution)/shard_map/assemble/pallas_call | solution.py:210
  (38 shorter events, 0.3 us)
Async XLA Ops:
  0.6 1.6 %copy-start = (bf16[1,2,64,8192]{3,2,1,0:T(8,128)(2,1)S(1)}, bf16[1,2,64,8192]{3,2,1,0:T(8,128)(2,1)}, u32[]{:S(2)}) copy-start(bf16[1,2,64,8192]{3,2,1,0:T(8,128)(2,1)} %grads.3) | copy-start | bytes 6291460
  2.2 2.0 %copy-start.1 = (bf16[1,2,64,8192]{3,2,1,0:T(8,128)(2,1)S(1)}, bf16[1,2,64,8192]{3,2,1,0:T(8,128)(2,1)}, u32[]{:S(2)}) copy-start(bf16[1,2,64,8192]{3,2,1,0:T(8,128)(2,1)} %grads.3) | copy-start | bytes 6291460
  3.2 2.4 %collective-permute-start = (bf16[2,8,64,256]{3,2,1,0:T(8,128)(2,1)}, bf16[2,8,64,256]{3,2,1,0:T(8,128)(2,1)}, u32[]{:S(2)}, u32[]{:S(2)}) collective-permute-start(bf16[2,8,64,256]{3,2,1,0:T(8,128)(2,1)} %get-tuple-element.18), channel_id=1, source_target_pairs={{0,8},{8,0},{16,24},{24,16},{1,9},{9,1},{17,25},{25,17},{2,10},{10... | collective-permute-start | bytes 1572872 | tf_op jit(solution)/shard_map/ppermute | solution.py:17
  3.7 6.7 %collective-permute-start.6 = (bf16[2,8,64,256]{3,2,1,0:T(8,128)(2,1)}, bf16[2,8,64,256]{3,2,1,0:T(8,128)(2,1)}, u32[]{:S(2)}, u32[]{:S(2)}) collective-permute-start(bf16[2,8,64,256]{3,2,1,0:T(8,128)(2,1)} %get-tuple-element.20), channel_id=1, source_target_pairs={{0,8},{8,0},{16,24},{24,16},{1,9},{9,1},{17,25},{25,17},{2,10},{10... | collective-permute-start | bytes 1572872 | tf_op jit(solution)/shard_map/ppermute | solution.py:17
  7.5 10.2 %collective-permute-start.1 = (bf16[1,8,64,256]{3,2,1,0:T(8,128)(2,1)}, bf16[1,8,64,256]{3,2,1,0:T(8,128)(2,1)S(1)}, u32[]{:S(2)}, u32[]{:S(2)}) collective-permute-start(bf16[1,8,64,256]{3,2,1,0:T(8,128)(2,1)} %get-tuple-element.34), channel_id=1, source_target_pairs={{0,16},{8,24},{16,0},{24,8},{1,17},{9,25},{17,1},{25,9},{2,18},{10... | collective-permute-start | bytes 786440 | tf_op jit(solution)/shard_map/ppermute | solution.py:17
  10.4 29.4 %copy-start.2 = (f32[1,512,512]{2,1,0:T(8,128)S(1)}, f32[1,512,512]{2,1,0:T(8,128)}, u32[]{:S(2)}) copy-start(f32[1,512,512]{2,1,0:T(8,128)} %accum.1) | copy-start | bytes 3145732
  10.4 29.4 %copy-start.5 = (bf16[1,512,512]{2,1,0:T(8,128)(2,1)S(1)}, bf16[1,512,512]{2,1,0:T(8,128)(2,1)}, u32[]{:S(2)}) copy-start(bf16[1,512,512]{2,1,0:T(8,128)(2,1)} %refs_9_.1) | copy-start | bytes 1572868
  10.4 29.4 %copy-start.6 = (bf16[1,512,512]{2,1,0:T(8,128)(2,1)S(1)}, bf16[1,512,512]{2,1,0:T(8,128)(2,1)}, u32[]{:S(2)}) copy-start(bf16[1,512,512]{2,1,0:T(8,128)(2,1)} %refs_10_.1) | copy-start | bytes 1572868
  12.4 10.4 %collective-permute-start.7 = (bf16[1,8,64,256]{3,2,1,0:T(8,128)(2,1)}, bf16[1,8,64,256]{3,2,1,0:T(8,128)(2,1)S(1)}, u32[]{:S(2)}, u32[]{:S(2)}) collective-permute-start(bf16[1,8,64,256]{3,2,1,0:T(8,128)(2,1)} %get-tuple-element.32), channel_id=1, source_target_pairs={{0,16},{8,24},{16,0},{24,8},{1,17},{9,25},{17,1},{25,9},{2,18},{10... | collective-permute-start | bytes 786440 | tf_op jit(solution)/shard_map/ppermute | solution.py:17
  17.7 7.0 %collective-permute-start.4 = (bf16[2,64,256]{2,1,0:T(8,128)(2,1)S(1)}, bf16[2,64,256]{2,1,0:T(8,128)(2,1)S(1)}, u32[]{:S(2)}, u32[]{:S(2)}) collective-permute-start(bf16[2,64,256]{2,1,0:T(8,128)(2,1)S(1)} %get-tuple-element.36), channel_id=1, source_target_pairs={{0,6},{1,7},{2,4},{3,5},{4,2},{5,3},{6,0},{7,1},{8,14},{9,15},{10,... | collective-permute-start | bytes 196616 | tf_op jit(solution)/shard_map/ppermute | solution.py:17
  21.9 5.2 %collective-permute-start.3 = (bf16[2,64,256]{2,1,0:T(8,128)(2,1)S(1)}, bf16[2,64,256]{2,1,0:T(8,128)(2,1)S(1)}, u32[]{:S(2)}, u32[]{:S(2)}) collective-permute-start(bf16[2,64,256]{2,1,0:T(8,128)(2,1)S(1)} %get-tuple-element.37), channel_id=1, source_target_pairs={{0,4},{1,5},{2,6},{3,7},{4,0},{5,1},{6,2},{7,3},{8,12},{9,13},{10,... | collective-permute-start | bytes 196616 | tf_op jit(solution)/shard_map/ppermute | solution.py:17
  21.9 5.2 %collective-permute-start.2 = (bf16[2,64,256]{2,1,0:T(8,128)(2,1)S(1)}, bf16[2,64,256]{2,1,0:T(8,128)(2,1)S(1)}, u32[]{:S(2)}, u32[]{:S(2)}) collective-permute-start(bf16[2,64,256]{2,1,0:T(8,128)(2,1)S(1)} %get-tuple-element.38), channel_id=1, source_target_pairs={{0,2},{1,3},{2,0},{3,1},{4,6},{5,7},{6,4},{7,5},{8,10},{9,11},{10,... | collective-permute-start | bytes 196616 | tf_op jit(solution)/shard_map/ppermute | solution.py:17
  22.9 5.8 %collective-permute-start.8 = (bf16[4,64,256]{2,1,0:T(8,128)(2,1)S(1)}, bf16[4,64,256]{2,1,0:T(8,128)(2,1)S(1)}, u32[]{:S(2)}, u32[]{:S(2)}) collective-permute-start(bf16[4,64,256]{2,1,0:T(8,128)(2,1)S(1)} %fusion), channel_id=1, source_target_pairs={{0,1},{1,0},{2,3},{3,2},{4,5},{5,4},{6,7},{7,6},{8,9},{9,8},{10,11... | collective-permute-start | bytes 393224 | tf_op jit(solution)/shard_map/ppermute | solution.py:17
  27.1 19.7 %copy-start.3 = (f32[1,512,512]{2,1,0:T(8,128)S(1)}, f32[1,512,512]{2,1,0:T(8,128)}, u32[]{:S(2)}) copy-start(f32[1,512,512]{2,1,0:T(8,128)} %left.1) | copy-start | bytes 3145732
  27.1 19.7 %copy-start.4 = (f32[1,512,512]{2,1,0:T(8,128)S(1)}, f32[1,512,512]{2,1,0:T(8,128)}, u32[]{:S(2)}) copy-start(f32[1,512,512]{2,1,0:T(8,128)} %right.1) | copy-start | bytes 3145732
  27.2 6.6 %collective-permute-start.5 = (bf16[4,64,256]{2,1,0:T(8,128)(2,1)S(1)}, bf16[4,64,256]{2,1,0:T(8,128)(2,1)S(1)}, u32[]{:S(2)}, u32[]{:S(2)}) collective-permute-start(bf16[4,64,256]{2,1,0:T(8,128)(2,1)S(1)} %pad_maximum_fusion), channel_id=1, source_target_pairs={{0,1},{1,0},{2,3},{3,2},{4,5},{5,4},{6,7},{7,6},{8,9},{9,8},{10,11... | collective-permute-start | bytes 393224 | tf_op jit(solution)/shard_map/ppermute | solution.py:17
  28.7 5.0 %collective-permute-start.9 = (bf16[2,64,256]{2,1,0:T(8,128)(2,1)S(1)}, bf16[2,64,256]{2,1,0:T(8,128)(2,1)S(1)}, u32[]{:S(2)}, u32[]{:S(2)}) collective-permute-start(bf16[2,64,256]{2,1,0:T(8,128)(2,1)S(1)} %pad_maximum_fusion.3), channel_id=1, source_target_pairs={{0,2},{1,3},{2,0},{3,1},{4,6},{5,7},{6,4},{7,5},{8,10},{9,11},{10,... | collective-permute-start | bytes 196616 | tf_op jit(solution)/shard_map/ppermute | solution.py:17
  31.0 6.0 %collective-permute-start.10 = (bf16[2,64,256]{2,1,0:T(8,128)(2,1)S(1)}, bf16[2,64,256]{2,1,0:T(8,128)(2,1)S(1)}, u32[]{:S(2)}, u32[]{:S(2)}) collective-permute-start(bf16[2,64,256]{2,1,0:T(8,128)(2,1)S(1)} %pad_maximum_fusion.4), channel_id=1, source_target_pairs={{0,4},{1,5},{2,6},{3,7},{4,0},{5,1},{6,2},{7,3},{8,12},{9,13},{10,... | collective-permute-start | bytes 196616 | tf_op jit(solution)/shard_map/ppermute | solution.py:17
  33.6 6.1 %collective-permute-start.11 = (bf16[2,64,256]{2,1,0:T(8,128)(2,1)S(1)}, bf16[2,64,256]{2,1,0:T(8,128)(2,1)S(1)}, u32[]{:S(2)}, u32[]{:S(2)}) collective-permute-start(bf16[2,64,256]{2,1,0:T(8,128)(2,1)S(1)} %pad_maximum_fusion.5), channel_id=1, source_target_pairs={{0,6},{1,7},{2,4},{3,5},{4,2},{5,3},{6,0},{7,1},{8,14},{9,15},{10,... | collective-permute-start | bytes 196616 | tf_op jit(solution)/shard_map/ppermute | solution.py:17
  41.6 7.3 %collective-permute-start.12 = (bf16[2,64,256]{2,1,0:T(8,128)(2,1)S(1)}, bf16[2,64,256]{2,1,0:T(8,128)(2,1)S(1)}, u32[]{:S(2)}, u32[]{:S(2)}) collective-permute-start(bf16[2,64,256]{2,1,0:T(8,128)(2,1)S(1)} %get-tuple-element.23), channel_id=1, source_target_pairs={{0,2},{1,3},{2,0},{3,1},{4,6},{5,7},{6,4},{7,5},{8,10},{9,11},{10,... | collective-permute-start | bytes 196616 | tf_op jit(solution)/shard_map/ppermute | solution.py:17
  41.7 9.1 %collective-permute-start.14 = (bf16[2,64,256]{2,1,0:T(8,128)(2,1)S(1)}, bf16[2,64,256]{2,1,0:T(8,128)(2,1)S(1)}, u32[]{:S(2)}, u32[]{:S(2)}) collective-permute-start(bf16[2,64,256]{2,1,0:T(8,128)(2,1)S(1)} %get-tuple-element.25), channel_id=1, source_target_pairs={{0,6},{1,7},{2,4},{3,5},{4,2},{5,3},{6,0},{7,1},{8,14},{9,15},{10,... | collective-permute-start | bytes 196616 | tf_op jit(solution)/shard_map/ppermute | solution.py:17
  43.3 7.4 %collective-permute-start.13 = (bf16[2,64,256]{2,1,0:T(8,128)(2,1)S(1)}, bf16[2,64,256]{2,1,0:T(8,128)(2,1)S(1)}, u32[]{:S(2)}, u32[]{:S(2)}) collective-permute-start(bf16[2,64,256]{2,1,0:T(8,128)(2,1)S(1)} %get-tuple-element.24), channel_id=1, source_target_pairs={{0,4},{1,5},{2,6},{3,7},{4,0},{5,1},{6,2},{7,3},{8,12},{9,13},{10,... | collective-permute-start | bytes 196616 | tf_op jit(solution)/shard_map/ppermute | solution.py:17
  45.3 7.0 %collective-permute-start.16 = (bf16[4,64,256]{2,1,0:T(8,128)(2,1)S(1)}, bf16[4,64,256]{2,1,0:T(8,128)(2,1)S(1)}, u32[]{:S(2)}, u32[]{:S(2)}) collective-permute-start(bf16[4,64,256]{2,1,0:T(8,128)(2,1)S(1)} %get-tuple-element.27), channel_id=1, source_target_pairs={{0,1},{1,0},{2,3},{3,2},{4,5},{5,4},{6,7},{7,6},{8,9},{9,8},{10,11... | collective-permute-start | bytes 393224 | tf_op jit(solution)/shard_map/ppermute | solution.py:17
  50.8 6.1 %collective-permute-start.15 = (bf16[4,64,256]{2,1,0:T(8,128)(2,1)S(1)}, bf16[4,64,256]{2,1,0:T(8,128)(2,1)S(1)}, u32[]{:S(2)}, u32[]{:S(2)}) collective-permute-start(bf16[4,64,256]{2,1,0:T(8,128)(2,1)S(1)} %pad_maximum_fusion.1), channel_id=1, source_target_pairs={{0,1},{1,0},{2,3},{3,2},{4,5},{5,4},{6,7},{7,6},{8,9},{9,8},{10,11... | collective-permute-start | bytes 393224 | tf_op jit(solution)/shard_map/ppermute | solution.py:17
  52.3 4.6 %collective-permute-start.17 = (bf16[2,64,256]{2,1,0:T(8,128)(2,1)S(1)}, bf16[2,64,256]{2,1,0:T(8,128)(2,1)S(1)}, u32[]{:S(2)}, u32[]{:S(2)}) collective-permute-start(bf16[2,64,256]{2,1,0:T(8,128)(2,1)S(1)} %pad_maximum_fusion.7), channel_id=1, source_target_pairs={{0,2},{1,3},{2,0},{3,1},{4,6},{5,7},{6,4},{7,5},{8,10},{9,11},{10,... | collective-permute-start | bytes 196616 | tf_op jit(solution)/shard_map/ppermute | solution.py:17
  52.4 5.5 %collective-permute-start.18 = (bf16[2,64,256]{2,1,0:T(8,128)(2,1)S(1)}, bf16[2,64,256]{2,1,0:T(8,128)(2,1)S(1)}, u32[]{:S(2)}, u32[]{:S(2)}) collective-permute-start(bf16[2,64,256]{2,1,0:T(8,128)(2,1)S(1)} %pad_maximum_fusion.8), channel_id=1, source_target_pairs={{0,4},{1,5},{2,6},{3,7},{4,0},{5,1},{6,2},{7,3},{8,12},{9,13},{10,... | collective-permute-start | bytes 196616 | tf_op jit(solution)/shard_map/ppermute | solution.py:17
  55.7 6.1 %collective-permute-start.19 = (bf16[2,64,256]{2,1,0:T(8,128)(2,1)S(1)}, bf16[2,64,256]{2,1,0:T(8,128)(2,1)S(1)}, u32[]{:S(2)}, u32[]{:S(2)}) collective-permute-start(bf16[2,64,256]{2,1,0:T(8,128)(2,1)S(1)} %pad_maximum_fusion.9), channel_id=1, source_target_pairs={{0,6},{1,7},{2,4},{3,5},{4,2},{5,3},{6,0},{7,1},{8,14},{9,15},{10,... | collective-permute-start | bytes 196616 | tf_op jit(solution)/shard_map/ppermute | solution.py:17

commit v2 on v1

v2 whole, which is shorter than its diff:
```python
import functools

import jax
import jax.numpy as jnp
from jax import lax
from jax.experimental import pallas as pl
from jax.experimental.pallas import tpu as pltpu
from jax.sharding import PartitionSpec as P

MIB = 1024 * 1024
ANY = pl.BlockSpec(memory_space=pl.ANY)
VMEM = pl.BlockSpec(memory_space=pltpu.VMEM)
HBM = pl.BlockSpec(memory_space=pltpu.HBM)


def swap(x, axis, bit):
    n = lax.axis_size(axis)
    return lax.ppermute(x, axis, [(i, i ^ bit) for i in range(n)])


def peer(k, e):
    return jnp.bitwise_xor(lax.axis_index("fsdp"), 2 * k + e)


def pick_kernel(groups, other, grads, *refs):
    outs, sem = refs[:-1], refs[-1]
    slabs = grads.shape[1]
    block = outs[0].shape[-1]
    per_rep = lax.axis_size("fsdp") // slabs
    rep = jnp.bitwise_xor(lax.axis_index("rep"), 1 if other else 0)
    copies = []
    for group, out in zip(groups, outs):
        for i, k in enumerate(group):
            for j in range(out.shape[1]):
                for e in range(2):
                    to = peer(k, e)
                    column = jnp.bitwise_xor(rep, 2 * j) * per_rep + to // slabs
                    start = pl.multiple_of(column * block, block)
                    copies.append(
                        pltpu.make_async_copy(
                            grads.at[0, lax.rem(to, slabs), :, pl.ds(start, block)],
                            out.at[i, j, e],
                            sem,
                        )
                    )
    for copy in copies:
        copy.start()
    for copy in copies:
        copy.wait()


def pick(grads, groups, other):
    rows = grads.shape[2]
    block = rows * lax.axis_size("fsdp")
    shapes = [
        jax.ShapeDtypeStruct((len(g), lax.axis_size("rep") // 2, 2, rows, block), grads.dtype)
        for g in groups
    ]
    return pl.pallas_call(
        functools.partial(pick_kernel, groups, other),
        out_shape=shapes,
        in_specs=[HBM],
        out_specs=[ANY] * len(groups),
        scratch_shapes=[pltpu.SemaphoreType.DMA],
        compiler_params=pltpu.CompilerParams(vmem_limit_bytes=4 * MIB),
        cost_estimate=pl.CostEstimate(flops=0, bytes_accessed=2 * MIB, transcendentals=0),
        name="pick_other" if other else "pick_own",
    )(pltpu.with_memory_space_constraint(grads, pltpu.HBM))


def place(k, e, rows):
    return pl.ds(pl.multiple_of(peer(k, e) * rows, rows), rows)


def main_kernel(spots, out_spots, *refs):
    ins, refs = refs[: len(spots)], refs[len(spots) :]
    left_root, right_root, accum = refs[:3]
    outs, refs = refs[3 : 3 + len(out_spots)], refs[3 + len(out_spots) :]
    block_out, lroot, rroot, acc, sems = refs
    rows = ins[0].shape[-2]

    lcopy = pltpu.make_async_copy(left_root.at[0], lroot, sems.at[1])
    rcopy = pltpu.make_async_copy(right_root.at[0], rroot, sems.at[2])
    acopy = pltpu.make_async_copy(accum.at[0], acc, sems.at[3])
    copies = [
        pltpu.make_async_copy(ref.at[i], block_out.at[place(k, e, rows)], sems.at[0])
        for ref, spot in zip(ins, spots)
        for i, (k, e) in enumerate(spot)
    ]
    lcopy.start()
    for copy in copies:
        copy.start()
    rcopy.start()
    acopy.start()
    lcopy.wait()
    for copy in copies:
        copy.wait()
    b = block_out[...]
    half = jnp.dot(lroot[...], b, preferred_element_type=jnp.float32).astype(jnp.bfloat16)
    rcopy.wait()
    precond = jnp.dot(half, rroot[...], preferred_element_type=jnp.float32)
    acopy.wait()
    wide = b.astype(jnp.float32)
    square = wide * wide
    ada_sq = jnp.sum(square / (acc[...] + square))
    pre_sq = jnp.sum(precond * precond)
    ratio = jnp.sqrt(ada_sq) / jnp.sqrt(pre_sq + 1e-06)
    lroot[...] = (ratio * precond).astype(jnp.bfloat16)
    for ref, spot in zip(outs, out_spots):
        for i, (k, e) in enumerate(spot):
            ref[i] = lroot[place(k, e, rows)]


def precondition(pieces, spots, out_spots, left_root, right_root, accum):
    side = left_root.shape[1]
    rows = pieces[0].shape[-2]
    outs = pl.pallas_call(
        functools.partial(main_kernel, spots, out_spots),
        out_shape=[
            jax.ShapeDtypeStruct((len(s), rows, side), jnp.bfloat16) for s in out_spots
        ]
        + [jax.ShapeDtypeStruct((side, side), jnp.bfloat16)],
        in_specs=[ANY] * (len(spots) + 3),
        out_specs=[VMEM] * (len(out_spots) + 1),
        scratch_shapes=[
            pltpu.VMEM((side, side), jnp.bfloat16),
            pltpu.VMEM((side, side), jnp.bfloat16),
            pltpu.VMEM((side, side), jnp.float32),
            pltpu.SemaphoreType.DMA((4,)),
        ],
        compiler_params=pltpu.CompilerParams(vmem_limit_bytes=16 * MIB),
        cost_estimate=pl.CostEstimate(
            flops=4 * side**3, bytes_accessed=12 * side * side, transcendentals=0
        ),
        name="precondition",
    )(*pieces, left_root, right_root, accum)
    return dict(zip(out_spots, outs)), outs[-1]


def stats_kernel(block, left, right, accum, left_out, right_out, accum_out):
    b = block[...]
    wide = b.astype(jnp.float32)
    accum_out[0] = accum[0] + wide * wide
    left_out[0] = left[0] + lax.dot_general(
        b, b, (((1,), (1,)), ((), ())), preferred_element_type=jnp.float32
    )
    right_out[0] = right[0] + lax.dot_general(
        b, b, (((0,), (0,)), ((), ())), preferred_element_type=jnp.float32
    )


def statistics(block, left, right, accum):
    shape = jax.ShapeDtypeStruct(left.shape, jnp.float32)
    side = left.shape[1]
    return pl.pallas_call(
        stats_kernel,
        out_shape=(shape,) * 3,
        in_specs=[VMEM] * 4,
        out_specs=(VMEM,) * 3,
        compiler_params=pltpu.CompilerParams(vmem_limit_bytes=20 * MIB),
        cost_estimate=pl.CostEstimate(
            flops=4 * side**3, bytes_accessed=26 * side * side, transcendentals=0
        ),
        name="statistics",
    )(block, left, right, accum)


def assemble_kernel(spots, *refs):
    ins, (update, sem) = refs[: len(spots)], refs[len(spots) :]
    slabs = update.shape[0]
    block = ins[0].shape[-1]
    copies = []
    for ref, spot in zip(ins, spots):
        for i, (k, e) in enumerate(spot):
            owner = peer(k, e)
            start = pl.multiple_of(owner // slabs * block, block)
            copies.append(
                pltpu.make_async_copy(
                    ref.at[i], update.at[lax.rem(owner, slabs), :, pl.ds(start, block)], sem
                )
            )
    for copy in copies:
        copy.start()
    for copy in copies:
        copy.wait()


def assemble(pieces, spots, shape):
    return pl.pallas_call(
        functools.partial(assemble_kernel, spots),
        out_shape=jax.ShapeDtypeStruct(shape, jnp.bfloat16),
        in_specs=[ANY] * len(pieces),
        out_specs=ANY,
        scratch_shapes=[pltpu.SemaphoreType.DMA],
        compiler_params=pltpu.CompilerParams(vmem_limit_bytes=4 * MIB),
        cost_estimate=pl.CostEstimate(flops=0, bytes_accessed=MIB, transcendentals=0),
        name="assemble",
    )(*pieces)


def far_pieces(peers):
    early = [k for k in range(peers - 1, 0, -1) if k % 2 == 0]
    late = [k for k in range(peers - 1, 0, -1) if k % 2 == 1]
    return early, late


def exchange(get, peers):
    early, late = far_pieces(peers)
    pieces, spots, crossing = [], [], {}
    for k in range(peers - 1, 0, -1):
        if k in early:
            near, far = get(k)
            come = swap(far, "fsdp", 1)
            both = swap(jnp.concatenate([near, come]), "fsdp", 2 * k)
            pieces.append(both)
            spots.append(((k, 0), (k, 1)))
        else:
            both = swap(get(k, whole=True), "fsdp", 2 * k)
            pieces.append(both)
            spots.append(((k, 0),))
            crossing[k] = both[1:]
    near, far = get(0)
    pieces.append(near)
    spots.append(((0, 0),))
    for group in ([0] + late[:-1], late[-1:]):
        lines = [far if k == 0 else crossing[k] for k in group]
        come = swap(jnp.concatenate(lines) if len(lines) > 1 else lines[0], "fsdp", 1)
        pieces.append(come)
        spots.append(tuple((k, 1) for k in group))
    return pieces, tuple(spots)


def total(terms):
    return sum(t.astype(jnp.float32) for t in terms).astype(jnp.bfloat16)


def body(grads, left_stat, right_stat, left_root, right_root, accum):
    rep_count, fsdp_count = lax.axis_size("rep"), lax.axis_size("fsdp")
    peers = fsdp_count // 2
    slabs, rows, width = grads.shape[1:]
    far = list(range(peers - 1, -1, -1))
    groups = (far[:1], far[1:2], far[2:])

    away = list(pick(grads, groups, True))
    for i, send in enumerate(away):
        if i > 0:
            send, away[i - 1] = lax.optimization_barrier((send, away[i - 1]))
        away[i] = swap(send, "rep", 1)
    mine = pick(grads, groups, False)

    summed = {}
    for group, theirs, ours in zip(groups, away, mine):
        for i, k in enumerate(group):
            terms, bit = [theirs[i], ours[i]], 1
            while 2 * bit < rep_count:
                bit *= 2
                pairs = [t.reshape((t.shape[0] // 2, 2) + t.shape[1:]) for t in terms]
                part = swap(total([p[:, 1] for p in pairs]), "rep", bit)
                terms = [p[:, 0] for p in pairs] + [part]
            summed[k] = [t[0] for t in terms]

    def summed_piece(k, whole=False):
        if whole:
            return total(summed[k])
        return [total([t[e : e + 1] for t in summed[k]]) for e in range(2)]

    pieces, spots = exchange(summed_piece, peers)

    early, late = far_pieces(peers)
    out_spots = tuple(((k, 0), (k, 1)) for k in late)
    out_spots += tuple(((k, e),) for k in early + [0] for e in range(2))
    scaled, block = precondition(pieces, spots, out_spots, left_root, right_root, accum)

    def scaled_piece(k, whole=False):
        return scaled[(k, 0), (k, 1)] if whole else [scaled[((k, e),)] for e in range(2)]

    pieces, spots = exchange(scaled_piece, peers)
    left_new, right_new, accum_new = statistics(block, left_stat, right_stat, accum)
    update = assemble(pieces, spots, (slabs, rows, width // rep_count))
    return (update, left_new, right_new, accum_new)


def solution(mesh):
    owned = P(("rep", "fsdp"), None, None)
    return jax.shard_map(
        body,
        mesh=mesh,
        in_specs=(P("rep", None, "fsdp", None),) + (owned,) * 5,
        out_specs=(P(None, "fsdp", "rep"),) + (owned,) * 3,
        check_vma=False,
    )
```

time: 62.8 us -> 53.2 us (0.85)
  waiting for transfers between devices: 21.7 us -> 17.6 us
  other arithmetic: 4.16 us -> 0.4 us
  local copies, waits for them, and re-layouts: 2.1 us -> 0.05 us
  starting transfers between devices: 27.8 us -> 25.9 us
  Pallas kernels: 5.97 us -> 7.83 us
    ppermute x20 -> x19, waiting for transfers between devices: 21.7 us -> 17.6 us  [swap(): return lax.ppermute(x, axis, [(i, i ^ bit) for i in range(n)])]
    convert_element_type x5 -> x7, other arithmetic: 4.06 us -> 0.34 us  [total(): return sum((t.astype(jnp.float32) for t in terms)).astype(jnp.bfloat16)]
    unnamed x14 -> x10, local copies, waits for them, and re-layouts: 2.01 us -> 0.03 us
    pallas_call x4, Pallas kernels: 3.81 us -> 5.69 us  [the longest x2 2.52 us: pick(): pl.pallas_call(functools.partial(pick_kernel, groups, other), out_shape=s...]
    ppermute x20 -> x19, starting transfers between devices: 27.8 us -> 25.9 us  [swap(): return lax.ppermute(x, axis, [(i, i ^ bit) for i in range(n)])]
  transfers between devices with their start and end apart: 20 -> 19, of which waited for: 9 -> 10; matrix products, arithmetic and copies ran while one was open for 7% -> 1% of each run, Pallas kernels for 4% -> 6%
where the time goes in v2:
time: 53.2 us; the launch traced here: 52.5 us
  starting transfers between devices  25.9 us (49%)
  waiting for transfers between devices  17.6 us (33%)
  Pallas kernels  7.83 us (15%)
  between operations  0.77 us (1%)
    ppermute x19, starting transfers between devices, swap(): return lax.ppermute(x, axis, [(i, i ^ bit) for i in range(n)])  25.9 us
    ppermute x19, waiting for transfers between devices, swap(): return lax.ppermute(x, axis, [(i, i ^ bit) for i in range(n)])  17.6 us
    pallas_call x2, Pallas kernels, pick(): pl.pallas_call(functools.partial(pick_kernel, groups, other), out_shape=s...  2.52 us
    pallas_call x1, Pallas kernels, precondition(): pl.pallas_call(functools.partial(main_kernel, spots, out_spots), out_shap...  2.38 us
    pallas_call x1, Pallas kernels, statistics(): pl.pallas_call(stats_kernel, out_shape=(shape,) * 3, in_specs=[VMEM] * 4,...  2.15 us
  transfers between devices with their start and end apart: 19, of which 10 were waited for; matrix products, arithmetic and copies ran while one was open for 1% of the time, Pallas kernels for 6%

profile of v2, /device:TPU:0, one launch (start us, length us, event | category | flops | bytes accessed | tf_op | source)
XLA Modules:
  0.0 52.5 jit_solution(16893646823220738921)
XLA Ops:
  0.6 1.3 %pick_other.1 = (bf16[1,2,2,64,512]{4,3,2,1,0:T(8,128)(2,1)S(1)}, bf16[1,2,2,64,512]{4,3,2,1,0:T(8,128)(2,1)S(1)}, bf16[2,2,2,64,512]{4,3,2,1,0:T(8,128)(2,1)S(1)}) custom-call(bf16[1,2,64,8192]{3,2,1,0:T(8,128)(2,1)} %grads.3), custom_call_target="tpu_custom_call" | custom-call | bytes 2097152 | tf_op jit(solution)/shard_map/pick_other/pallas_call | solution.py:59
  1.9 0.5 collective-permute-start
  2.4 1.2 %collective-permute-done = bf16[1,2,2,64,512]{4,3,2,1,0:T(8,128)(2,1)S(1)} collective-permute-done((bf16[1,2,2,64,512]{4,3,2,1,0:T(8,128)(2,1)S(1)}, bf16[1,2,2,64,512]{4,3,2,1,0:T(8,128)(2,1)S(1)}, u32[]{:S(2)}, u32[]{:S(2)}) %collective-permute-start) | collective-permute-done | bytes 262176 | tf_op jit(solution)/shard_map/ppermute | solution.py:18
  3.6 0.4 collective-permute-start.3
  4.0 1.2 %pick_own.1 = (bf16[1,2,2,64,512]{4,3,2,1,0:T(8,128)(2,1)S(1)}, bf16[1,2,2,64,512]{4,3,2,1,0:T(8,128)(2,1)S(1)}, bf16[2,2,2,64,512]{4,3,2,1,0:T(8,128)(2,1)S(1)}) custom-call(bf16[1,2,64,8192]{3,2,1,0:T(8,128)(2,1)} %grads.3), custom_call_target="tpu_custom_call" | custom-call | bytes 2097152 | tf_op jit(solution)/shard_map/pick_own/pallas_call | solution.py:59
  5.3 0.0 copy-start
  5.3 0.0 copy-start.3
  5.3 0.0 copy-start.4
  5.3 2.7 %collective-permute-start.1 = (bf16[1,2,64,512]{3,2,1,0:T(8,128)(2,1)S(1)}, bf16[1,2,64,512]{3,2,1,0:T(8,128)(2,1)S(1)}, u32[]{:S(2)}, u32[]{:S(2)}) collective-permute-start(bf16[1,2,64,512]{3,2,1,0:T(8,128)(2,1)S(1)} %fusion.2), channel_id=1, source_target_pairs={{0,16},{8,24},{16,0},{24,8},{1,17},{9,25},{17,1},{25,9},{2,18},{10... | collective-permute-start | bytes 393224 | tf_op jit(solution)/shard_map/ppermute | solution.py:18
  8.0 0.0 collective-permute-done.3
  8.0 0.1 collective-permute-start.7
  8.2 0.4 collective-permute-start.4
  8.6 3.8 %collective-permute-done.1 = bf16[1,2,64,512]{3,2,1,0:T(8,128)(2,1)S(1)} collective-permute-done((bf16[1,2,64,512]{3,2,1,0:T(8,128)(2,1)S(1)}, bf16[1,2,64,512]{3,2,1,0:T(8,128)(2,1)S(1)}, u32[]{:S(2)}, u32[]{:S(2)}) %collective-permute-start.1) | collective-permute-done | bytes 131104 | tf_op jit(solution)/shard_map/ppermute | solution.py:18
  12.4 0.1 fusion.1
  12.4 4.1 %collective-permute-start.2 = (bf16[2,64,512]{2,1,0:T(8,128)(2,1)S(1)}, bf16[2,64,512]{2,1,0:T(8,128)(2,1)S(1)}, u32[]{:S(2)}, u32[]{:S(2)}) collective-permute-start(bf16[2,64,512]{2,1,0:T(8,128)(2,1)S(1)} %fusion.1), channel_id=1, source_target_pairs={{0,6},{1,7},{2,4},{3,5},{4,2},{5,3},{6,0},{7,1},{8,14},{9,15},{10,... | collective-permute-start | bytes 393224 | tf_op jit(solution)/shard_map/ppermute | solution.py:18
  16.6 0.1 fusion.9
  16.6 1.6 %collective-permute-start.5 = (bf16[1,64,512]{2,1,0:T(8,128)(2,1)S(1)}, bf16[1,64,512]{2,1,0:T(8,128)(2,1)S(1)}, u32[]{:S(2)}, u32[]{:S(2)}) collective-permute-start(bf16[1,64,512]{2,1,0:T(8,128)(2,1)S(1)} %get-tuple-element.49), channel_id=1, source_target_pairs={{0,1},{1,0},{2,3},{3,2},{4,5},{5,4},{6,7},{7,6},{8,9},{9,8},{10,11... | collective-permute-start | bytes 196616 | tf_op jit(solution)/shard_map/ppermute | solution.py:18
  18.2 0.0 collective-permute-done.7
  18.2 0.1 fusion.5
  18.2 1.6 %collective-permute-start.8 = (bf16[1,2,64,512]{3,2,1,0:T(8,128)(2,1)S(1)}, bf16[1,2,64,512]{3,2,1,0:T(8,128)(2,1)S(1)}, u32[]{:S(2)}, u32[]{:S(2)}) collective-permute-start(bf16[1,2,64,512]{3,2,1,0:T(8,128)(2,1)S(1)} %get-tuple-element.47), channel_id=1, source_target_pairs={{0,16},{8,24},{16,0},{24,8},{1,17},{9,25},{17,1},{25,9},{2,18},{10... | collective-permute-start | bytes 393224 | tf_op jit(solution)/shard_map/ppermute | solution.py:18
  19.8 1.1 %collective-permute-done.5 = bf16[1,64,512]{2,1,0:T(8,128)(2,1)S(1)} collective-permute-done((bf16[1,64,512]{2,1,0:T(8,128)(2,1)S(1)}, bf16[1,64,512]{2,1,0:T(8,128)(2,1)S(1)}, u32[]{:S(2)}, u32[]{:S(2)}) %collective-permute-start.5) | collective-permute-done | bytes 65568 | tf_op jit(solution)/shard_map/ppermute | solution.py:18
  21.0 2.4 %collective-permute-start.6 = (bf16[2,64,512]{2,1,0:T(8,128)(2,1)S(1)}, bf16[2,64,512]{2,1,0:T(8,128)(2,1)S(1)}, u32[]{:S(2)}, u32[]{:S(2)}) collective-permute-start(bf16[2,64,512]{2,1,0:T(8,128)(2,1)S(1)} %pad_maximum_fusion), channel_id=1, source_target_pairs={{0,4},{1,5},{2,6},{3,7},{4,0},{5,1},{6,2},{7,3},{8,12},{9,13},{10,... | collective-permute-start | bytes 393224 | tf_op jit(solution)/shard_map/ppermute | solution.py:18
  23.4 1.5 %collective-permute-start.10 = (bf16[1,2,64,512]{3,2,1,0:T(8,128)(2,1)S(1)}, bf16[1,2,64,512]{3,2,1,0:T(8,128)(2,1)S(1)}, u32[]{:S(2)}, u32[]{:S(2)}) collective-permute-start(bf16[1,2,64,512]{3,2,1,0:T(8,128)(2,1)S(1)} %get-tuple-element.46), channel_id=1, source_target_pairs={{0,16},{8,24},{16,0},{24,8},{1,17},{9,25},{17,1},{25,9},{2,18},{10... | collective-permute-start | bytes 393224 | tf_op jit(solution)/shard_map/ppermute | solution.py:18
  24.9 0.1 fusion
  24.9 0.8 %collective-permute-start.9 = (bf16[2,64,512]{2,1,0:T(8,128)(2,1)S(1)}, bf16[2,64,512]{2,1,0:T(8,128)(2,1)S(1)}, u32[]{:S(2)}, u32[]{:S(2)}) collective-permute-start(bf16[2,64,512]{2,1,0:T(8,128)(2,1)S(1)} %fusion), channel_id=1, source_target_pairs={{0,2},{1,3},{2,0},{3,1},{4,6},{5,7},{6,4},{7,5},{8,10},{9,11},{10,... | collective-permute-start | bytes 393224 | tf_op jit(solution)/shard_map/ppermute | solution.py:18
  25.7 2.6 %collective-permute-done.10 = bf16[1,2,64,512]{3,2,1,0:T(8,128)(2,1)S(1)} collective-permute-done((bf16[1,2,64,512]{3,2,1,0:T(8,128)(2,1)S(1)}, bf16[1,2,64,512]{3,2,1,0:T(8,128)(2,1)S(1)}, u32[]{:S(2)}, u32[]{:S(2)}) %collective-permute-start.10) | collective-permute-done | bytes 131104 | tf_op jit(solution)/shard_map/ppermute | solution.py:18
  28.3 0.1 fusion.6
  28.4 0.0 copy-start.1
  28.4 0.0 copy-start.2
  28.4 1.6 %collective-permute-start.11 = (bf16[2,64,512]{2,1,0:T(8,128)(2,1)S(1)}, bf16[2,64,512]{2,1,0:T(8,128)(2,1)S(1)}, u32[]{:S(2)}, u32[]{:S(2)}) collective-permute-start(bf16[2,64,512]{2,1,0:T(8,128)(2,1)S(1)} %pad_maximum_fusion.1), channel_id=1, source_target_pairs={{0,1},{1,0},{2,3},{3,2},{4,5},{5,4},{6,7},{7,6},{8,9},{9,8},{10,11... | collective-permute-start | bytes 393224 | tf_op jit(solution)/shard_map/ppermute | solution.py:18
  30.0 1.5 %collective-permute-start.12 = (bf16[1,64,512]{2,1,0:T(8,128)(2,1)S(1)}, bf16[1,64,512]{2,1,0:T(8,128)(2,1)S(1)}, u32[]{:S(2)}, u32[]{:S(2)}) collective-permute-start(bf16[1,64,512]{2,1,0:T(8,128)(2,1)S(1)} %slice.158), channel_id=1, source_target_pairs={{0,1},{1,0},{2,3},{3,2},{4,5},{5,4},{6,7},{7,6},{8,9},{9,8},{10,11... | collective-permute-start | bytes 196616 | tf_op jit(solution)/shard_map/ppermute | solution.py:18
  31.5 2.0 %collective-permute-done.11.refs_4_ = bf16[2,64,512]{2,1,0:T(8,128)(2,1)S(1)} collective-permute-done((bf16[2,64,512]{2,1,0:T(8,128)(2,1)S(1)}, bf16[2,64,512]{2,1,0:T(8,128)(2,1)S(1)}, u32[]{:S(2)}, u32[]{:S(2)}) %collective-permute-start.11) | collective-permute-done | bytes 131104 | tf_op jit(solution)/shard_map/ppermute | solution.py:18
  33.5 0.9 %collective-permute-done.12.refs_5_ = bf16[1,64,512]{2,1,0:T(8,128)(2,1)S(1)} collective-permute-done((bf16[1,64,512]{2,1,0:T(8,128)(2,1)S(1)}, bf16[1,64,512]{2,1,0:T(8,128)(2,1)S(1)}, u32[]{:S(2)}, u32[]{:S(2)}) %collective-permute-start.12) | collective-permute-done | bytes 65568 | tf_op jit(solution)/shard_map/ppermute | solution.py:18
  34.3 2.4 %precondition.1 = (bf16[2,64,512]{2,1,0:T(8,128)(2,1)S(1)}, bf16[2,64,512]{2,1,0:T(8,128)(2,1)S(1)}, bf16[1,64,512]{2,1,0:T(8,128)(2,1)S(1)}, bf16[1,64,512]{2,1...) custom-call(bf16[2,64,512]{2,1,0:T(8,128)(2,1)S(1)} %collective-perm, ...), custom_call_target="tpu_custom_call" | custom-call | flops 536870912 | bytes 3145728 | tf_op jit(solution)/shard_map/precondition/pallas_call | solution.py:117
  36.7 1.5 %collective-permute-start.14 = (bf16[1,64,512]{2,1,0:T(8,128)(2,1)S(1)}, bf16[1,64,512]{2,1,0:T(8,128)(2,1)S(1)}, u32[]{:S(2)}, u32[]{:S(2)}) collective-permute-start(bf16[1,64,512]{2,1,0:T(8,128)(2,1)S(1)} %get-tuple-element.36), channel_id=1, source_target_pairs={{0,1},{1,0},{2,3},{3,2},{4,5},{5,4},{6,7},{7,6},{8,9},{9,8},{10,11... | collective-permute-start | bytes 196616 | tf_op jit(solution)/shard_map/ppermute | solution.py:18
  38.2 2.1 %collective-permute-start.13 = (bf16[2,64,512]{2,1,0:T(8,128)(2,1)S(1)}, bf16[2,64,512]{2,1,0:T(8,128)(2,1)S(1)}, u32[]{:S(2)}, u32[]{:S(2)}) collective-permute-start(bf16[2,64,512]{2,1,0:T(8,128)(2,1)S(1)} %get-tuple-element.34), channel_id=1, source_target_pairs={{0,6},{1,7},{2,4},{3,5},{4,2},{5,3},{6,0},{7,1},{8,14},{9,15},{10,... | collective-permute-start | bytes 393224 | tf_op jit(solution)/shard_map/ppermute | solution.py:18
  40.3 0.0 collective-permute-start.16
  40.3 0.8 %collective-permute-done.14 = bf16[1,64,512]{2,1,0:T(8,128)(2,1)S(1)} collective-permute-done((bf16[1,64,512]{2,1,0:T(8,128)(2,1)S(1)}, bf16[1,64,512]{2,1,0:T(8,128)(2,1)S(1)}, u32[]{:S(2)}, u32[]{:S(2)}) %collective-permute-start.14) | collective-permute-done | bytes 65568 | tf_op jit(solution)/shard_map/ppermute | solution.py:18
  41.1 1.6 %collective-permute-start.15 = (bf16[2,64,512]{2,1,0:T(8,128)(2,1)S(1)}, bf16[2,64,512]{2,1,0:T(8,128)(2,1)S(1)}, u32[]{:S(2)}, u32[]{:S(2)}) collective-permute-start(bf16[2,64,512]{2,1,0:T(8,128)(2,1)S(1)} %pad_maximum_fusion.2), channel_id=1, source_target_pairs={{0,4},{1,5},{2,6},{3,7},{4,0},{5,1},{6,2},{7,3},{8,12},{9,13},{10,... | collective-permute-start | bytes 393224 | tf_op jit(solution)/shard_map/ppermute | solution.py:18
  42.7 3.3 %collective-permute-done.13.refs_0_ = bf16[2,64,512]{2,1,0:T(8,128)(2,1)S(1)} collective-permute-done((bf16[2,64,512]{2,1,0:T(8,128)(2,1)S(1)}, bf16[2,64,512]{2,1,0:T(8,128)(2,1)S(1)}, u32[]{:S(2)}, u32[]{:S(2)}) %collective-permute-start.13) | collective-permute-done | bytes 131104 | tf_op jit(solution)/shard_map/ppermute | solution.py:18
  46.0 0.6 %collective-permute-start.17 = (bf16[2,64,512]{2,1,0:T(8,128)(2,1)S(1)}, bf16[2,64,512]{2,1,0:T(8,128)(2,1)S(1)}, u32[]{:S(2)}, u32[]{:S(2)}) collective-permute-start(bf16[2,64,512]{2,1,0:T(8,128)(2,1)S(1)} %pad_maximum_fusion.3), channel_id=1, source_target_pairs={{0,1},{1,0},{2,3},{3,2},{4,5},{5,4},{6,7},{7,6},{8,9},{9,8},{10,11... | collective-permute-start | bytes 393224 | tf_op jit(solution)/shard_map/ppermute | solution.py:18
  46.6 0.6 %collective-permute-done.16.refs_2_ = bf16[2,64,512]{2,1,0:T(8,128)(2,1)S(1)} collective-permute-done((bf16[2,64,512]{2,1,0:T(8,128)(2,1)S(1)}, bf16[2,64,512]{2,1,0:T(8,128)(2,1)S(1)}, u32[]{:S(2)}, u32[]{:S(2)}) %collective-permute-start.16) | collective-permute-done | bytes 131104 | tf_op jit(solution)/shard_map/ppermute | solution.py:18
  47.2 1.0 %collective-permute-start.18 = (bf16[1,64,512]{2,1,0:T(8,128)(2,1)S(1)}, bf16[1,64,512]{2,1,0:T(8,128)(2,1)S(1)}, u32[]{:S(2)}, u32[]{:S(2)}) collective-permute-start(bf16[1,64,512]{2,1,0:T(8,128)(2,1)S(1)} %slice.160), channel_id=1, source_target_pairs={{0,1},{1,0},{2,3},{3,2},{4,5},{5,4},{6,7},{7,6},{8,9},{9,8},{10,11... | collective-permute-start | bytes 196616 | tf_op jit(solution)/shard_map/ppermute | solution.py:18
  48.2 2.1 %statistics.1 = (f32[1,512,512]{2,1,0:T(8,128)}, f32[1,512,512]{2,1,0:T(8,128)}, f32[1,512,512]{2,1,0:T(8,128)}) custom-call(bf16[512,512]{1,0:T(8,128)(2,1)S(1)} %get-tuple-element.40.block, f32[1,512,512]{2,1,0:T(8,128)S(1)} %copy-done.1, f32[1,512,512]{2,1,0:T(8,128)S(1)} %copy-done.2, f32[1,512,512]{2,1,0:T(8,128)S(1)} %copy-done), custom_call_target="tpu_custom_call" | custom-call | flops 536870912 | bytes 6815744 | tf_op jit(solution)/shard_map/statistics/pallas_call | solution.py:155
  50.3 0.0 collective-permute-done.15.refs_1_
  50.3 1.4 %collective-permute-done.18.refs_5_ = bf16[1,64,512]{2,1,0:T(8,128)(2,1)S(1)} collective-permute-done((bf16[1,64,512]{2,1,0:T(8,128)(2,1)S(1)}, bf16[1,64,512]{2,1,0:T(8,128)(2,1)S(1)}, u32[]{:S(2)}, u32[]{:S(2)}) %collective-permute-start.18) | collective-permute-done | bytes 65568 | tf_op jit(solution)/shard_map/ppermute | solution.py:18
  51.8 0.0 collective-permute-done.17.refs_4_
  51.8 0.8 %assemble.1 = bf16[2,64,2048]{2,1,0:T(8,128)(2,1)} custom-call(bf16[2,64,512]{2,1,0:T(8,128)(2,1)S(1)} %collective-permute-done.13.refs_0_, bf16[2,64,512]{2,1,0:T(8,128)(2,1)S(1)} %collective-permute-done.15.refs_1_, bf16[2,64,512]{2,1,0:T(8,128)(2,1)S(1)} %collective-permute-done.16.refs_2_, bf16[1,64,512]{2,1,0:T(8,128)(2,1)S(1)} %get-tuple-element.38.refs_3_, ...), custom_call_target="tpu_custom_call" | custom-call | bytes 1048576 | tf_op jit(solution)/shard_map/assemble/pallas_call | solution.py:189
  (20 shorter events, 0.2 us)
Async XLA Ops:
  1.9 1.7 %collective-permute-start = (bf16[1,2,2,64,512]{4,3,2,1,0:T(8,128)(2,1)S(1)}, bf16[1,2,2,64,512]{4,3,2,1,0:T(8,128)(2,1)S(1)}, u32[]{:S(2)}, u32[]{:S(2)}) collective-permute-start(bf16[1,2,2,64,512]{4,3,2,1,0:T(8,128)(2,1)S(1)} %get-tuple-element.25), channel_id=1, source_target_pairs={{0,8},{8,0},{16,24},{24,16},{1,9},{9,1},{17,25},{25,17},{2,10},{10... | collective-permute-start | bytes 786440 | tf_op jit(solution)/shard_map/ppermute | solution.py:18
  3.6 4.4 %collective-permute-start.3 = (bf16[1,2,2,64,512]{4,3,2,1,0:T(8,128)(2,1)S(1)}, bf16[1,2,2,64,512]{4,3,2,1,0:T(8,128)(2,1)S(1)}, u32[]{:S(2)}, u32[]{:S(2)}) collective-permute-start(bf16[1,2,2,64,512]{4,3,2,1,0:T(8,128)(2,1)S(1)} %get-tuple-element.29), channel_id=1, source_target_pairs={{0,8},{8,0},{16,24},{24,16},{1,9},{9,1},{17,25},{25,17},{2,10},{10... | collective-permute-start | bytes 786440 | tf_op jit(solution)/shard_map/ppermute | solution.py:18
  5.3 29.1 %copy-start = (f32[1,512,512]{2,1,0:T(8,128)S(1)}, f32[1,512,512]{2,1,0:T(8,128)}, u32[]{:S(2)}) copy-start(f32[1,512,512]{2,1,0:T(8,128)} %accum.1) | copy-start | bytes 3145732
  5.3 29.1 %copy-start.3 = (bf16[1,512,512]{2,1,0:T(8,128)(2,1)S(1)}, bf16[1,512,512]{2,1,0:T(8,128)(2,1)}, u32[]{:S(2)}) copy-start(bf16[1,512,512]{2,1,0:T(8,128)(2,1)} %refs_6_.1) | copy-start | bytes 1572868
  5.3 29.0 %copy-start.4 = (bf16[1,512,512]{2,1,0:T(8,128)(2,1)S(1)}, bf16[1,512,512]{2,1,0:T(8,128)(2,1)}, u32[]{:S(2)}) copy-start(bf16[1,512,512]{2,1,0:T(8,128)(2,1)} %refs_7_.1) | copy-start | bytes 1572868
  5.3 7.1 %collective-permute-start.1 = (bf16[1,2,64,512]{3,2,1,0:T(8,128)(2,1)S(1)}, bf16[1,2,64,512]{3,2,1,0:T(8,128)(2,1)S(1)}, u32[]{:S(2)}, u32[]{:S(2)}) collective-permute-start(bf16[1,2,64,512]{3,2,1,0:T(8,128)(2,1)S(1)} %fusion.2), channel_id=1, source_target_pairs={{0,16},{8,24},{16,0},{24,8},{1,17},{9,25},{17,1},{25,9},{2,18},{10... | collective-permute-start | bytes 393224 | tf_op jit(solution)/shard_map/ppermute | solution.py:18
  8.0 10.1 %collective-permute-start.7 = (bf16[2,2,2,64,512]{4,3,2,1,0:T(8,128)(2,1)S(1)}, bf16[2,2,2,64,512]{4,3,2,1,0:T(8,128)(2,1)S(1)}, u32[]{:S(2)}, u32[]{:S(2)}) collective-permute-start(bf16[2,2,2,64,512]{4,3,2,1,0:T(8,128)(2,1)S(1)} %get-tuple-element.32), channel_id=1, source_target_pairs={{0,8},{8,0},{16,24},{24,16},{1,9},{9,1},{17,25},{25,17},{2,10},{10... | collective-permute-start | bytes 1572872 | tf_op jit(solution)/shard_map/ppermute | solution.py:18
  8.2 8.4 %collective-permute-start.4 = (bf16[1,2,64,512]{3,2,1,0:T(8,128)(2,1)S(1)}, bf16[1,2,64,512]{3,2,1,0:T(8,128)(2,1)S(1)}, u32[]{:S(2)}, u32[]{:S(2)}) collective-permute-start(bf16[1,2,64,512]{3,2,1,0:T(8,128)(2,1)S(1)} %fusion.3), channel_id=1, source_target_pairs={{0,16},{8,24},{16,0},{24,8},{1,17},{9,25},{17,1},{25,9},{2,18},{10... | collective-permute-start | bytes 393224 | tf_op jit(solution)/shard_map/ppermute | solution.py:18
  12.4 7.4 %collective-permute-start.2 = (bf16[2,64,512]{2,1,0:T(8,128)(2,1)S(1)}, bf16[2,64,512]{2,1,0:T(8,128)(2,1)S(1)}, u32[]{:S(2)}, u32[]{:S(2)}) collective-permute-start(bf16[2,64,512]{2,1,0:T(8,128)(2,1)S(1)} %fusion.1), channel_id=1, source_target_pairs={{0,6},{1,7},{2,4},{3,5},{4,2},{5,3},{6,0},{7,1},{8,14},{9,15},{10,... | collective-permute-start | bytes 393224 | tf_op jit(solution)/shard_map/ppermute | solution.py:18
  16.6 4.3 %collective-permute-start.5 = (bf16[1,64,512]{2,1,0:T(8,128)(2,1)S(1)}, bf16[1,64,512]{2,1,0:T(8,128)(2,1)S(1)}, u32[]{:S(2)}, u32[]{:S(2)}) collective-permute-start(bf16[1,64,512]{2,1,0:T(8,128)(2,1)S(1)} %get-tuple-element.49), channel_id=1, source_target_pairs={{0,1},{1,0},{2,3},{3,2},{4,5},{5,4},{6,7},{7,6},{8,9},{9,8},{10,11... | collective-permute-start | bytes 196616 | tf_op jit(solution)/shard_map/ppermute | solution.py:18
  18.2 6.6 %collective-permute-start.8 = (bf16[1,2,64,512]{3,2,1,0:T(8,128)(2,1)S(1)}, bf16[1,2,64,512]{3,2,1,0:T(8,128)(2,1)S(1)}, u32[]{:S(2)}, u32[]{:S(2)}) collective-permute-start(bf16[1,2,64,512]{3,2,1,0:T(8,128)(2,1)S(1)} %get-tuple-element.47), channel_id=1, source_target_pairs={{0,16},{8,24},{16,0},{24,8},{1,17},{9,25},{17,1},{25,9},{2,18},{10... | collective-permute-start | bytes 393224 | tf_op jit(solution)/shard_map/ppermute | solution.py:18
  21.0 10.5 %collective-permute-start.6 = (bf16[2,64,512]{2,1,0:T(8,128)(2,1)S(1)}, bf16[2,64,512]{2,1,0:T(8,128)(2,1)S(1)}, u32[]{:S(2)}, u32[]{:S(2)}) collective-permute-start(bf16[2,64,512]{2,1,0:T(8,128)(2,1)S(1)} %pad_maximum_fusion), channel_id=1, source_target_pairs={{0,4},{1,5},{2,6},{3,7},{4,0},{5,1},{6,2},{7,3},{8,12},{9,13},{10,... | collective-permute-start | bytes 393224 | tf_op jit(solution)/shard_map/ppermute | solution.py:18
  23.4 5.0 %collective-permute-start.10 = (bf16[1,2,64,512]{3,2,1,0:T(8,128)(2,1)S(1)}, bf16[1,2,64,512]{3,2,1,0:T(8,128)(2,1)S(1)}, u32[]{:S(2)}, u32[]{:S(2)}) collective-permute-start(bf16[1,2,64,512]{3,2,1,0:T(8,128)(2,1)S(1)} %get-tuple-element.46), channel_id=1, source_target_pairs={{0,16},{8,24},{16,0},{24,8},{1,17},{9,25},{17,1},{25,9},{2,18},{10... | collective-permute-start | bytes 393224 | tf_op jit(solution)/shard_map/ppermute | solution.py:18
  24.9 5.1 %collective-permute-start.9 = (bf16[2,64,512]{2,1,0:T(8,128)(2,1)S(1)}, bf16[2,64,512]{2,1,0:T(8,128)(2,1)S(1)}, u32[]{:S(2)}, u32[]{:S(2)}) collective-permute-start(bf16[2,64,512]{2,1,0:T(8,128)(2,1)S(1)} %fusion), channel_id=1, source_target_pairs={{0,2},{1,3},{2,0},{3,1},{4,6},{5,7},{6,4},{7,5},{8,10},{9,11},{10,... | collective-permute-start | bytes 393224 | tf_op jit(solution)/shard_map/ppermute | solution.py:18
  28.4 19.8 %copy-start.1 = (f32[1,512,512]{2,1,0:T(8,128)S(1)}, f32[1,512,512]{2,1,0:T(8,128)}, u32[]{:S(2)}) copy-start(f32[1,512,512]{2,1,0:T(8,128)} %left.1) | copy-start | bytes 3145732
  28.4 19.8 %copy-start.2 = (f32[1,512,512]{2,1,0:T(8,128)S(1)}, f32[1,512,512]{2,1,0:T(8,128)}, u32[]{:S(2)}) copy-start(f32[1,512,512]{2,1,0:T(8,128)} %right.1) | copy-start | bytes 3145732
  28.4 5.0 %collective-permute-start.11 = (bf16[2,64,512]{2,1,0:T(8,128)(2,1)S(1)}, bf16[2,64,512]{2,1,0:T(8,128)(2,1)S(1)}, u32[]{:S(2)}, u32[]{:S(2)}) collective-permute-start(bf16[2,64,512]{2,1,0:T(8,128)(2,1)S(1)} %pad_maximum_fusion.1), channel_id=1, source_target_pairs={{0,1},{1,0},{2,3},{3,2},{4,5},{5,4},{6,7},{7,6},{8,9},{9,8},{10,11... | collective-permute-start | bytes 393224 | tf_op jit(solution)/shard_map/ppermute | solution.py:18
  30.0 4.3 %collective-permute-start.12 = (bf16[1,64,512]{2,1,0:T(8,128)(2,1)S(1)}, bf16[1,64,512]{2,1,0:T(8,128)(2,1)S(1)}, u32[]{:S(2)}, u32[]{:S(2)}) collective-permute-start(bf16[1,64,512]{2,1,0:T(8,128)(2,1)S(1)} %slice.158), channel_id=1, source_target_pairs={{0,1},{1,0},{2,3},{3,2},{4,5},{5,4},{6,7},{7,6},{8,9},{9,8},{10,11... | collective-permute-start | bytes 196616 | tf_op jit(solution)/shard_map/ppermute | solution.py:18
  36.7 4.3 %collective-permute-start.14 = (bf16[1,64,512]{2,1,0:T(8,128)(2,1)S(1)}, bf16[1,64,512]{2,1,0:T(8,128)(2,1)S(1)}, u32[]{:S(2)}, u32[]{:S(2)}) collective-permute-start(bf16[1,64,512]{2,1,0:T(8,128)(2,1)S(1)} %get-tuple-element.36), channel_id=1, source_target_pairs={{0,1},{1,0},{2,3},{3,2},{4,5},{5,4},{6,7},{7,6},{8,9},{9,8},{10,11... | collective-permute-start | bytes 196616 | tf_op jit(solution)/shard_map/ppermute | solution.py:18
  38.2 7.8 %collective-permute-start.13 = (bf16[2,64,512]{2,1,0:T(8,128)(2,1)S(1)}, bf16[2,64,512]{2,1,0:T(8,128)(2,1)S(1)}, u32[]{:S(2)}, u32[]{:S(2)}) collective-permute-start(bf16[2,64,512]{2,1,0:T(8,128)(2,1)S(1)} %get-tuple-element.34), channel_id=1, source_target_pairs={{0,6},{1,7},{2,4},{3,5},{4,2},{5,3},{6,0},{7,1},{8,14},{9,15},{10,... | collective-permute-start | bytes 393224 | tf_op jit(solution)/shard_map/ppermute | solution.py:18
  40.3 6.9 %collective-permute-start.16 = (bf16[2,64,512]{2,1,0:T(8,128)(2,1)S(1)}, bf16[2,64,512]{2,1,0:T(8,128)(2,1)S(1)}, u32[]{:S(2)}, u32[]{:S(2)}) collective-permute-start(bf16[2,64,512]{2,1,0:T(8,128)(2,1)S(1)} %get-tuple-element.37), channel_id=1, source_target_pairs={{0,2},{1,3},{2,0},{3,1},{4,6},{5,7},{6,4},{7,5},{8,10},{9,11},{10,... | collective-permute-start | bytes 393224 | tf_op jit(solution)/shard_map/ppermute | solution.py:18
  41.1 9.3 %collective-permute-start.15 = (bf16[2,64,512]{2,1,0:T(8,128)(2,1)S(1)}, bf16[2,64,512]{2,1,0:T(8,128)(2,1)S(1)}, u32[]{:S(2)}, u32[]{:S(2)}) collective-permute-start(bf16[2,64,512]{2,1,0:T(8,128)(2,1)S(1)} %pad_maximum_fusion.2), channel_id=1, source_target_pairs={{0,4},{1,5},{2,6},{3,7},{4,0},{5,1},{6,2},{7,3},{8,12},{9,13},{10,... | collective-permute-start | bytes 393224 | tf_op jit(solution)/shard_map/ppermute | solution.py:18
  46.0 5.7 %collective-permute-start.17 = (bf16[2,64,512]{2,1,0:T(8,128)(2,1)S(1)}, bf16[2,64,512]{2,1,0:T(8,128)(2,1)S(1)}, u32[]{:S(2)}, u32[]{:S(2)}) collective-permute-start(bf16[2,64,512]{2,1,0:T(8,128)(2,1)S(1)} %pad_maximum_fusion.3), channel_id=1, source_target_pairs={{0,1},{1,0},{2,3},{3,2},{4,5},{5,4},{6,7},{7,6},{8,9},{9,8},{10,11... | collective-permute-start | bytes 393224 | tf_op jit(solution)/shard_map/ppermute | solution.py:18
  47.2 4.6 %collective-permute-start.18 = (bf16[1,64,512]{2,1,0:T(8,128)(2,1)S(1)}, bf16[1,64,512]{2,1,0:T(8,128)(2,1)S(1)}, u32[]{:S(2)}, u32[]{:S(2)}) collective-permute-start(bf16[1,64,512]{2,1,0:T(8,128)(2,1)S(1)} %slice.160), channel_id=1, source_target_pairs={{0,1},{1,0},{2,3},{3,2},{4,5},{5,4},{6,7},{7,6},{8,9},{9,8},{10,11... | collective-permute-start | bytes 196616 | tf_op jit(solution)/shard_map/ppermute | solution.py:18

commit v3 on v2

v3 whole, which is shorter than its diff:
```python
import functools

import jax
import jax.numpy as jnp
from jax import lax
from jax.experimental import pallas as pl
from jax.experimental.pallas import tpu as pltpu
from jax.sharding import PartitionSpec as P

MIB = 1024 * 1024
ANY = pl.BlockSpec(memory_space=pl.ANY)
VMEM = pl.BlockSpec(memory_space=pltpu.VMEM)


def swap(x, axis, bit):
    n = lax.axis_size(axis)
    return lax.ppermute(x, axis, [(i, i ^ bit) for i in range(n)])


def peer(k, e):
    return jnp.bitwise_xor(lax.axis_index("fsdp"), 2 * k + e)


def pick_kernel(other, grads, out, sem):
    slabs = grads.shape[1]
    block = out.shape[-1]
    per_rep = lax.axis_size("fsdp") // slabs
    rep = jnp.bitwise_xor(lax.axis_index("rep"), 1 if other else 0)
    copies = []
    for k in range(out.shape[0]):
        for j in range(out.shape[1]):
            for e in range(2):
                to = peer(k, e)
                column = jnp.bitwise_xor(rep, 2 * j) * per_rep + to // slabs
                start = pl.multiple_of(column * block, block)
                copies.append(
                    pltpu.make_async_copy(
                        grads.at[0, lax.rem(to, slabs), :, pl.ds(start, block)],
                        out.at[k, j, e],
                        sem,
                    )
                )
    for copy in copies:
        copy.start()
    for copy in copies:
        copy.wait()


def pick(grads, other):
    rows = grads.shape[2]
    fsdp_count = lax.axis_size("fsdp")
    shape = (fsdp_count // 2, lax.axis_size("rep") // 2, 2, rows, rows * fsdp_count)
    return pl.pallas_call(
        functools.partial(pick_kernel, other),
        out_shape=jax.ShapeDtypeStruct(shape, grads.dtype),
        in_specs=[ANY],
        out_specs=ANY,
        scratch_shapes=[pltpu.SemaphoreType.DMA],
        compiler_params=pltpu.CompilerParams(vmem_limit_bytes=4 * MIB),
        cost_estimate=pl.CostEstimate(flops=0, bytes_accessed=2 * MIB, transcendentals=0),
        name="pick_other" if other else "pick_own",
    )(pltpu.with_memory_space_constraint(grads, pltpu.HBM))


def place(k, e, rows):
    return pl.ds(pl.multiple_of(peer(k, e) * rows, rows), rows)


def main_kernel(spots, *refs):
    ins, refs = refs[: len(spots)], refs[len(spots) :]
    left_root, right_root, accum = refs[:3]
    outs, refs = refs[3 : 3 + len(spots)], refs[3 + len(spots) :]
    block_out, lroot, rroot, acc, sems = refs
    rows = ins[0].shape[-2]

    lcopy = pltpu.make_async_copy(left_root.at[0], lroot, sems.at[1])
    rcopy = pltpu.make_async_copy(right_root.at[0], rroot, sems.at[2])
    acopy = pltpu.make_async_copy(accum.at[0], acc, sems.at[3])
    copies = [
        pltpu.make_async_copy(ref.at[i], block_out.at[place(k, e, rows)], sems.at[0])
        for ref, spot in zip(ins, spots)
        for i, (k, e) in enumerate(spot)
    ]
    lcopy.start()
    for copy in copies:
        copy.start()
    rcopy.start()
    acopy.start()
    lcopy.wait()
    for copy in copies:
        copy.wait()
    b = block_out[...]
    half = jnp.dot(lroot[...], b, preferred_element_type=jnp.float32).astype(jnp.bfloat16)
    rcopy.wait()
    precond = jnp.dot(half, rroot[...], preferred_element_type=jnp.float32)
    acopy.wait()
    wide = b.astype(jnp.float32)
    square = wide * wide
    ada_sq = jnp.sum(square / (acc[...] + square))
    pre_sq = jnp.sum(precond * precond)
    ratio = jnp.sqrt(ada_sq) / jnp.sqrt(pre_sq + 1e-06)
    lroot[...] = (ratio * precond).astype(jnp.bfloat16)
    for ref, spot in zip(outs, spots):
        for i, (k, e) in enumerate(spot):
            ref[i] = lroot[place(k, e, rows)]


def precondition(pieces, spots, left_root, right_root, accum):
    side = left_root.shape[1]
    rows = pieces[0].shape[-2]
    outs = pl.pallas_call(
        functools.partial(main_kernel, spots),
        out_shape=[
            jax.ShapeDtypeStruct((len(s), rows, side), jnp.bfloat16) for s in spots
        ]
        + [jax.ShapeDtypeStruct((side, side), jnp.bfloat16)],
        in_specs=[ANY] * (len(spots) + 3),
        out_specs=[VMEM] * (len(spots) + 1),
        scratch_shapes=[
            pltpu.VMEM((side, side), jnp.bfloat16),
            pltpu.VMEM((side, side), jnp.bfloat16),
            pltpu.VMEM((side, side), jnp.float32),
            pltpu.SemaphoreType.DMA((4,)),
        ],
        compiler_params=pltpu.CompilerParams(vmem_limit_bytes=16 * MIB),
        cost_estimate=pl.CostEstimate(
            flops=4 * side**3, bytes_accessed=12 * side * side, transcendentals=0
        ),
        name="precondition",
    )(*pieces, left_root, right_root, accum)
    return dict(zip(spots, outs)), outs[-1]


def stats_kernel(block, left, right, accum, left_out, right_out, accum_out):
    b = block[...]
    wide = b.astype(jnp.float32)
    accum_out[0] = accum[0] + wide * wide
    left_out[0] = left[0] + lax.dot_general(
        b, b, (((1,), (1,)), ((), ())), preferred_element_type=jnp.float32
    )
    right_out[0] = right[0] + lax.dot_general(
        b, b, (((0,), (0,)), ((), ())), preferred_element_type=jnp.float32
    )


def statistics(block, left, right, accum):
    shape = jax.ShapeDtypeStruct(left.shape, jnp.float32)
    side = left.shape[1]
    return pl.pallas_call(
        stats_kernel,
        out_shape=(shape,) * 3,
        in_specs=[VMEM] * 4,
        out_specs=(VMEM,) * 3,
        compiler_params=pltpu.CompilerParams(vmem_limit_bytes=20 * MIB),
        cost_estimate=pl.CostEstimate(
            flops=4 * side**3, bytes_accessed=26 * side * side, transcendentals=0
        ),
        name="statistics",
    )(block, left, right, accum)


def assemble_kernel(spots, *refs):
    ins, (update, sem) = refs[: len(spots)], refs[len(spots) :]
    slabs = update.shape[0]
    block = ins[0].shape[-1]
    copies = []
    for ref, spot in zip(ins, spots):
        for i, (k, e) in enumerate(spot):
            owner = peer(k, e)
            start = pl.multiple_of(owner // slabs * block, block)
            copies.append(
                pltpu.make_async_copy(
                    ref.at[i], update.at[lax.rem(owner, slabs), :, pl.ds(start, block)], sem
                )
            )
    for copy in copies:
        copy.start()
    for copy in copies:
        copy.wait()


def assemble(pieces, spots, shape):
    return pl.pallas_call(
        functools.partial(assemble_kernel, spots),
        out_shape=jax.ShapeDtypeStruct(shape, jnp.bfloat16),
        in_specs=[ANY] * len(pieces),
        out_specs=ANY,
        scratch_shapes=[pltpu.SemaphoreType.DMA],
        compiler_params=pltpu.CompilerParams(vmem_limit_bytes=4 * MIB),
        cost_estimate=pl.CostEstimate(flops=0, bytes_accessed=MIB, transcendentals=0),
        name="assemble",
    )(*pieces)


def exchange(get, peers, far_last):
    ks = range(peers) if far_last else range(peers - 1, -1, -1)
    spots = [(k, e) for k in ks for e in (1, 0)]
    pieces = [swap(get(k, e), "fsdp", 2 * k + e) if k + e else get(k, e) for k, e in spots]
    return pieces, tuple((spot,) for spot in spots)


def wide(terms):
    return sum(t.astype(jnp.float32) for t in terms)


def total(terms):
    return wide(terms).astype(jnp.bfloat16)


def body(grads, left_stat, right_stat, left_root, right_root, accum):
    rep_count, fsdp_count = lax.axis_size("rep"), lax.axis_size("fsdp")
    peers = fsdp_count // 2
    slabs, rows, width = grads.shape[1:]

    theirs = swap(pick(grads, True), "rep", 1)
    ours = pick(grads, False)
    summed = {}
    for k in range(peers):
        terms, bit = [theirs[k], ours[k]], 1
        while 2 * bit < rep_count:
            bit *= 2
            pairs = [t.reshape((t.shape[0] // 2, 2) + t.shape[1:]) for t in terms]
            part = swap(total([p[:, 1] for p in pairs]), "rep", bit)
            kept = lax.optimization_barrier(wide([p[:, 0] for p in pairs]))
            terms = [kept, part]
        summed[k] = [t[0] for t in terms]

    def summed_piece(k, e):
        return total([t[e : e + 1] for t in summed[k]])

    pieces, spots = exchange(summed_piece, peers, True)

    scaled, block = precondition(pieces, spots, left_root, right_root, accum)
    pieces, spots = exchange(lambda k, e: scaled[((k, e),)], peers, False)
    left_new, right_new, accum_new = statistics(block, left_stat, right_stat, accum)
    update = assemble(pieces, spots, (slabs, rows, width // rep_count))
    return (update, left_new, right_new, accum_new)


def solution(mesh):
    owned = P(("rep", "fsdp"), None, None)
    return jax.shard_map(
        body,
        mesh=mesh,
        in_specs=(P("rep", None, "fsdp", None),) + (owned,) * 5,
        out_specs=(P(None, "fsdp", "rep"),) + (owned,) * 3,
        check_vma=False,
    )
```

time: 53.2 us -> 47.7 us (0.90)
  waiting for transfers between devices: 17.6 us -> 8.32 us
  starting transfers between devices: 25.9 us -> 30 us
    ppermute x19, waiting for transfers between devices: 17.6 us -> 8.32 us  [swap(): return lax.ppermute(x, axis, [(i, i ^ bit) for i in range(n)])]
    ppermute x19, starting transfers between devices: 25.9 us -> 30 us  [swap(): return lax.ppermute(x, axis, [(i, i ^ bit) for i in range(n)])]
  transfers between devices with their start and end apart: 19 -> 19, of which waited for: 10 -> 9; matrix products, arithmetic and copies ran while one was open for 1% -> 0% of each run, Pallas kernels for 6% -> 7%
where the time goes in v3:
time: 47.7 us; the launch traced here: 47.4 us
  starting transfers between devices  30 us (63%)
  waiting for transfers between devices  8.32 us (17%)
  Pallas kernels  7.9 us (17%)
  between operations  0.74 us (2%)
    ppermute x19, starting transfers between devices, swap(): return lax.ppermute(x, axis, [(i, i ^ bit) for i in range(n)])  30 us
    ppermute x19, waiting for transfers between devices, swap(): return lax.ppermute(x, axis, [(i, i ^ bit) for i in range(n)])  8.32 us
    pallas_call x2, Pallas kernels, pick(): pl.pallas_call(functools.partial(pick_kernel, other), out_shape=jax.Shape...  2.52 us
    pallas_call x1, Pallas kernels, precondition(): pl.pallas_call(functools.partial(main_kernel, spots), out_shape=[jax.Shap...  2.45 us
    pallas_call x1, Pallas kernels, statistics(): pl.pallas_call(stats_kernel, out_shape=(shape,) * 3, in_specs=[VMEM] * 4,...  2.15 us
  transfers between devices with their start and end apart: 19, of which 9 were waited for; matrix products, arithmetic and copies ran while one was open for 0% of the time, Pallas kernels for 7%

profile of v3, /device:TPU:0, one launch (start us, length us, event | category | flops | bytes accessed | tf_op | source)
XLA Modules:
  0.0 47.4 jit_solution(14812241276350552749)
XLA Ops:
  0.6 1.3 %pick_other.1 = bf16[4,2,2,64,512]{4,3,2,1,0:T(8,128)(2,1)S(1)} custom-call(bf16[1,2,64,8192]{3,2,1,0:T(8,128)(2,1)} %grads.3), custom_call_target="tpu_custom_call" | custom-call | bytes 2097152 | tf_op jit(solution)/shard_map/pick_other/pallas_call | solution.py:53
  1.9 0.5 %collective-permute-start = (bf16[4,2,2,64,512]{4,3,2,1,0:T(8,128)(2,1)S(1)}, bf16[4,2,2,64,512]{4,3,2,1,0:T(8,128)(2,1)S(1)}, u32[]{:S(2)}, u32[]{:S(2)}) collective-permute-start(bf16[4,2,2,64,512]{4,3,2,1,0:T(8,128)(2,1)S(1)} %pick_other.1), channel_id=1, source_target_pairs={{0,8},{8,0},{16,24},{24,16},{1,9},{9,1},{17,25},{25,17},{2,10},{10... | collective-permute-start | bytes 3145736 | tf_op jit(solution)/shard_map/ppermute | solution.py:17
  2.4 1.2 %pick_own.1 = bf16[4,2,2,64,512]{4,3,2,1,0:T(8,128)(2,1)S(1)} custom-call(bf16[1,2,64,8192]{3,2,1,0:T(8,128)(2,1)} %grads.3), custom_call_target="tpu_custom_call" | custom-call | bytes 2097152 | tf_op jit(solution)/shard_map/pick_own/pallas_call | solution.py:53
  3.7 0.0 copy-start
  3.7 0.0 copy-start.3
  3.7 0.0 copy-start.4
  3.7 1.0 %collective-permute-done = bf16[4,2,2,64,512]{4,3,2,1,0:T(8,128)(2,1)S(1)} collective-permute-done((bf16[4,2,2,64,512]{4,3,2,1,0:T(8,128)(2,1)S(1)}, bf16[4,2,2,64,512]{4,3,2,1,0:T(8,128)(2,1)S(1)}, u32[]{:S(2)}, u32[]{:S(2)}) %collective-permute-start) | collective-permute-done | bytes 1048608 | tf_op jit(solution)/shard_map/ppermute | solution.py:17
  4.7 0.3 fusion.3
  5.0 3.0 %collective-permute-start.9 = (bf16[1,2,64,512]{3,2,1,0:T(8,128)(2,1)S(1)}, bf16[1,2,64,512]{3,2,1,0:T(8,128)(2,1)S(1)}, u32[]{:S(2)}, u32[]{:S(2)}) collective-permute-start(bf16[1,2,64,512]{3,2,1,0:T(8,128)(2,1)S(1)} %get-tuple-element.28), channel_id=1, source_target_pairs={{0,16},{8,24},{16,0},{24,8},{1,17},{9,25},{17,1},{25,9},{2,18},{10... | collective-permute-start | bytes 393224 | tf_op jit(solution)/shard_map/ppermute | solution.py:17
  8.0 0.1 collective-permute-start.6
  8.0 1.9 %collective-permute-start.3 = (bf16[1,2,64,512]{3,2,1,0:T(8,128)(2,1)S(1)}, bf16[1,2,64,512]{3,2,1,0:T(8,128)(2,1)S(1)}, u32[]{:S(2)}, u32[]{:S(2)}) collective-permute-start(bf16[1,2,64,512]{3,2,1,0:T(8,128)(2,1)S(1)} %get-tuple-element.32), channel_id=1, source_target_pairs={{0,16},{8,24},{16,0},{24,8},{1,17},{9,25},{17,1},{25,9},{2,18},{10... | collective-permute-start | bytes 393224 | tf_op jit(solution)/shard_map/ppermute | solution.py:17
  10.0 0.1 collective-permute-start.1
  10.1 2.2 %collective-permute-done.9 = bf16[1,2,64,512]{3,2,1,0:T(8,128)(2,1)S(1)} collective-permute-done((bf16[1,2,64,512]{3,2,1,0:T(8,128)(2,1)S(1)}, bf16[1,2,64,512]{3,2,1,0:T(8,128)(2,1)S(1)}, u32[]{:S(2)}, u32[]{:S(2)}) %collective-permute-start.9) | collective-permute-done | bytes 131104 | tf_op jit(solution)/shard_map/ppermute | solution.py:17
  12.3 4.2 %collective-permute-start.11 = (bf16[1,64,512]{2,1,0:T(8,128)(2,1)S(1)}, bf16[1,64,512]{2,1,0:T(8,128)(2,1)S(1)}, u32[]{:S(2)}, u32[]{:S(2)}) collective-permute-start(bf16[1,64,512]{2,1,0:T(8,128)(2,1)S(1)} %get-tuple-element.36), channel_id=1, source_target_pairs={{0,6},{1,7},{2,4},{3,5},{4,2},{5,3},{6,0},{7,1},{8,14},{9,15},{10,... | collective-permute-start | bytes 196616 | tf_op jit(solution)/shard_map/ppermute | solution.py:17
  16.5 1.1 %collective-permute-start.10 = (bf16[1,64,512]{2,1,0:T(8,128)(2,1)S(1)}, bf16[1,64,512]{2,1,0:T(8,128)(2,1)S(1)}, u32[]{:S(2)}, u32[]{:S(2)}) collective-permute-start(bf16[1,64,512]{2,1,0:T(8,128)(2,1)S(1)} %get-tuple-element.37), channel_id=1, source_target_pairs={{0,7},{1,6},{2,5},{3,4},{4,3},{5,2},{6,1},{7,0},{8,15},{9,14},{10,... | collective-permute-start | bytes 196616 | tf_op jit(solution)/shard_map/ppermute | solution.py:17
  17.6 0.0 collective-permute-done.6
  17.7 0.9 %collective-permute-start.8 = (bf16[1,64,512]{2,1,0:T(8,128)(2,1)S(1)}, bf16[1,64,512]{2,1,0:T(8,128)(2,1)S(1)}, u32[]{:S(2)}, u32[]{:S(2)}) collective-permute-start(bf16[1,64,512]{2,1,0:T(8,128)(2,1)S(1)} %get-tuple-element.38), channel_id=1, source_target_pairs={{0,4},{1,5},{2,6},{3,7},{4,0},{5,1},{6,2},{7,3},{8,12},{9,13},{10,... | collective-permute-start | bytes 196616 | tf_op jit(solution)/shard_map/ppermute | solution.py:17
  18.5 0.0 collective-permute-done.3
  18.5 3.4 %collective-permute-start.7 = (bf16[1,64,512]{2,1,0:T(8,128)(2,1)S(1)}, bf16[1,64,512]{2,1,0:T(8,128)(2,1)S(1)}, u32[]{:S(2)}, u32[]{:S(2)}) collective-permute-start(bf16[1,64,512]{2,1,0:T(8,128)(2,1)S(1)} %get-tuple-element.39), channel_id=1, source_target_pairs={{0,5},{1,4},{2,7},{3,6},{4,1},{5,0},{6,3},{7,2},{8,13},{9,12},{10,... | collective-permute-start | bytes 196616 | tf_op jit(solution)/shard_map/ppermute | solution.py:17
  22.0 0.0 collective-permute-done.1
  22.0 1.6 %collective-permute-start.5 = (bf16[1,64,512]{2,1,0:T(8,128)(2,1)S(1)}, bf16[1,64,512]{2,1,0:T(8,128)(2,1)S(1)}, u32[]{:S(2)}, u32[]{:S(2)}) collective-permute-start(bf16[1,64,512]{2,1,0:T(8,128)(2,1)S(1)} %get-tuple-element.40), channel_id=1, source_target_pairs={{0,2},{1,3},{2,0},{3,1},{4,6},{5,7},{6,4},{7,5},{8,10},{9,11},{10,... | collective-permute-start | bytes 196616 | tf_op jit(solution)/shard_map/ppermute | solution.py:17
  23.6 0.0 collective-permute-done.11.refs_7_
  23.7 0.5 %collective-permute-start.4 = (bf16[1,64,512]{2,1,0:T(8,128)(2,1)S(1)}, bf16[1,64,512]{2,1,0:T(8,128)(2,1)S(1)}, u32[]{:S(2)}, u32[]{:S(2)}) collective-permute-start(bf16[1,64,512]{2,1,0:T(8,128)(2,1)S(1)} %get-tuple-element.41), channel_id=1, source_target_pairs={{0,3},{1,2},{2,1},{3,0},{4,7},{5,6},{6,5},{7,4},{8,11},{9,10},{10,... | collective-permute-start | bytes 196616 | tf_op jit(solution)/shard_map/ppermute | solution.py:17
  24.1 0.0 collective-permute-done.10.refs_6_
  24.1 1.5 %collective-permute-start.2 = (bf16[1,64,512]{2,1,0:T(8,128)(2,1)S(1)}, bf16[1,64,512]{2,1,0:T(8,128)(2,1)S(1)}, u32[]{:S(2)}, u32[]{:S(2)}) collective-permute-start(bf16[1,64,512]{2,1,0:T(8,128)(2,1)S(1)} %get-tuple-element.43), channel_id=1, source_target_pairs={{0,1},{1,0},{2,3},{3,2},{4,5},{5,4},{6,7},{7,6},{8,9},{9,8},{10,11... | collective-permute-start | bytes 196616 | tf_op jit(solution)/shard_map/ppermute | solution.py:17
  25.6 0.0 collective-permute-done.8.refs_5_
  25.7 1.4 %collective-permute-done.7.refs_4_ = bf16[1,64,512]{2,1,0:T(8,128)(2,1)S(1)} collective-permute-done((bf16[1,64,512]{2,1,0:T(8,128)(2,1)S(1)}, bf16[1,64,512]{2,1,0:T(8,128)(2,1)S(1)}, u32[]{:S(2)}, u32[]{:S(2)}) %collective-permute-start.7) | collective-permute-done | bytes 65568 | tf_op jit(solution)/shard_map/ppermute | solution.py:17
  27.1 0.5 %collective-permute-done.5.refs_3_ = bf16[1,64,512]{2,1,0:T(8,128)(2,1)S(1)} collective-permute-done((bf16[1,64,512]{2,1,0:T(8,128)(2,1)S(1)}, bf16[1,64,512]{2,1,0:T(8,128)(2,1)S(1)}, u32[]{:S(2)}, u32[]{:S(2)}) %collective-permute-start.5) | collective-permute-done | bytes 65568 | tf_op jit(solution)/shard_map/ppermute | solution.py:17
  27.6 1.4 %collective-permute-done.4.refs_2_ = bf16[1,64,512]{2,1,0:T(8,128)(2,1)S(1)} collective-permute-done((bf16[1,64,512]{2,1,0:T(8,128)(2,1)S(1)}, bf16[1,64,512]{2,1,0:T(8,128)(2,1)S(1)}, u32[]{:S(2)}, u32[]{:S(2)}) %collective-permute-start.4) | collective-permute-done | bytes 65568 | tf_op jit(solution)/shard_map/ppermute | solution.py:17
  29.1 0.3 collective-permute-done.2.refs_0_
  29.4 0.0 copy-done.3
  29.4 2.4 %precondition.1 = (bf16[1,64,512]{2,1,0:T(8,128)(2,1)S(1)}, bf16[1,64,512]{2,1,0:T(8,128)(2,1)S(1)}, bf16[1,64,512]{2,1,0:T(8,128)(2,1)S(1)}, bf16[1,64,512]{2,1...) custom-call(bf16[1,64,512]{2,1,0:T(8,128)(2,1)S(1)} %collective-perm, ...), custom_call_target="tpu_custom_call" | custom-call | flops 536870912 | bytes 3145728 | tf_op jit(solution)/shard_map/precondition/pallas_call | solution.py:111
  31.9 3.2 %collective-permute-start.12 = (bf16[1,64,512]{2,1,0:T(8,128)(2,1)S(1)}, bf16[1,64,512]{2,1,0:T(8,128)(2,1)S(1)}, u32[]{:S(2)}, u32[]{:S(2)}) collective-permute-start(bf16[1,64,512]{2,1,0:T(8,128)(2,1)S(1)} %get-tuple-element.16), channel_id=1, source_target_pairs={{0,7},{1,6},{2,5},{3,4},{4,3},{5,2},{6,1},{7,0},{8,15},{9,14},{10,... | collective-permute-start | bytes 196616 | tf_op jit(solution)/shard_map/ppermute | solution.py:17
  35.1 1.2 %collective-permute-start.13 = (bf16[1,64,512]{2,1,0:T(8,128)(2,1)S(1)}, bf16[1,64,512]{2,1,0:T(8,128)(2,1)S(1)}, u32[]{:S(2)}, u32[]{:S(2)}) collective-permute-start(bf16[1,64,512]{2,1,0:T(8,128)(2,1)S(1)} %get-tuple-element.17), channel_id=1, source_target_pairs={{0,6},{1,7},{2,4},{3,5},{4,2},{5,3},{6,0},{7,1},{8,14},{9,15},{10,... | collective-permute-start | bytes 196616 | tf_op jit(solution)/shard_map/ppermute | solution.py:17
  36.3 0.4 collective-permute-start.14
  36.7 2.9 %collective-permute-start.15 = (bf16[1,64,512]{2,1,0:T(8,128)(2,1)S(1)}, bf16[1,64,512]{2,1,0:T(8,128)(2,1)S(1)}, u32[]{:S(2)}, u32[]{:S(2)}) collective-permute-start(bf16[1,64,512]{2,1,0:T(8,128)(2,1)S(1)} %get-tuple-element.19), channel_id=1, source_target_pairs={{0,4},{1,5},{2,6},{3,7},{4,0},{5,1},{6,2},{7,3},{8,12},{9,13},{10,... | collective-permute-start | bytes 196616 | tf_op jit(solution)/shard_map/ppermute | solution.py:17
  39.6 0.8 %collective-permute-start.16 = (bf16[1,64,512]{2,1,0:T(8,128)(2,1)S(1)}, bf16[1,64,512]{2,1,0:T(8,128)(2,1)S(1)}, u32[]{:S(2)}, u32[]{:S(2)}) collective-permute-start(bf16[1,64,512]{2,1,0:T(8,128)(2,1)S(1)} %get-tuple-element.20), channel_id=1, source_target_pairs={{0,3},{1,2},{2,1},{3,0},{4,7},{5,6},{6,5},{7,4},{8,11},{9,10},{10,... | collective-permute-start | bytes 196616 | tf_op jit(solution)/shard_map/ppermute | solution.py:17
  40.4 0.0 collective-permute-done.12.refs_0_
  40.4 1.8 %collective-permute-start.17 = (bf16[1,64,512]{2,1,0:T(8,128)(2,1)S(1)}, bf16[1,64,512]{2,1,0:T(8,128)(2,1)S(1)}, u32[]{:S(2)}, u32[]{:S(2)}) collective-permute-start(bf16[1,64,512]{2,1,0:T(8,128)(2,1)S(1)} %get-tuple-element.21), channel_id=1, source_target_pairs={{0,2},{1,3},{2,0},{3,1},{4,6},{5,7},{6,4},{7,5},{8,10},{9,11},{10,... | collective-permute-start | bytes 196616 | tf_op jit(solution)/shard_map/ppermute | solution.py:17
  42.1 0.0 collective-permute-done.13.refs_1_
  42.1 1.0 %collective-permute-start.18 = (bf16[1,64,512]{2,1,0:T(8,128)(2,1)S(1)}, bf16[1,64,512]{2,1,0:T(8,128)(2,1)S(1)}, u32[]{:S(2)}, u32[]{:S(2)}) collective-permute-start(bf16[1,64,512]{2,1,0:T(8,128)(2,1)S(1)} %get-tuple-element.22), channel_id=1, source_target_pairs={{0,1},{1,0},{2,3},{3,2},{4,5},{5,4},{6,7},{7,6},{8,9},{9,8},{10,11... | collective-permute-start | bytes 196616 | tf_op jit(solution)/shard_map/ppermute | solution.py:17
  43.1 2.1 %statistics.1 = (f32[1,512,512]{2,1,0:T(8,128)}, f32[1,512,512]{2,1,0:T(8,128)}, f32[1,512,512]{2,1,0:T(8,128)}) custom-call(bf16[512,512]{1,0:T(8,128)(2,1)S(1)} %get-tuple-element.24.block, f32[1,512,512]{2,1,0:T(8,128)S(1)} %copy-done.1, f32[1,512,512]{2,1,0:T(8,128)S(1)} %copy-done.2, f32[1,512,512]{2,1,0:T(8,128)S(1)} %copy-done), custom_call_target="tpu_custom_call" | custom-call | flops 536870912 | bytes 6815744 | tf_op jit(solution)/shard_map/statistics/pallas_call | solution.py:149
  45.3 0.6 %collective-permute-done.14.refs_2_ = bf16[1,64,512]{2,1,0:T(8,128)(2,1)S(1)} collective-permute-done((bf16[1,64,512]{2,1,0:T(8,128)(2,1)S(1)}, bf16[1,64,512]{2,1,0:T(8,128)(2,1)S(1)}, u32[]{:S(2)}, u32[]{:S(2)}) %collective-permute-start.14) | collective-permute-done | bytes 65568 | tf_op jit(solution)/shard_map/ppermute | solution.py:17
  45.8 0.2 collective-permute-done.15.refs_3_
  46.0 0.0 collective-permute-done.16.refs_4_
  46.0 0.6 %collective-permute-done.17.refs_5_ = bf16[1,64,512]{2,1,0:T(8,128)(2,1)S(1)} collective-permute-done((bf16[1,64,512]{2,1,0:T(8,128)(2,1)S(1)}, bf16[1,64,512]{2,1,0:T(8,128)(2,1)S(1)}, u32[]{:S(2)}, u32[]{:S(2)}) %collective-permute-start.17) | collective-permute-done | bytes 65568 | tf_op jit(solution)/shard_map/ppermute | solution.py:17
  46.6 0.0 collective-permute-done.18.refs_6_
  46.6 0.8 %assemble.1 = bf16[2,64,2048]{2,1,0:T(8,128)(2,1)} custom-call(bf16[1,64,512]{2,1,0:T(8,128)(2,1)S(1)} %collective-permute-done.12.refs_0_, bf16[1,64,512]{2,1,0:T(8,128)(2,1)S(1)} %collective-permute-done.13.refs_1_, bf16[1,64,512]{2,1,0:T(8,128)(2,1)S(1)} %collective-permute-done.14.refs_2_, bf16[1,64,512]{2,1,0:T(8,128)(2,1)S(1)} %collective-permute-done.15.refs_3_, ...), custom_call_target="tpu_custom_call" | custom-call | bytes 1048576 | tf_op jit(solution)/shard_map/assemble/pallas_call | solution.py:183
  (10 shorter events, 0.1 us)
Async XLA Ops:
  1.9 2.8 %collective-permute-start = (bf16[4,2,2,64,512]{4,3,2,1,0:T(8,128)(2,1)S(1)}, bf16[4,2,2,64,512]{4,3,2,1,0:T(8,128)(2,1)S(1)}, u32[]{:S(2)}, u32[]{:S(2)}) collective-permute-start(bf16[4,2,2,64,512]{4,3,2,1,0:T(8,128)(2,1)S(1)} %pick_other.1), channel_id=1, source_target_pairs={{0,8},{8,0},{16,24},{24,16},{1,9},{9,1},{17,25},{25,17},{2,10},{10... | collective-permute-start | bytes 3145736 | tf_op jit(solution)/shard_map/ppermute | solution.py:17
  3.7 25.7 %copy-start = (f32[1,512,512]{2,1,0:T(8,128)S(1)}, f32[1,512,512]{2,1,0:T(8,128)}, u32[]{:S(2)}) copy-start(f32[1,512,512]{2,1,0:T(8,128)} %accum.1) | copy-start | bytes 3145732
  3.7 25.7 %copy-start.3 = (bf16[1,512,512]{2,1,0:T(8,128)(2,1)S(1)}, bf16[1,512,512]{2,1,0:T(8,128)(2,1)}, u32[]{:S(2)}) copy-start(bf16[1,512,512]{2,1,0:T(8,128)(2,1)} %refs_8_.1) | copy-start | bytes 1572868
  3.7 25.7 %copy-start.4 = (bf16[1,512,512]{2,1,0:T(8,128)(2,1)S(1)}, bf16[1,512,512]{2,1,0:T(8,128)(2,1)}, u32[]{:S(2)}) copy-start(bf16[1,512,512]{2,1,0:T(8,128)(2,1)} %refs_9_.1) | copy-start | bytes 1572868
  5.0 7.2 %collective-permute-start.9 = (bf16[1,2,64,512]{3,2,1,0:T(8,128)(2,1)S(1)}, bf16[1,2,64,512]{3,2,1,0:T(8,128)(2,1)S(1)}, u32[]{:S(2)}, u32[]{:S(2)}) collective-permute-start(bf16[1,2,64,512]{3,2,1,0:T(8,128)(2,1)S(1)} %get-tuple-element.28), channel_id=1, source_target_pairs={{0,16},{8,24},{16,0},{24,8},{1,17},{9,25},{17,1},{25,9},{2,18},{10... | collective-permute-start | bytes 393224 | tf_op jit(solution)/shard_map/ppermute | solution.py:17
  8.0 9.7 %collective-permute-start.6 = (bf16[1,2,64,512]{3,2,1,0:T(8,128)(2,1)S(1)}, bf16[1,2,64,512]{3,2,1,0:T(8,128)(2,1)S(1)}, u32[]{:S(2)}, u32[]{:S(2)}) collective-permute-start(bf16[1,2,64,512]{3,2,1,0:T(8,128)(2,1)S(1)} %get-tuple-element.30), channel_id=1, source_target_pairs={{0,16},{8,24},{16,0},{24,8},{1,17},{9,25},{17,1},{25,9},{2,18},{10... | collective-permute-start | bytes 393224 | tf_op jit(solution)/shard_map/ppermute | solution.py:17
  8.0 10.5 %collective-permute-start.3 = (bf16[1,2,64,512]{3,2,1,0:T(8,128)(2,1)S(1)}, bf16[1,2,64,512]{3,2,1,0:T(8,128)(2,1)S(1)}, u32[]{:S(2)}, u32[]{:S(2)}) collective-permute-start(bf16[1,2,64,512]{3,2,1,0:T(8,128)(2,1)S(1)} %get-tuple-element.32), channel_id=1, source_target_pairs={{0,16},{8,24},{16,0},{24,8},{1,17},{9,25},{17,1},{25,9},{2,18},{10... | collective-permute-start | bytes 393224 | tf_op jit(solution)/shard_map/ppermute | solution.py:17
  10.0 12.0 %collective-permute-start.1 = (bf16[1,2,64,512]{3,2,1,0:T(8,128)(2,1)S(1)}, bf16[1,2,64,512]{3,2,1,0:T(8,128)(2,1)S(1)}, u32[]{:S(2)}, u32[]{:S(2)}) collective-permute-start(bf16[1,2,64,512]{3,2,1,0:T(8,128)(2,1)S(1)} %get-tuple-element.34), channel_id=1, source_target_pairs={{0,16},{8,24},{16,0},{24,8},{1,17},{9,25},{17,1},{25,9},{2,18},{10... | collective-permute-start | bytes 393224 | tf_op jit(solution)/shard_map/ppermute | solution.py:17
  12.3 11.4 %collective-permute-start.11 = (bf16[1,64,512]{2,1,0:T(8,128)(2,1)S(1)}, bf16[1,64,512]{2,1,0:T(8,128)(2,1)S(1)}, u32[]{:S(2)}, u32[]{:S(2)}) collective-permute-start(bf16[1,64,512]{2,1,0:T(8,128)(2,1)S(1)} %get-tuple-element.36), channel_id=1, source_target_pairs={{0,6},{1,7},{2,4},{3,5},{4,2},{5,3},{6,0},{7,1},{8,14},{9,15},{10,... | collective-permute-start | bytes 196616 | tf_op jit(solution)/shard_map/ppermute | solution.py:17
  16.5 26.6 %copy-start.1 = (f32[1,512,512]{2,1,0:T(8,128)S(1)}, f32[1,512,512]{2,1,0:T(8,128)}, u32[]{:S(2)}) copy-start(f32[1,512,512]{2,1,0:T(8,128)} %left.1) | copy-start | bytes 3145732
  16.5 26.6 %copy-start.2 = (f32[1,512,512]{2,1,0:T(8,128)S(1)}, f32[1,512,512]{2,1,0:T(8,128)}, u32[]{:S(2)}) copy-start(f32[1,512,512]{2,1,0:T(8,128)} %right.1) | copy-start | bytes 3145732
  16.5 7.7 %collective-permute-start.10 = (bf16[1,64,512]{2,1,0:T(8,128)(2,1)S(1)}, bf16[1,64,512]{2,1,0:T(8,128)(2,1)S(1)}, u32[]{:S(2)}, u32[]{:S(2)}) collective-permute-start(bf16[1,64,512]{2,1,0:T(8,128)(2,1)S(1)} %get-tuple-element.37), channel_id=1, source_target_pairs={{0,7},{1,6},{2,5},{3,4},{4,3},{5,2},{6,1},{7,0},{8,15},{9,14},{10,... | collective-permute-start | bytes 196616 | tf_op jit(solution)/shard_map/ppermute | solution.py:17
  17.7 8.0 %collective-permute-start.8 = (bf16[1,64,512]{2,1,0:T(8,128)(2,1)S(1)}, bf16[1,64,512]{2,1,0:T(8,128)(2,1)S(1)}, u32[]{:S(2)}, u32[]{:S(2)}) collective-permute-start(bf16[1,64,512]{2,1,0:T(8,128)(2,1)S(1)} %get-tuple-element.38), channel_id=1, source_target_pairs={{0,4},{1,5},{2,6},{3,7},{4,0},{5,1},{6,2},{7,3},{8,12},{9,13},{10,... | collective-permute-start | bytes 196616 | tf_op jit(solution)/shard_map/ppermute | solution.py:17
  18.5 8.5 %collective-permute-start.7 = (bf16[1,64,512]{2,1,0:T(8,128)(2,1)S(1)}, bf16[1,64,512]{2,1,0:T(8,128)(2,1)S(1)}, u32[]{:S(2)}, u32[]{:S(2)}) collective-permute-start(bf16[1,64,512]{2,1,0:T(8,128)(2,1)S(1)} %get-tuple-element.39), channel_id=1, source_target_pairs={{0,5},{1,4},{2,7},{3,6},{4,1},{5,0},{6,3},{7,2},{8,13},{9,12},{10,... | collective-permute-start | bytes 196616 | tf_op jit(solution)/shard_map/ppermute | solution.py:17
  22.0 5.7 %collective-permute-start.5 = (bf16[1,64,512]{2,1,0:T(8,128)(2,1)S(1)}, bf16[1,64,512]{2,1,0:T(8,128)(2,1)S(1)}, u32[]{:S(2)}, u32[]{:S(2)}) collective-permute-start(bf16[1,64,512]{2,1,0:T(8,128)(2,1)S(1)} %get-tuple-element.40), channel_id=1, source_target_pairs={{0,2},{1,3},{2,0},{3,1},{4,6},{5,7},{6,4},{7,5},{8,10},{9,11},{10,... | collective-permute-start | bytes 196616 | tf_op jit(solution)/shard_map/ppermute | solution.py:17
  23.7 5.4 %collective-permute-start.4 = (bf16[1,64,512]{2,1,0:T(8,128)(2,1)S(1)}, bf16[1,64,512]{2,1,0:T(8,128)(2,1)S(1)}, u32[]{:S(2)}, u32[]{:S(2)}) collective-permute-start(bf16[1,64,512]{2,1,0:T(8,128)(2,1)S(1)} %get-tuple-element.41), channel_id=1, source_target_pairs={{0,3},{1,2},{2,1},{3,0},{4,7},{5,6},{6,5},{7,4},{8,11},{9,10},{10,... | collective-permute-start | bytes 196616 | tf_op jit(solution)/shard_map/ppermute | solution.py:17
  24.1 5.2 %collective-permute-start.2 = (bf16[1,64,512]{2,1,0:T(8,128)(2,1)S(1)}, bf16[1,64,512]{2,1,0:T(8,128)(2,1)S(1)}, u32[]{:S(2)}, u32[]{:S(2)}) collective-permute-start(bf16[1,64,512]{2,1,0:T(8,128)(2,1)S(1)} %get-tuple-element.43), channel_id=1, source_target_pairs={{0,1},{1,0},{2,3},{3,2},{4,5},{5,4},{6,7},{7,6},{8,9},{9,8},{10,11... | collective-permute-start | bytes 196616 | tf_op jit(solution)/shard_map/ppermute | solution.py:17
  31.9 8.5 %collective-permute-start.12 = (bf16[1,64,512]{2,1,0:T(8,128)(2,1)S(1)}, bf16[1,64,512]{2,1,0:T(8,128)(2,1)S(1)}, u32[]{:S(2)}, u32[]{:S(2)}) collective-permute-start(bf16[1,64,512]{2,1,0:T(8,128)(2,1)S(1)} %get-tuple-element.16), channel_id=1, source_target_pairs={{0,7},{1,6},{2,5},{3,4},{4,3},{5,2},{6,1},{7,0},{8,15},{9,14},{10,... | collective-permute-start | bytes 196616 | tf_op jit(solution)/shard_map/ppermute | solution.py:17
  35.1 7.1 %collective-permute-start.13 = (bf16[1,64,512]{2,1,0:T(8,128)(2,1)S(1)}, bf16[1,64,512]{2,1,0:T(8,128)(2,1)S(1)}, u32[]{:S(2)}, u32[]{:S(2)}) collective-permute-start(bf16[1,64,512]{2,1,0:T(8,128)(2,1)S(1)} %get-tuple-element.17), channel_id=1, source_target_pairs={{0,6},{1,7},{2,4},{3,5},{4,2},{5,3},{6,0},{7,1},{8,14},{9,15},{10,... | collective-permute-start | bytes 196616 | tf_op jit(solution)/shard_map/ppermute | solution.py:17
  36.3 9.5 %collective-permute-start.14 = (bf16[1,64,512]{2,1,0:T(8,128)(2,1)S(1)}, bf16[1,64,512]{2,1,0:T(8,128)(2,1)S(1)}, u32[]{:S(2)}, u32[]{:S(2)}) collective-permute-start(bf16[1,64,512]{2,1,0:T(8,128)(2,1)S(1)} %get-tuple-element.18), channel_id=1, source_target_pairs={{0,5},{1,4},{2,7},{3,6},{4,1},{5,0},{6,3},{7,2},{8,13},{9,12},{10,... | collective-permute-start | bytes 196616 | tf_op jit(solution)/shard_map/ppermute | solution.py:17
  36.7 9.4 %collective-permute-start.15 = (bf16[1,64,512]{2,1,0:T(8,128)(2,1)S(1)}, bf16[1,64,512]{2,1,0:T(8,128)(2,1)S(1)}, u32[]{:S(2)}, u32[]{:S(2)}) collective-permute-start(bf16[1,64,512]{2,1,0:T(8,128)(2,1)S(1)} %get-tuple-element.19), channel_id=1, source_target_pairs={{0,4},{1,5},{2,6},{3,7},{4,0},{5,1},{6,2},{7,3},{8,12},{9,13},{10,... | collective-permute-start | bytes 196616 | tf_op jit(solution)/shard_map/ppermute | solution.py:17
  39.6 6.5 %collective-permute-start.16 = (bf16[1,64,512]{2,1,0:T(8,128)(2,1)S(1)}, bf16[1,64,512]{2,1,0:T(8,128)(2,1)S(1)}, u32[]{:S(2)}, u32[]{:S(2)}) collective-permute-start(bf16[1,64,512]{2,1,0:T(8,128)(2,1)S(1)} %get-tuple-element.20), channel_id=1, source_target_pairs={{0,3},{1,2},{2,1},{3,0},{4,7},{5,6},{6,5},{7,4},{8,11},{9,10},{10,... | collective-permute-start | bytes 196616 | tf_op jit(solution)/shard_map/ppermute | solution.py:17
  40.4 6.3 %collective-permute-start.17 = (bf16[1,64,512]{2,1,0:T(8,128)(2,1)S(1)}, bf16[1,64,512]{2,1,0:T(8,128)(2,1)S(1)}, u32[]{:S(2)}, u32[]{:S(2)}) collective-permute-start(bf16[1,64,512]{2,1,0:T(8,128)(2,1)S(1)} %get-tuple-element.21), channel_id=1, source_target_pairs={{0,2},{1,3},{2,0},{3,1},{4,6},{5,7},{6,4},{7,5},{8,10},{9,11},{10,... | collective-permute-start | bytes 196616 | tf_op jit(solution)/shard_map/ppermute | solution.py:17
  42.1 4.5 %collective-permute-start.18 = (bf16[1,64,512]{2,1,0:T(8,128)(2,1)S(1)}, bf16[1,64,512]{2,1,0:T(8,128)(2,1)S(1)}, u32[]{:S(2)}, u32[]{:S(2)}) collective-permute-start(bf16[1,64,512]{2,1,0:T(8,128)(2,1)S(1)} %get-tuple-element.22), channel_id=1, source_target_pairs={{0,1},{1,0},{2,3},{3,2},{4,5},{5,4},{6,7},{7,6},{8,9},{9,8},{10,11... | collective-permute-start | bytes 196616 | tf_op jit(solution)/shard_map/ppermute | solution.py:17

commit v4 on v3

--- a/solution.py
+++ b/solution.py
@@ -21,45 +21,49 @@
     return jnp.bitwise_xor(lax.axis_index("fsdp"), 2 * k + e)
 
 
-def pick_kernel(other, grads, out, sem):
+def pick_kernel(groups, grads, *refs):
+    outs, sem = refs[:-1], refs[-1]
     slabs = grads.shape[1]
-    block = out.shape[-1]
+    block = outs[0].shape[-1]
     per_rep = lax.axis_size("fsdp") // slabs
-    rep = jnp.bitwise_xor(lax.axis_index("rep"), 1 if other else 0)
     copies = []
-    for k in range(out.shape[0]):
-        for j in range(out.shape[1]):
-            for e in range(2):
-                to = peer(k, e)
-                column = jnp.bitwise_xor(rep, 2 * j) * per_rep + to // slabs
-                start = pl.multiple_of(column * block, block)
-                copies.append(
-                    pltpu.make_async_copy(
-                        grads.at[0, lax.rem(to, slabs), :, pl.ds(start, block)],
-                        out.at[k, j, e],
-                        sem,
+    for n, out in enumerate(outs):
+        rep = jnp.bitwise_xor(lax.axis_index("rep"), 1 if n < len(groups) else 0)
+        for i, k in enumerate(groups[n % len(groups)]):
+            for j in range(out.shape[1]):
+                for e in range(2):
+                    to = peer(k, e)
+                    column = jnp.bitwise_xor(rep, 2 * j) * per_rep + to // slabs
+                    start = pl.multiple_of(column * block, block)
+                    copies.append(
+                        pltpu.make_async_copy(
+                            grads.at[0, lax.rem(to, slabs), :, pl.ds(start, block)],
+                            out.at[i, j, e],
+                            sem,
+                        )
                     )
-                )
     for copy in copies:
         copy.start()
     for copy in copies:
         copy.wait()
 
 
-def pick(grads, other):
+def pick(grads, groups):
     rows = grads.shape[2]
-    fsdp_count = lax.axis_size("fsdp")
-    shape = (fsdp_count // 2, lax.axis_size("rep") // 2, 2, rows, rows * fsdp_count)
-    return pl.pallas_call(
-        functools.partial(pick_kernel, other),
-        out_shape=jax.ShapeDtypeStruct(shape, grads.dtype),
+    block = rows * lax.axis_size("fsdp")
+    reps = lax.axis_size("rep") // 2
+    shapes = [jax.ShapeDtypeStruct((len(g), reps, 2, rows, block), grads.dtype) for g in groups]
+    outs = pl.pallas_call(
+        functools.partial(pick_kernel, groups),
+        out_shape=shapes * 2,
         in_specs=[ANY],
-        out_specs=ANY,
+        out_specs=[ANY] * (2 * len(groups)),
         scratch_shapes=[pltpu.SemaphoreType.DMA],
         compiler_params=pltpu.CompilerParams(vmem_limit_bytes=4 * MIB),
-        cost_estimate=pl.CostEstimate(flops=0, bytes_accessed=2 * MIB, transcendentals=0),
-        name="pick_other" if other else "pick_own",
+        cost_estimate=pl.CostEstimate(flops=0, bytes_accessed=4 * MIB, transcendentals=0),
+        name="pick",
     )(pltpu.with_memory_space_constraint(grads, pltpu.HBM))
+    return outs[: len(groups)], outs[len(groups) :]
 
 
 def place(k, e, rows):
@@ -69,40 +73,24 @@
 def main_kernel(spots, *refs):
     ins, refs = refs[: len(spots)], refs[len(spots) :]
     left_root, right_root, accum = refs[:3]
-    outs, refs = refs[3 : 3 + len(spots)], refs[3 + len(spots) :]
-    block_out, lroot, rroot, acc, sems = refs
+    outs, (block_out, scaled) = refs[3:-2], refs[-2:]
     rows = ins[0].shape[-2]
 
-    lcopy = pltpu.make_async_copy(left_root.at[0], lroot, sems.at[1])
-    rcopy = pltpu.make_async_copy(right_root.at[0], rroot, sems.at[2])
-    acopy = pltpu.make_async_copy(accum.at[0], acc, sems.at[3])
-    copies = [
-        pltpu.make_async_copy(ref.at[i], block_out.at[place(k, e, rows)], sems.at[0])
-        for ref, spot in zip(ins, spots)
-        for i, (k, e) in enumerate(spot)
-    ]
-    lcopy.start()
-    for copy in copies:
-        copy.start()
-    rcopy.start()
-    acopy.start()
-    lcopy.wait()
-    for copy in copies:
-        copy.wait()
+    for ref, spot in zip(ins, spots):
+        for i, (k, e) in enumerate(spot):
+            block_out[place(k, e, rows)] = ref[i]
     b = block_out[...]
-    half = jnp.dot(lroot[...], b, preferred_element_type=jnp.float32).astype(jnp.bfloat16)
-    rcopy.wait()
-    precond = jnp.dot(half, rroot[...], preferred_element_type=jnp.float32)
-    acopy.wait()
+    half = jnp.dot(left_root[0], b, preferred_element_type=jnp.float32).astype(jnp.bfloat16)
+    precond = jnp.dot(half, right_root[0], preferred_element_type=jnp.float32)
     wide = b.astype(jnp.float32)
     square = wide * wide
-    ada_sq = jnp.sum(square / (acc[...] + square))
+    ada_sq = jnp.sum(square / (accum[0] + square))
     pre_sq = jnp.sum(precond * precond)
     ratio = jnp.sqrt(ada_sq) / jnp.sqrt(pre_sq + 1e-06)
-    lroot[...] = (ratio * precond).astype(jnp.bfloat16)
+    scaled[...] = (ratio * precond).astype(jnp.bfloat16)
     for ref, spot in zip(outs, spots):
         for i, (k, e) in enumerate(spot):
-            ref[i] = lroot[place(k, e, rows)]
+            ref[i] = scaled[place(k, e, rows)]
 
 
 def precondition(pieces, spots, left_root, right_root, accum):
@@ -114,14 +102,9 @@
             jax.ShapeDtypeStruct((len(s), rows, side), jnp.bfloat16) for s in spots
         ]
         + [jax.ShapeDtypeStruct((side, side), jnp.bfloat16)],
-        in_specs=[ANY] * (len(spots) + 3),
+        in_specs=[VMEM] * (len(spots) + 3),
         out_specs=[VMEM] * (len(spots) + 1),
-        scratch_shapes=[
-            pltpu.VMEM((side, side), jnp.bfloat16),
-            pltpu.VMEM((side, side), jnp.bfloat16),
-            pltpu.VMEM((side, side), jnp.float32),
-            pltpu.SemaphoreType.DMA((4,)),
-        ],
+        scratch_shapes=[pltpu.VMEM((side, side), jnp.bfloat16)],
         compiler_params=pltpu.CompilerParams(vmem_limit_bytes=16 * MIB),
         cost_estimate=pl.CostEstimate(
             flops=4 * side**3, bytes_accessed=12 * side * side, transcendentals=0
@@ -212,18 +195,19 @@
     peers = fsdp_count // 2
     slabs, rows, width = grads.shape[1:]
 
-    theirs = swap(pick(grads, True), "rep", 1)
-    ours = pick(grads, False)
+    groups = [[0, 1]] + [[k] for k in range(2, peers)]
+    away, mine = pick(grads, groups)
     summed = {}
-    for k in range(peers):
-        terms, bit = [theirs[k], ours[k]], 1
+    for group, theirs, ours in zip(groups, away, mine):
+        terms, bit = [swap(theirs, "rep", 1), ours], 1
         while 2 * bit < rep_count:
             bit *= 2
-            pairs = [t.reshape((t.shape[0] // 2, 2) + t.shape[1:]) for t in terms]
-            part = swap(total([p[:, 1] for p in pairs]), "rep", bit)
-            kept = lax.optimization_barrier(wide([p[:, 0] for p in pairs]))
+            pairs = [t.reshape((t.shape[0], t.shape[1] // 2, 2) + t.shape[2:]) for t in terms]
+            part = swap(total([p[:, :, 1] for p in pairs]), "rep", bit)
+            kept = lax.optimization_barrier(wide([p[:, :, 0] for p in pairs]))
             terms = [kept, part]
-        summed[k] = [t[0] for t in terms]
+        for i, k in enumerate(group):
+            summed[k] = [t[i, 0] for t in terms]
 
     def summed_piece(k, e):
         return total([t[e : e + 1] for t in summed[k]])

time: 47.7 us -> 45.3 us (0.950)
  Pallas kernels: 7.9 us -> 5.85 us
  starting transfers between devices: 30 us -> 29.3 us
    pallas_call x1, Pallas kernels: 2.45 us -> 1.31 us  [precondition(): pl.pallas_call(functools.partial(main_kernel, spots), out_shape=[jax.Shap...]
    pallas_call x2 -> x1, Pallas kernels: 2.52 us -> 1.61 us  [pick(): pl.pallas_call(functools.partial(pick_kernel, groups), out_shape=shapes *...]
    ppermute x19 -> x20, starting transfers between devices: 30 us -> 29.3 us  [swap(): return lax.ppermute(x, axis, [(i, i ^ bit) for i in range(n)])]
    ppermute x19 -> x20, waiting for transfers between devices: 8.32 us -> 8.79 us  [swap(): return lax.ppermute(x, axis, [(i, i ^ bit) for i in range(n)])]
  transfers between devices with their start and end apart: 19 -> 20, of which waited for: 9 -> 9; matrix products, arithmetic and copies ran while one was open for 0% -> 1% of each run, Pallas kernels for 7% -> 5%
where the time goes in v4:
time: 45.3 us; the launch traced here: 45.1 us
  starting transfers between devices  29.3 us (65%)
  waiting for transfers between devices  8.79 us (19%)
  Pallas kernels  5.85 us (13%)
  between operations  0.74 us (2%)
    ppermute x20, starting transfers between devices, swap(): return lax.ppermute(x, axis, [(i, i ^ bit) for i in range(n)])  29.3 us
    ppermute x20, waiting for transfers between devices, swap(): return lax.ppermute(x, axis, [(i, i ^ bit) for i in range(n)])  8.79 us
    pallas_call x1, Pallas kernels, statistics(): pl.pallas_call(stats_kernel, out_shape=(shape,) * 3, in_specs=[VMEM] * 4,...  2.15 us
    pallas_call x1, Pallas kernels, pick(): pl.pallas_call(functools.partial(pick_kernel, groups), out_shape=shapes *...  1.61 us
    pallas_call x1, Pallas kernels, precondition(): pl.pallas_call(functools.partial(main_kernel, spots), out_shape=[jax.Shap...  1.31 us
  transfers between devices with their start and end apart: 20, of which 9 were waited for; matrix products, arithmetic and copies ran while one was open for 1% of the time, Pallas kernels for 5%

profile of v4, /device:TPU:0, one launch (start us, length us, event | category | flops | bytes accessed | tf_op | source)
XLA Modules:
  0.0 45.1 jit_solution(13605120019797318367)
XLA Ops:
  0.6 1.6 %pick.1 = (bf16[2,2,2,64,512]{4,3,2,1,0:T(8,128)(2,1)S(1)}, bf16[1,2,2,64,512]{4,3,2,1,0:T(8,128)(2,1)S(1)}, bf16[1,2,2,64,512]{4,3,2,1,0:T(8,128)(2,1)S(1)}, bf...) custom-call(bf16[1,2,64,8192]{3,2,1,0:T(8,128)(2,1)} %grads.1), custom_call_target="tpu_custom_call" | custom-call | bytes 4194304 | tf_op jit(solution)/shard_map/pick/pallas_call | solution.py:56
  2.3 0.5 %collective-permute-start.5 = (bf16[1,2,2,64,512]{4,3,2,1,0:T(8,128)(2,1)S(1)}, bf16[1,2,2,64,512]{4,3,2,1,0:T(8,128)(2,1)S(1)}, u32[]{:S(2)}, u32[]{:S(2)}) collective-permute-start(bf16[1,2,2,64,512]{4,3,2,1,0:T(8,128)(2,1)S(1)} %get-tuple-element.24), channel_id=1, source_target_pairs={{0,8},{8,0},{16,24},{24,16},{1,9},{9,1},{17,25},{25,17},{2,10},{10... | collective-permute-start | bytes 786440 | tf_op jit(solution)/shard_map/ppermute | solution.py:17
  2.8 0.1 collective-permute-start
  2.9 0.5 %collective-permute-start.9 = (bf16[1,2,2,64,512]{4,3,2,1,0:T(8,128)(2,1)S(1)}, bf16[1,2,2,64,512]{4,3,2,1,0:T(8,128)(2,1)S(1)}, u32[]{:S(2)}, u32[]{:S(2)}) collective-permute-start(bf16[1,2,2,64,512]{4,3,2,1,0:T(8,128)(2,1)S(1)} %get-tuple-element.26), channel_id=1, source_target_pairs={{0,8},{8,0},{16,24},{24,16},{1,9},{9,1},{17,25},{25,17},{2,10},{10... | collective-permute-start | bytes 786440 | tf_op jit(solution)/shard_map/ppermute | solution.py:17
  3.4 0.5 %collective-permute-done.5 = bf16[1,2,2,64,512]{4,3,2,1,0:T(8,128)(2,1)S(1)} collective-permute-done((bf16[1,2,2,64,512]{4,3,2,1,0:T(8,128)(2,1)S(1)}, bf16[1,2,2,64,512]{4,3,2,1,0:T(8,128)(2,1)S(1)}, u32[]{:S(2)}, u32[]{:S(2)}) %collective-permute-start.5) | collective-permute-done | bytes 262176 | tf_op jit(solution)/shard_map/ppermute | solution.py:17
  3.9 0.1 fusion.1
  4.0 3.0 %collective-permute-start.6 = (bf16[1,1,2,64,512]{4,3,2,1,0:T(8,128)(2,1)S(1)}, bf16[1,1,2,64,512]{4,3,2,1,0:T(8,128)(2,1)S(1)}, u32[]{:S(2)}, u32[]{:S(2)}) collective-permute-start(bf16[1,1,2,64,512]{4,3,2,1,0:T(8,128)(2,1)S(1)} %get-tuple-element.48), channel_id=1, source_target_pairs={{0,16},{8,24},{16,0},{24,8},{1,17},{9,25},{17,1},{25,9},{2,18},{10... | collective-permute-start | bytes 393224 | tf_op jit(solution)/shard_map/ppermute | solution.py:17
  7.0 0.1 fusion.2
  7.0 0.0 copy-start
  7.0 0.0 copy-start.3
  7.0 0.0 copy-start.4
  7.1 1.1 %collective-permute-start.10 = (bf16[1,1,2,64,512]{4,3,2,1,0:T(8,128)(2,1)S(1)}, bf16[1,1,2,64,512]{4,3,2,1,0:T(8,128)(2,1)S(1)}, u32[]{:S(2)}, u32[]{:S(2)}) collective-permute-start(bf16[1,1,2,64,512]{4,3,2,1,0:T(8,128)(2,1)S(1)} %get-tuple-element.46), channel_id=1, source_target_pairs={{0,16},{8,24},{16,0},{24,8},{1,17},{9,25},{17,1},{25,9},{2,18},{10... | collective-permute-start | bytes 393224 | tf_op jit(solution)/shard_map/ppermute | solution.py:17
  8.1 0.1 fusion
  8.3 1.1 %collective-permute-start.1 = (bf16[2,1,2,64,512]{4,3,2,1,0:T(8,128)(2,1)S(1)}, bf16[2,1,2,64,512]{4,3,2,1,0:T(8,128)(2,1)S(1)}, u32[]{:S(2)}, u32[]{:S(2)}) collective-permute-start(bf16[2,1,2,64,512]{4,3,2,1,0:T(8,128)(2,1)S(1)} %get-tuple-element.40), channel_id=1, source_target_pairs={{0,16},{8,24},{16,0},{24,8},{1,17},{9,25},{17,1},{25,9},{2,18},{10... | collective-permute-start | bytes 786440 | tf_op jit(solution)/shard_map/ppermute | solution.py:17
  9.4 1.9 %collective-permute-done.6 = bf16[1,1,2,64,512]{4,3,2,1,0:T(8,128)(2,1)S(1)} collective-permute-done((bf16[1,1,2,64,512]{4,3,2,1,0:T(8,128)(2,1)S(1)}, bf16[1,1,2,64,512]{4,3,2,1,0:T(8,128)(2,1)S(1)}, u32[]{:S(2)}, u32[]{:S(2)}) %collective-permute-start.6) | collective-permute-done | bytes 131104 | tf_op jit(solution)/shard_map/ppermute | solution.py:17
  11.3 3.2 %collective-permute-start.8 = (bf16[1,64,512]{2,1,0:T(8,128)(2,1)S(1)}, bf16[1,64,512]{2,1,0:T(8,128)(2,1)S(1)}, u32[]{:S(2)}, u32[]{:S(2)}) collective-permute-start(bf16[1,64,512]{2,1,0:T(8,128)(2,1)S(1)} %get-tuple-element.52), channel_id=1, source_target_pairs={{0,4},{1,5},{2,6},{3,7},{4,0},{5,1},{6,2},{7,3},{8,12},{9,13},{10,... | collective-permute-start | bytes 196616 | tf_op jit(solution)/shard_map/ppermute | solution.py:17
  14.5 1.3 %collective-permute-start.7 = (bf16[1,64,512]{2,1,0:T(8,128)(2,1)S(1)}, bf16[1,64,512]{2,1,0:T(8,128)(2,1)S(1)}, u32[]{:S(2)}, u32[]{:S(2)}) collective-permute-start(bf16[1,64,512]{2,1,0:T(8,128)(2,1)S(1)} %get-tuple-element.53), channel_id=1, source_target_pairs={{0,5},{1,4},{2,7},{3,6},{4,1},{5,0},{6,3},{7,2},{8,13},{9,12},{10,... | collective-permute-start | bytes 196616 | tf_op jit(solution)/shard_map/ppermute | solution.py:17
  15.7 0.0 collective-permute-done.10
  15.8 3.7 %collective-permute-start.12 = (bf16[1,64,512]{2,1,0:T(8,128)(2,1)S(1)}, bf16[1,64,512]{2,1,0:T(8,128)(2,1)S(1)}, u32[]{:S(2)}, u32[]{:S(2)}) collective-permute-start(bf16[1,64,512]{2,1,0:T(8,128)(2,1)S(1)} %get-tuple-element.50), channel_id=1, source_target_pairs={{0,6},{1,7},{2,4},{3,5},{4,2},{5,3},{6,0},{7,1},{8,14},{9,15},{10,... | collective-permute-start | bytes 196616 | tf_op jit(solution)/shard_map/ppermute | solution.py:17
  19.4 0.1 collective-permute-start.11
  19.5 0.0 collective-permute-done.1
  19.5 0.1 fusion.14
  19.6 1.6 %collective-permute-start.4 = (bf16[1,64,512]{2,1,0:T(8,128)(2,1)S(1)}, bf16[1,64,512]{2,1,0:T(8,128)(2,1)S(1)}, u32[]{:S(2)}, u32[]{:S(2)}) collective-permute-start(bf16[1,64,512]{2,1,0:T(8,128)(2,1)S(1)} %get-tuple-element.42), channel_id=1, source_target_pairs={{0,2},{1,3},{2,0},{3,1},{4,6},{5,7},{6,4},{7,5},{8,10},{9,11},{10,... | collective-permute-start | bytes 196616 | tf_op jit(solution)/shard_map/ppermute | solution.py:17
  21.1 0.0 collective-permute-done.8.refs_5_
  21.1 1.6 %collective-permute-start.3 = (bf16[1,64,512]{2,1,0:T(8,128)(2,1)S(1)}, bf16[1,64,512]{2,1,0:T(8,128)(2,1)S(1)}, u32[]{:S(2)}, u32[]{:S(2)}) collective-permute-start(bf16[1,64,512]{2,1,0:T(8,128)(2,1)S(1)} %get-tuple-element.43), channel_id=1, source_target_pairs={{0,3},{1,2},{2,1},{3,0},{4,7},{5,6},{6,5},{7,4},{8,11},{9,10},{10,... | collective-permute-start | bytes 196616 | tf_op jit(solution)/shard_map/ppermute | solution.py:17
  22.7 1.6 %collective-permute-done.7.refs_4_ = bf16[1,64,512]{2,1,0:T(8,128)(2,1)S(1)} collective-permute-done((bf16[1,64,512]{2,1,0:T(8,128)(2,1)S(1)}, bf16[1,64,512]{2,1,0:T(8,128)(2,1)S(1)}, u32[]{:S(2)}, u32[]{:S(2)}) %collective-permute-start.7) | collective-permute-done | bytes 65568 | tf_op jit(solution)/shard_map/ppermute | solution.py:17
  24.3 0.6 %collective-permute-start.2 = (bf16[1,64,512]{2,1,0:T(8,128)(2,1)S(1)}, bf16[1,64,512]{2,1,0:T(8,128)(2,1)S(1)}, u32[]{:S(2)}, u32[]{:S(2)}) collective-permute-start(bf16[1,64,512]{2,1,0:T(8,128)(2,1)S(1)} %get-tuple-element.45), channel_id=1, source_target_pairs={{0,1},{1,0},{2,3},{3,2},{4,5},{5,4},{6,7},{7,6},{8,9},{9,8},{10,11... | collective-permute-start | bytes 196616 | tf_op jit(solution)/shard_map/ppermute | solution.py:17
  24.9 0.0 collective-permute-done.12.refs_7_
  24.9 2.2 %collective-permute-done.11.refs_6_ = bf16[1,64,512]{2,1,0:T(8,128)(2,1)S(1)} collective-permute-done((bf16[1,64,512]{2,1,0:T(8,128)(2,1)S(1)}, bf16[1,64,512]{2,1,0:T(8,128)(2,1)S(1)}, u32[]{:S(2)}, u32[]{:S(2)}) %collective-permute-start.11) | collective-permute-done | bytes 65568 | tf_op jit(solution)/shard_map/ppermute | solution.py:17
  27.2 0.0 collective-permute-done.4.refs_3_
  27.2 0.0 collective-permute-done.3.refs_2_
  27.2 1.4 %collective-permute-done.2.refs_0_ = bf16[1,64,512]{2,1,0:T(8,128)(2,1)S(1)} collective-permute-done((bf16[1,64,512]{2,1,0:T(8,128)(2,1)S(1)}, bf16[1,64,512]{2,1,0:T(8,128)(2,1)S(1)}, u32[]{:S(2)}, u32[]{:S(2)}) %collective-permute-start.2) | collective-permute-done | bytes 65568 | tf_op jit(solution)/shard_map/ppermute | solution.py:17
  28.6 1.3 %precondition.1 = (bf16[1,64,512]{2,1,0:T(8,128)(2,1)S(1)}, bf16[1,64,512]{2,1,0:T(8,128)(2,1)S(1)}, bf16[1,64,512]{2,1,0:T(8,128)(2,1)S(1)}, bf16[1,64,512]{2,1...) custom-call(bf16[1,64,512]{2,1,0:T(8,128)(2,1)S(1)} %collective-perm, ...), custom_call_target="tpu_custom_call" | custom-call | flops 536870912 | bytes 3145728 | tf_op jit(solution)/shard_map/precondition/pallas_call | solution.py:99
  29.9 3.2 %collective-permute-start.13 = (bf16[1,64,512]{2,1,0:T(8,128)(2,1)S(1)}, bf16[1,64,512]{2,1,0:T(8,128)(2,1)S(1)}, u32[]{:S(2)}, u32[]{:S(2)}) collective-permute-start(bf16[1,64,512]{2,1,0:T(8,128)(2,1)S(1)} %get-tuple-element.28), channel_id=1, source_target_pairs={{0,7},{1,6},{2,5},{3,4},{4,3},{5,2},{6,1},{7,0},{8,15},{9,14},{10,... | collective-permute-start | bytes 196616 | tf_op jit(solution)/shard_map/ppermute | solution.py:17
  33.1 0.8 %collective-permute-start.14 = (bf16[1,64,512]{2,1,0:T(8,128)(2,1)S(1)}, bf16[1,64,512]{2,1,0:T(8,128)(2,1)S(1)}, u32[]{:S(2)}, u32[]{:S(2)}) collective-permute-start(bf16[1,64,512]{2,1,0:T(8,128)(2,1)S(1)} %get-tuple-element.29), channel_id=1, source_target_pairs={{0,6},{1,7},{2,4},{3,5},{4,2},{5,3},{6,0},{7,1},{8,14},{9,15},{10,... | collective-permute-start | bytes 196616 | tf_op jit(solution)/shard_map/ppermute | solution.py:17
  33.8 1.1 %collective-permute-start.15 = (bf16[1,64,512]{2,1,0:T(8,128)(2,1)S(1)}, bf16[1,64,512]{2,1,0:T(8,128)(2,1)S(1)}, u32[]{:S(2)}, u32[]{:S(2)}) collective-permute-start(bf16[1,64,512]{2,1,0:T(8,128)(2,1)S(1)} %get-tuple-element.30), channel_id=1, source_target_pairs={{0,5},{1,4},{2,7},{3,6},{4,1},{5,0},{6,3},{7,2},{8,13},{9,12},{10,... | collective-permute-start | bytes 196616 | tf_op jit(solution)/shard_map/ppermute | solution.py:17
  35.0 2.6 %collective-permute-start.16 = (bf16[1,64,512]{2,1,0:T(8,128)(2,1)S(1)}, bf16[1,64,512]{2,1,0:T(8,128)(2,1)S(1)}, u32[]{:S(2)}, u32[]{:S(2)}) collective-permute-start(bf16[1,64,512]{2,1,0:T(8,128)(2,1)S(1)} %get-tuple-element.31), channel_id=1, source_target_pairs={{0,4},{1,5},{2,6},{3,7},{4,0},{5,1},{6,2},{7,3},{8,12},{9,13},{10,... | collective-permute-start | bytes 196616 | tf_op jit(solution)/shard_map/ppermute | solution.py:17
  37.6 1.3 %collective-permute-start.17 = (bf16[1,64,512]{2,1,0:T(8,128)(2,1)S(1)}, bf16[1,64,512]{2,1,0:T(8,128)(2,1)S(1)}, u32[]{:S(2)}, u32[]{:S(2)}) collective-permute-start(bf16[1,64,512]{2,1,0:T(8,128)(2,1)S(1)} %get-tuple-element.32), channel_id=1, source_target_pairs={{0,3},{1,2},{2,1},{3,0},{4,7},{5,6},{6,5},{7,4},{8,11},{9,10},{10,... | collective-permute-start | bytes 196616 | tf_op jit(solution)/shard_map/ppermute | solution.py:17
  38.9 0.0 collective-permute-done.13.refs_0_
  38.9 0.8 %collective-permute-start.18 = (bf16[1,64,512]{2,1,0:T(8,128)(2,1)S(1)}, bf16[1,64,512]{2,1,0:T(8,128)(2,1)S(1)}, u32[]{:S(2)}, u32[]{:S(2)}) collective-permute-start(bf16[1,64,512]{2,1,0:T(8,128)(2,1)S(1)} %get-tuple-element.33), channel_id=1, source_target_pairs={{0,2},{1,3},{2,0},{3,1},{4,6},{5,7},{6,4},{7,5},{8,10},{9,11},{10,... | collective-permute-start | bytes 196616 | tf_op jit(solution)/shard_map/ppermute | solution.py:17
  39.7 0.3 collective-permute-done.14.refs_1_
  40.0 1.3 %collective-permute-start.19 = (bf16[1,64,512]{2,1,0:T(8,128)(2,1)S(1)}, bf16[1,64,512]{2,1,0:T(8,128)(2,1)S(1)}, u32[]{:S(2)}, u32[]{:S(2)}) collective-permute-start(bf16[1,64,512]{2,1,0:T(8,128)(2,1)S(1)} %get-tuple-element.34), channel_id=1, source_target_pairs={{0,1},{1,0},{2,3},{3,2},{4,5},{5,4},{6,7},{7,6},{8,9},{9,8},{10,11... | collective-permute-start | bytes 196616 | tf_op jit(solution)/shard_map/ppermute | solution.py:17
  41.2 2.1 %statistics.1 = (f32[1,512,512]{2,1,0:T(8,128)}, f32[1,512,512]{2,1,0:T(8,128)}, f32[1,512,512]{2,1,0:T(8,128)}) custom-call(bf16[512,512]{1,0:T(8,128)(2,1)S(1)} %get-tuple-element.36.block, f32[1,512,512]{2,1,0:T(8,128)S(1)} %copy-done.1, f32[1,512,512]{2,1,0:T(8,128)S(1)} %copy-done.2, f32[1,512,512]{2,1,0:T(8,128)S(1)} %copy-done), custom_call_target="tpu_custom_call" | custom-call | flops 536870912 | bytes 6815744 | tf_op jit(solution)/shard_map/statistics/pallas_call | solution.py:132
  43.4 0.4 collective-permute-done.15.refs_2_
  43.8 0.0 collective-permute-done.16.refs_3_
  43.8 0.3 collective-permute-done.18.refs_5_
  44.1 0.2 collective-permute-done.19.refs_6_
  44.3 0.8 %assemble.1 = bf16[2,64,2048]{2,1,0:T(8,128)(2,1)} custom-call(bf16[1,64,512]{2,1,0:T(8,128)(2,1)S(1)} %collective-permute-done.13.refs_0_, bf16[1,64,512]{2,1,0:T(8,128)(2,1)S(1)} %collective-permute-done.14.refs_1_, bf16[1,64,512]{2,1,0:T(8,128)(2,1)S(1)} %collective-permute-done.15.refs_2_, bf16[1,64,512]{2,1,0:T(8,128)(2,1)S(1)} %collective-permute-done.16.refs_3_, ...), custom_call_target="tpu_custom_call" | custom-call | bytes 1048576 | tf_op jit(solution)/shard_map/assemble/pallas_call | solution.py:166
  (14 shorter events, 0.1 us)
Async XLA Ops:
  2.3 1.7 %collective-permute-start.5 = (bf16[1,2,2,64,512]{4,3,2,1,0:T(8,128)(2,1)S(1)}, bf16[1,2,2,64,512]{4,3,2,1,0:T(8,128)(2,1)S(1)}, u32[]{:S(2)}, u32[]{:S(2)}) collective-permute-start(bf16[1,2,2,64,512]{4,3,2,1,0:T(8,128)(2,1)S(1)} %get-tuple-element.24), channel_id=1, source_target_pairs={{0,8},{8,0},{16,24},{24,16},{1,9},{9,1},{17,25},{25,17},{2,10},{10... | collective-permute-start | bytes 786440 | tf_op jit(solution)/shard_map/ppermute | solution.py:17
  2.8 5.3 %collective-permute-start = (bf16[2,2,2,64,512]{4,3,2,0,1:T(8,128)(2,1)S(1)}, bf16[2,2,2,64,512]{4,3,2,0,1:T(8,128)(2,1)S(1)}, u32[]{:S(2)}, u32[]{:S(2)}) collective-permute-start(bf16[2,2,2,64,512]{4,3,2,0,1:T(8,128)(2,1)S(1)} %copy.10), channel_id=1, source_target_pairs={{0,8},{8,0},{16,24},{24,16},{1,9},{9,1},{17,25},{25,17},{2,10},{10... | collective-permute-start | bytes 1572872 | tf_op jit(solution)/shard_map/ppermute | solution.py:17
  2.9 4.0 %collective-permute-start.9 = (bf16[1,2,2,64,512]{4,3,2,1,0:T(8,128)(2,1)S(1)}, bf16[1,2,2,64,512]{4,3,2,1,0:T(8,128)(2,1)S(1)}, u32[]{:S(2)}, u32[]{:S(2)}) collective-permute-start(bf16[1,2,2,64,512]{4,3,2,1,0:T(8,128)(2,1)S(1)} %get-tuple-element.26), channel_id=1, source_target_pairs={{0,8},{8,0},{16,24},{24,16},{1,9},{9,1},{17,25},{25,17},{2,10},{10... | collective-permute-start | bytes 786440 | tf_op jit(solution)/shard_map/ppermute | solution.py:17
  4.0 7.2 %collective-permute-start.6 = (bf16[1,1,2,64,512]{4,3,2,1,0:T(8,128)(2,1)S(1)}, bf16[1,1,2,64,512]{4,3,2,1,0:T(8,128)(2,1)S(1)}, u32[]{:S(2)}, u32[]{:S(2)}) collective-permute-start(bf16[1,1,2,64,512]{4,3,2,1,0:T(8,128)(2,1)S(1)} %get-tuple-element.48), channel_id=1, source_target_pairs={{0,16},{8,24},{16,0},{24,8},{1,17},{9,25},{17,1},{25,9},{2,18},{10... | collective-permute-start | bytes 393224 | tf_op jit(solution)/shard_map/ppermute | solution.py:17
  7.0 21.5 %copy-start = (f32[1,512,512]{2,1,0:T(8,128)S(1)}, f32[1,512,512]{2,1,0:T(8,128)}, u32[]{:S(2)}) copy-start(f32[1,512,512]{2,1,0:T(8,128)} %accum.1) | copy-start | bytes 3145732
  7.0 21.5 %copy-start.3 = (bf16[1,512,512]{2,1,0:T(8,128)(2,1)S(1)}, bf16[1,512,512]{2,1,0:T(8,128)(2,1)}, u32[]{:S(2)}) copy-start(bf16[1,512,512]{2,1,0:T(8,128)(2,1)} %refs_8_.1) | copy-start | bytes 1572868
  7.0 21.5 %copy-start.4 = (bf16[1,512,512]{2,1,0:T(8,128)(2,1)S(1)}, bf16[1,512,512]{2,1,0:T(8,128)(2,1)}, u32[]{:S(2)}) copy-start(bf16[1,512,512]{2,1,0:T(8,128)(2,1)} %refs_9_.1) | copy-start | bytes 1572868
  7.1 8.7 %collective-permute-start.10 = (bf16[1,1,2,64,512]{4,3,2,1,0:T(8,128)(2,1)S(1)}, bf16[1,1,2,64,512]{4,3,2,1,0:T(8,128)(2,1)S(1)}, u32[]{:S(2)}, u32[]{:S(2)}) collective-permute-start(bf16[1,1,2,64,512]{4,3,2,1,0:T(8,128)(2,1)S(1)} %get-tuple-element.46), channel_id=1, source_target_pairs={{0,16},{8,24},{16,0},{24,8},{1,17},{9,25},{17,1},{25,9},{2,18},{10... | collective-permute-start | bytes 393224 | tf_op jit(solution)/shard_map/ppermute | solution.py:17
  8.3 11.2 %collective-permute-start.1 = (bf16[2,1,2,64,512]{4,3,2,1,0:T(8,128)(2,1)S(1)}, bf16[2,1,2,64,512]{4,3,2,1,0:T(8,128)(2,1)S(1)}, u32[]{:S(2)}, u32[]{:S(2)}) collective-permute-start(bf16[2,1,2,64,512]{4,3,2,1,0:T(8,128)(2,1)S(1)} %get-tuple-element.40), channel_id=1, source_target_pairs={{0,16},{8,24},{16,0},{24,8},{1,17},{9,25},{17,1},{25,9},{2,18},{10... | collective-permute-start | bytes 786440 | tf_op jit(solution)/shard_map/ppermute | solution.py:17
  11.3 9.9 %collective-permute-start.8 = (bf16[1,64,512]{2,1,0:T(8,128)(2,1)S(1)}, bf16[1,64,512]{2,1,0:T(8,128)(2,1)S(1)}, u32[]{:S(2)}, u32[]{:S(2)}) collective-permute-start(bf16[1,64,512]{2,1,0:T(8,128)(2,1)S(1)} %get-tuple-element.52), channel_id=1, source_target_pairs={{0,4},{1,5},{2,6},{3,7},{4,0},{5,1},{6,2},{7,3},{8,12},{9,13},{10,... | collective-permute-start | bytes 196616 | tf_op jit(solution)/shard_map/ppermute | solution.py:17
  14.5 26.8 %copy-start.1 = (f32[1,512,512]{2,1,0:T(8,128)S(1)}, f32[1,512,512]{2,1,0:T(8,128)}, u32[]{:S(2)}) copy-start(f32[1,512,512]{2,1,0:T(8,128)} %left.1) | copy-start | bytes 3145732
  14.5 26.8 %copy-start.2 = (f32[1,512,512]{2,1,0:T(8,128)S(1)}, f32[1,512,512]{2,1,0:T(8,128)}, u32[]{:S(2)}) copy-start(f32[1,512,512]{2,1,0:T(8,128)} %right.1) | copy-start | bytes 3145732
  14.5 9.8 %collective-permute-start.7 = (bf16[1,64,512]{2,1,0:T(8,128)(2,1)S(1)}, bf16[1,64,512]{2,1,0:T(8,128)(2,1)S(1)}, u32[]{:S(2)}, u32[]{:S(2)}) collective-permute-start(bf16[1,64,512]{2,1,0:T(8,128)(2,1)S(1)} %get-tuple-element.53), channel_id=1, source_target_pairs={{0,5},{1,4},{2,7},{3,6},{4,1},{5,0},{6,3},{7,2},{8,13},{9,12},{10,... | collective-permute-start | bytes 196616 | tf_op jit(solution)/shard_map/ppermute | solution.py:17
  15.8 9.2 %collective-permute-start.12 = (bf16[1,64,512]{2,1,0:T(8,128)(2,1)S(1)}, bf16[1,64,512]{2,1,0:T(8,128)(2,1)S(1)}, u32[]{:S(2)}, u32[]{:S(2)}) collective-permute-start(bf16[1,64,512]{2,1,0:T(8,128)(2,1)S(1)} %get-tuple-element.50), channel_id=1, source_target_pairs={{0,6},{1,7},{2,4},{3,5},{4,2},{5,3},{6,0},{7,1},{8,14},{9,15},{10,... | collective-permute-start | bytes 196616 | tf_op jit(solution)/shard_map/ppermute | solution.py:17
  19.4 7.7 %collective-permute-start.11 = (bf16[1,64,512]{2,1,0:T(8,128)(2,1)S(1)}, bf16[1,64,512]{2,1,0:T(8,128)(2,1)S(1)}, u32[]{:S(2)}, u32[]{:S(2)}) collective-permute-start(bf16[1,64,512]{2,1,0:T(8,128)(2,1)S(1)} %get-tuple-element.51), channel_id=1, source_target_pairs={{0,7},{1,6},{2,5},{3,4},{4,3},{5,2},{6,1},{7,0},{8,15},{9,14},{10,... | collective-permute-start | bytes 196616 | tf_op jit(solution)/shard_map/ppermute | solution.py:17
  19.6 7.6 %collective-permute-start.4 = (bf16[1,64,512]{2,1,0:T(8,128)(2,1)S(1)}, bf16[1,64,512]{2,1,0:T(8,128)(2,1)S(1)}, u32[]{:S(2)}, u32[]{:S(2)}) collective-permute-start(bf16[1,64,512]{2,1,0:T(8,128)(2,1)S(1)} %get-tuple-element.42), channel_id=1, source_target_pairs={{0,2},{1,3},{2,0},{3,1},{4,6},{5,7},{6,4},{7,5},{8,10},{9,11},{10,... | collective-permute-start | bytes 196616 | tf_op jit(solution)/shard_map/ppermute | solution.py:17
  21.1 6.1 %collective-permute-start.3 = (bf16[1,64,512]{2,1,0:T(8,128)(2,1)S(1)}, bf16[1,64,512]{2,1,0:T(8,128)(2,1)S(1)}, u32[]{:S(2)}, u32[]{:S(2)}) collective-permute-start(bf16[1,64,512]{2,1,0:T(8,128)(2,1)S(1)} %get-tuple-element.43), channel_id=1, source_target_pairs={{0,3},{1,2},{2,1},{3,0},{4,7},{5,6},{6,5},{7,4},{8,11},{9,10},{10,... | collective-permute-start | bytes 196616 | tf_op jit(solution)/shard_map/ppermute | solution.py:17
  24.3 4.3 %collective-permute-start.2 = (bf16[1,64,512]{2,1,0:T(8,128)(2,1)S(1)}, bf16[1,64,512]{2,1,0:T(8,128)(2,1)S(1)}, u32[]{:S(2)}, u32[]{:S(2)}) collective-permute-start(bf16[1,64,512]{2,1,0:T(8,128)(2,1)S(1)} %get-tuple-element.45), channel_id=1, source_target_pairs={{0,1},{1,0},{2,3},{3,2},{4,5},{5,4},{6,7},{7,6},{8,9},{9,8},{10,11... | collective-permute-start | bytes 196616 | tf_op jit(solution)/shard_map/ppermute | solution.py:17
  29.9 9.0 %collective-permute-start.13 = (bf16[1,64,512]{2,1,0:T(8,128)(2,1)S(1)}, bf16[1,64,512]{2,1,0:T(8,128)(2,1)S(1)}, u32[]{:S(2)}, u32[]{:S(2)}) collective-permute-start(bf16[1,64,512]{2,1,0:T(8,128)(2,1)S(1)} %get-tuple-element.28), channel_id=1, source_target_pairs={{0,7},{1,6},{2,5},{3,4},{4,3},{5,2},{6,1},{7,0},{8,15},{9,14},{10,... | collective-permute-start | bytes 196616 | tf_op jit(solution)/shard_map/ppermute | solution.py:17
  33.1 6.9 %collective-permute-start.14 = (bf16[1,64,512]{2,1,0:T(8,128)(2,1)S(1)}, bf16[1,64,512]{2,1,0:T(8,128)(2,1)S(1)}, u32[]{:S(2)}, u32[]{:S(2)}) collective-permute-start(bf16[1,64,512]{2,1,0:T(8,128)(2,1)S(1)} %get-tuple-element.29), channel_id=1, source_target_pairs={{0,6},{1,7},{2,4},{3,5},{4,2},{5,3},{6,0},{7,1},{8,14},{9,15},{10,... | collective-permute-start | bytes 196616 | tf_op jit(solution)/shard_map/ppermute | solution.py:17
  33.8 10.0 %collective-permute-start.15 = (bf16[1,64,512]{2,1,0:T(8,128)(2,1)S(1)}, bf16[1,64,512]{2,1,0:T(8,128)(2,1)S(1)}, u32[]{:S(2)}, u32[]{:S(2)}) collective-permute-start(bf16[1,64,512]{2,1,0:T(8,128)(2,1)S(1)} %get-tuple-element.30), channel_id=1, source_target_pairs={{0,5},{1,4},{2,7},{3,6},{4,1},{5,0},{6,3},{7,2},{8,13},{9,12},{10,... | collective-permute-start | bytes 196616 | tf_op jit(solution)/shard_map/ppermute | solution.py:17
  35.0 8.8 %collective-permute-start.16 = (bf16[1,64,512]{2,1,0:T(8,128)(2,1)S(1)}, bf16[1,64,512]{2,1,0:T(8,128)(2,1)S(1)}, u32[]{:S(2)}, u32[]{:S(2)}) collective-permute-start(bf16[1,64,512]{2,1,0:T(8,128)(2,1)S(1)} %get-tuple-element.31), channel_id=1, source_target_pairs={{0,4},{1,5},{2,6},{3,7},{4,0},{5,1},{6,2},{7,3},{8,12},{9,13},{10,... | collective-permute-start | bytes 196616 | tf_op jit(solution)/shard_map/ppermute | solution.py:17
  37.6 6.2 %collective-permute-start.17 = (bf16[1,64,512]{2,1,0:T(8,128)(2,1)S(1)}, bf16[1,64,512]{2,1,0:T(8,128)(2,1)S(1)}, u32[]{:S(2)}, u32[]{:S(2)}) collective-permute-start(bf16[1,64,512]{2,1,0:T(8,128)(2,1)S(1)} %get-tuple-element.32), channel_id=1, source_target_pairs={{0,3},{1,2},{2,1},{3,0},{4,7},{5,6},{6,5},{7,4},{8,11},{9,10},{10,... | collective-permute-start | bytes 196616 | tf_op jit(solution)/shard_map/ppermute | solution.py:17
  38.9 5.2 %collective-permute-start.18 = (bf16[1,64,512]{2,1,0:T(8,128)(2,1)S(1)}, bf16[1,64,512]{2,1,0:T(8,128)(2,1)S(1)}, u32[]{:S(2)}, u32[]{:S(2)}) collective-permute-start(bf16[1,64,512]{2,1,0:T(8,128)(2,1)S(1)} %get-tuple-element.33), channel_id=1, source_target_pairs={{0,2},{1,3},{2,0},{3,1},{4,6},{5,7},{6,4},{7,5},{8,10},{9,11},{10,... | collective-permute-start | bytes 196616 | tf_op jit(solution)/shard_map/ppermute | solution.py:17
  40.0 4.4 %collective-permute-start.19 = (bf16[1,64,512]{2,1,0:T(8,128)(2,1)S(1)}, bf16[1,64,512]{2,1,0:T(8,128)(2,1)S(1)}, u32[]{:S(2)}, u32[]{:S(2)}) collective-permute-start(bf16[1,64,512]{2,1,0:T(8,128)(2,1)S(1)} %get-tuple-element.34), channel_id=1, source_target_pairs={{0,1},{1,0},{2,3},{3,2},{4,5},{5,4},{6,7},{7,6},{8,9},{9,8},{10,11... | collective-permute-start | bytes 196616 | tf_op jit(solution)/shard_map/ppermute | solution.py:17

commit v5 on v4

--- a/solution.py
+++ b/solution.py
@@ -176,8 +176,8 @@
 
 
 def exchange(get, peers, far_last):
-    ks = range(peers) if far_last else range(peers - 1, -1, -1)
-    spots = [(k, e) for k in ks for e in (1, 0)]
+    ks = [0, 1, *range(peers - 1, 1, -1)] if far_last else range(peers - 1, -1, -1)
+    spots = [(k, e) for k in ks for e in ((0, 1) if far_last else (1, 0))]
     pieces = [swap(get(k, e), "fsdp", 2 * k + e) if k + e else get(k, e) for k, e in spots]
     return pieces, tuple((spot,) for spot in spots)
 
@@ -195,22 +195,25 @@
     peers = fsdp_count // 2
     slabs, rows, width = grads.shape[1:]
 
-    groups = [[0, 1]] + [[k] for k in range(2, peers)]
+    groups = [[0, 1]] + [[k] for k in range(peers - 1, 1, -1)]
     away, mine = pick(grads, groups)
     summed = {}
     for group, theirs, ours in zip(groups, away, mine):
-        terms, bit = [swap(theirs, "rep", 1), ours], 1
-        while 2 * bit < rep_count:
-            bit *= 2
-            pairs = [t.reshape((t.shape[0], t.shape[1] // 2, 2) + t.shape[2:]) for t in terms]
-            part = swap(total([p[:, :, 1] for p in pairs]), "rep", bit)
-            kept = lax.optimization_barrier(wide([p[:, :, 0] for p in pairs]))
-            terms = [kept, part]
-        for i, k in enumerate(group):
-            summed[k] = [t[i, 0] for t in terms]
+        theirs = swap(theirs, "rep", 1)
+        for es in [[0], [1]] if group[-1] == 2 else [[0, 1]]:
+            terms, bit = [a[:, :, es[0] : es[-1] + 1] for a in (theirs, ours)], 1
+            while 2 * bit < rep_count:
+                bit *= 2
+                pairs = [t.reshape((t.shape[0], t.shape[1] // 2, 2) + t.shape[2:]) for t in terms]
+                part = swap(total([p[:, :, 1] for p in pairs]), "rep", bit)
+                kept = lax.optimization_barrier(wide([p[:, :, 0] for p in pairs]))
+                terms = [kept, part]
+            for i, k in enumerate(group):
+                for j, e in enumerate(es):
+                    summed[k, e] = [t[i, 0, j : j + 1] for t in terms]
 
     def summed_piece(k, e):
-        return total([t[e : e + 1] for t in summed[k]])
+        return total(summed[k, e])
 
     pieces, spots = exchange(summed_piece, peers, True)
 

time: 45.3 us -> 44.6 us (0.985)
  waiting for transfers between devices: 8.79 us -> 5.68 us
  starting transfers between devices: 29.3 us -> 31.5 us
    ppermute x20 -> x21, waiting for transfers between devices: 8.79 us -> 5.68 us  [swap(): return lax.ppermute(x, axis, [(i, i ^ bit) for i in range(n)])]
    ppermute x20 -> x21, starting transfers between devices: 29.3 us -> 31.5 us  [swap(): return lax.ppermute(x, axis, [(i, i ^ bit) for i in range(n)])]
  transfers between devices with their start and end apart: 20 -> 21, of which waited for: 9 -> 10; matrix products, arithmetic and copies ran while one was open for 1% -> 1% of each run, Pallas kernels for 5% -> 5%
where the time goes in v5:
time: 44.6 us; the launch traced here: 44.4 us
  starting transfers between devices  31.5 us (71%)
  Pallas kernels  5.86 us (13%)
  waiting for transfers between devices  5.68 us (13%)
  between operations  0.79 us (2%)
    ppermute x21, starting transfers between devices, swap(): return lax.ppermute(x, axis, [(i, i ^ bit) for i in range(n)])  31.5 us
    ppermute x21, waiting for transfers between devices, swap(): return lax.ppermute(x, axis, [(i, i ^ bit) for i in range(n)])  5.68 us
    pallas_call x1, Pallas kernels, statistics(): pl.pallas_call(stats_kernel, out_shape=(shape,) * 3, in_specs=[VMEM] * 4,...  2.15 us
    pallas_call x1, Pallas kernels, pick(): pl.pallas_call(functools.partial(pick_kernel, groups), out_shape=shapes *...  1.61 us
    pallas_call x1, Pallas kernels, precondition(): pl.pallas_call(functools.partial(main_kernel, spots), out_shape=[jax.Shap...  1.31 us
  transfers between devices with their start and end apart: 21, of which 10 were waited for; matrix products, arithmetic and copies ran while one was open for 1% of the time, Pallas kernels for 5%

profile of v5, /device:TPU:0, one launch (start us, length us, event | category | flops | bytes accessed | tf_op | source)
XLA Modules:
  0.0 44.4 jit_solution(13567935049040266101)
XLA Ops:
  0.6 1.6 %pick.1 = (bf16[2,2,2,64,512]{4,3,2,1,0:T(8,128)(2,1)S(1)}, bf16[1,2,2,64,512]{4,3,2,1,0:T(8,128)(2,1)S(1)}, bf16[1,2,2,64,512]{4,3,2,1,0:T(8,128)(2,1)S(1)}, bf...) custom-call(bf16[1,2,64,8192]{3,2,1,0:T(8,128)(2,1)} %grads.1), custom_call_target="tpu_custom_call" | custom-call | bytes 4194304 | tf_op jit(solution)/shard_map/pick/pallas_call | solution.py:56
  2.3 0.5 %collective-permute-start.9 = (bf16[1,2,2,64,512]{4,3,1,2,0:T(8,128)(2,1)S(1)}, bf16[1,2,2,64,512]{4,3,1,2,0:T(8,128)(2,1)S(1)}, u32[]{:S(2)}, u32[]{:S(2)}) collective-permute-start(bf16[1,2,2,64,512]{4,3,1,2,0:T(8,128)(2,1)S(1)} %copy.13), channel_id=1, source_target_pairs={{0,8},{8,0},{16,24},{24,16},{1,9},{9,1},{17,25},{25,17},{2,10},{10... | collective-permute-start | bytes 786440 | tf_op jit(solution)/shard_map/ppermute | solution.py:17
  2.8 0.1 collective-permute-start.5
  2.9 0.5 %collective-permute-start = (bf16[2,2,2,64,512]{4,3,2,0,1:T(8,128)(2,1)S(1)}, bf16[2,2,2,64,512]{4,3,2,0,1:T(8,128)(2,1)S(1)}, u32[]{:S(2)}, u32[]{:S(2)}) collective-permute-start(bf16[2,2,2,64,512]{4,3,2,0,1:T(8,128)(2,1)S(1)} %copy.10), channel_id=1, source_target_pairs={{0,8},{8,0},{16,24},{24,16},{1,9},{9,1},{17,25},{25,17},{2,10},{10... | collective-permute-start | bytes 1572872 | tf_op jit(solution)/shard_map/ppermute | solution.py:17
  3.5 0.5 %collective-permute-done.9 = bf16[1,2,2,64,512]{4,3,1,2,0:T(8,128)(2,1)S(1)} collective-permute-done((bf16[1,2,2,64,512]{4,3,1,2,0:T(8,128)(2,1)S(1)}, bf16[1,2,2,64,512]{4,3,1,2,0:T(8,128)(2,1)S(1)}, u32[]{:S(2)}, u32[]{:S(2)}) %collective-permute-start.9) | collective-permute-done | bytes 262176 | tf_op jit(solution)/shard_map/ppermute | solution.py:17
  4.1 3.0 %collective-permute-start.10 = (bf16[1,1,1,64,512]{4,3,2,1,0:T(8,128)(2,1)S(1)}, bf16[1,1,1,64,512]{4,3,2,1,0:T(8,128)(2,1)S(1)}, u32[]{:S(2)}, u32[]{:S(2)}) collective-permute-start(bf16[1,1,1,64,512]{4,3,2,1,0:T(8,128)(2,1)S(1)} %fusion.12), channel_id=1, source_target_pairs={{0,16},{8,24},{16,0},{24,8},{1,17},{9,25},{17,1},{25,9},{2,18},{10... | collective-permute-start | bytes 196616 | tf_op jit(solution)/shard_map/ppermute | solution.py:17
  7.0 0.1 collective-permute-start.12
  7.1 0.0 collective-permute-done.5
  7.1 0.1 fusion.1
  7.2 0.0 copy-start
  7.2 0.0 copy-start.3
  7.2 0.0 copy-start.4
  7.2 2.0 %collective-permute-start.6 = (bf16[1,1,2,64,512]{4,3,2,1,0:T(8,128)(2,1)S(1)}, bf16[1,1,2,64,512]{4,3,2,1,0:T(8,128)(2,1)S(1)}, u32[]{:S(2)}, u32[]{:S(2)}) collective-permute-start(bf16[1,1,2,64,512]{4,3,2,1,0:T(8,128)(2,1)S(1)} %get-tuple-element.46), channel_id=1, source_target_pairs={{0,16},{8,24},{16,0},{24,8},{1,17},{9,25},{17,1},{25,9},{2,18},{10... | collective-permute-start | bytes 393224 | tf_op jit(solution)/shard_map/ppermute | solution.py:17
  9.2 0.3 collective-permute-done.10
  9.5 3.3 %collective-permute-start.11 = (bf16[1,64,512]{2,1,0:T(8,128)(2,1)S(1)}, bf16[1,64,512]{2,1,0:T(8,128)(2,1)S(1)}, u32[]{:S(2)}, u32[]{:S(2)}) collective-permute-start(bf16[1,64,512]{2,1,0:T(8,128)(2,1)S(1)} %fusion.9), channel_id=1, source_target_pairs={{0,4},{1,5},{2,6},{3,7},{4,0},{5,1},{6,2},{7,3},{8,12},{9,13},{10,... | collective-permute-start | bytes 196616 | tf_op jit(solution)/shard_map/ppermute | solution.py:17
  12.8 0.0 collective-permute-done
  12.8 0.1 fusion
  13.0 1.9 %collective-permute-start.1 = (bf16[2,1,2,64,512]{4,3,2,1,0:T(8,128)(2,1)S(1)}, bf16[2,1,2,64,512]{4,3,2,1,0:T(8,128)(2,1)S(1)}, u32[]{:S(2)}, u32[]{:S(2)}) collective-permute-start(bf16[2,1,2,64,512]{4,3,2,1,0:T(8,128)(2,1)S(1)} %get-tuple-element.40), channel_id=1, source_target_pairs={{0,16},{8,24},{16,0},{24,8},{1,17},{9,25},{17,1},{25,9},{2,18},{10... | collective-permute-start | bytes 786440 | tf_op jit(solution)/shard_map/ppermute | solution.py:17
  14.9 0.0 copy-start.1
  14.9 0.0 copy-start.2
  14.9 1.3 %collective-permute-start.13 = (bf16[1,64,512]{2,1,0:T(8,128)(2,1)S(1)}, bf16[1,64,512]{2,1,0:T(8,128)(2,1)S(1)}, u32[]{:S(2)}, u32[]{:S(2)}) collective-permute-start(bf16[1,64,512]{2,1,0:T(8,128)(2,1)S(1)} %fusion.11), channel_id=1, source_target_pairs={{0,5},{1,4},{2,7},{3,6},{4,1},{5,0},{6,3},{7,2},{8,13},{9,12},{10,... | collective-permute-start | bytes 196616 | tf_op jit(solution)/shard_map/ppermute | solution.py:17
  16.2 0.0 collective-permute-done.6
  16.3 3.6 %collective-permute-start.8 = (bf16[1,64,512]{2,1,0:T(8,128)(2,1)S(1)}, bf16[1,64,512]{2,1,0:T(8,128)(2,1)S(1)}, u32[]{:S(2)}, u32[]{:S(2)}) collective-permute-start(bf16[1,64,512]{2,1,0:T(8,128)(2,1)S(1)} %get-tuple-element.48), channel_id=1, source_target_pairs={{0,7},{1,6},{2,5},{3,4},{4,3},{5,2},{6,1},{7,0},{8,15},{9,14},{10,... | collective-permute-start | bytes 196616 | tf_op jit(solution)/shard_map/ppermute | solution.py:17
  19.9 0.2 collective-permute-start.7
  20.1 0.1 fusion.16
  20.2 2.1 %collective-permute-start.4 = (bf16[1,64,512]{2,1,0:T(8,128)(2,1)S(1)}, bf16[1,64,512]{2,1,0:T(8,128)(2,1)S(1)}, u32[]{:S(2)}, u32[]{:S(2)}) collective-permute-start(bf16[1,64,512]{2,1,0:T(8,128)(2,1)S(1)} %get-tuple-element.42), channel_id=1, source_target_pairs={{0,3},{1,2},{2,1},{3,0},{4,7},{5,6},{6,5},{7,4},{8,11},{9,10},{10,... | collective-permute-start | bytes 196616 | tf_op jit(solution)/shard_map/ppermute | solution.py:17
  22.3 1.0 %collective-permute-start.3 = (bf16[1,64,512]{2,1,0:T(8,128)(2,1)S(1)}, bf16[1,64,512]{2,1,0:T(8,128)(2,1)S(1)}, u32[]{:S(2)}, u32[]{:S(2)}) collective-permute-start(bf16[1,64,512]{2,1,0:T(8,128)(2,1)S(1)} %get-tuple-element.43), channel_id=1, source_target_pairs={{0,2},{1,3},{2,0},{3,1},{4,6},{5,7},{6,4},{7,5},{8,10},{9,11},{10,... | collective-permute-start | bytes 196616 | tf_op jit(solution)/shard_map/ppermute | solution.py:17
  23.2 0.0 collective-permute-done.13.refs_7_
  23.2 0.5 %collective-permute-start.2 = (bf16[1,64,512]{2,1,0:T(8,128)(2,1)S(1)}, bf16[1,64,512]{2,1,0:T(8,128)(2,1)S(1)}, u32[]{:S(2)}, u32[]{:S(2)}) collective-permute-start(bf16[1,64,512]{2,1,0:T(8,128)(2,1)S(1)} %get-tuple-element.44), channel_id=1, source_target_pairs={{0,1},{1,0},{2,3},{3,2},{4,5},{5,4},{6,7},{7,6},{8,9},{9,8},{10,11... | collective-permute-start | bytes 196616 | tf_op jit(solution)/shard_map/ppermute | solution.py:17
  23.8 0.1 collective-permute-done.8.refs_5_
  23.9 2.3 %collective-permute-done.7.refs_4_ = bf16[1,64,512]{2,1,0:T(8,128)(2,1)S(1)} collective-permute-done((bf16[1,64,512]{2,1,0:T(8,128)(2,1)S(1)}, bf16[1,64,512]{2,1,0:T(8,128)(2,1)S(1)}, u32[]{:S(2)}, u32[]{:S(2)}) %collective-permute-start.7) | collective-permute-done | bytes 65568 | tf_op jit(solution)/shard_map/ppermute | solution.py:17
  26.2 0.0 collective-permute-done.4.refs_3_
  26.2 0.7 %collective-permute-done.3.refs_2_ = bf16[1,64,512]{2,1,0:T(8,128)(2,1)S(1)} collective-permute-done((bf16[1,64,512]{2,1,0:T(8,128)(2,1)S(1)}, bf16[1,64,512]{2,1,0:T(8,128)(2,1)S(1)}, u32[]{:S(2)}, u32[]{:S(2)}) %collective-permute-start.3) | collective-permute-done | bytes 65568 | tf_op jit(solution)/shard_map/ppermute | solution.py:17
  26.9 0.6 %collective-permute-done.2.refs_1_ = bf16[1,64,512]{2,1,0:T(8,128)(2,1)S(1)} collective-permute-done((bf16[1,64,512]{2,1,0:T(8,128)(2,1)S(1)}, bf16[1,64,512]{2,1,0:T(8,128)(2,1)S(1)}, u32[]{:S(2)}, u32[]{:S(2)}) %collective-permute-start.2) | collective-permute-done | bytes 65568 | tf_op jit(solution)/shard_map/ppermute | solution.py:17
  27.5 1.3 %precondition.1 = (bf16[1,64,512]{2,1,0:T(8,128)(2,1)S(1)}, bf16[1,64,512]{2,1,0:T(8,128)(2,1)S(1)}, bf16[1,64,512]{2,1,0:T(8,128)(2,1)S(1)}, bf16[1,64,512]{2,1...) custom-call(bf16[1,64,512]{2,1,0:T(8,128)(2,1)S(1)} %get-tuple-eleme, ...), custom_call_target="tpu_custom_call" | custom-call | flops 536870912 | bytes 3145728 | tf_op jit(solution)/shard_map/precondition/pallas_call | solution.py:99
  28.8 3.6 %collective-permute-start.14 = (bf16[1,64,512]{2,1,0:T(8,128)(2,1)S(1)}, bf16[1,64,512]{2,1,0:T(8,128)(2,1)S(1)}, u32[]{:S(2)}, u32[]{:S(2)}) collective-permute-start(bf16[1,64,512]{2,1,0:T(8,128)(2,1)S(1)} %get-tuple-element.28), channel_id=1, source_target_pairs={{0,7},{1,6},{2,5},{3,4},{4,3},{5,2},{6,1},{7,0},{8,15},{9,14},{10,... | collective-permute-start | bytes 196616 | tf_op jit(solution)/shard_map/ppermute | solution.py:17
  32.5 0.3 collective-permute-start.15
  32.8 1.3 %collective-permute-start.16 = (bf16[1,64,512]{2,1,0:T(8,128)(2,1)S(1)}, bf16[1,64,512]{2,1,0:T(8,128)(2,1)S(1)}, u32[]{:S(2)}, u32[]{:S(2)}) collective-permute-start(bf16[1,64,512]{2,1,0:T(8,128)(2,1)S(1)} %get-tuple-element.30), channel_id=1, source_target_pairs={{0,5},{1,4},{2,7},{3,6},{4,1},{5,0},{6,3},{7,2},{8,13},{9,12},{10,... | collective-permute-start | bytes 196616 | tf_op jit(solution)/shard_map/ppermute | solution.py:17
  34.0 2.5 %collective-permute-start.17 = (bf16[1,64,512]{2,1,0:T(8,128)(2,1)S(1)}, bf16[1,64,512]{2,1,0:T(8,128)(2,1)S(1)}, u32[]{:S(2)}, u32[]{:S(2)}) collective-permute-start(bf16[1,64,512]{2,1,0:T(8,128)(2,1)S(1)} %get-tuple-element.31), channel_id=1, source_target_pairs={{0,4},{1,5},{2,6},{3,7},{4,0},{5,1},{6,2},{7,3},{8,12},{9,13},{10,... | collective-permute-start | bytes 196616 | tf_op jit(solution)/shard_map/ppermute | solution.py:17
  36.6 1.3 %collective-permute-start.18 = (bf16[1,64,512]{2,1,0:T(8,128)(2,1)S(1)}, bf16[1,64,512]{2,1,0:T(8,128)(2,1)S(1)}, u32[]{:S(2)}, u32[]{:S(2)}) collective-permute-start(bf16[1,64,512]{2,1,0:T(8,128)(2,1)S(1)} %get-tuple-element.32), channel_id=1, source_target_pairs={{0,3},{1,2},{2,1},{3,0},{4,7},{5,6},{6,5},{7,4},{8,11},{9,10},{10,... | collective-permute-start | bytes 196616 | tf_op jit(solution)/shard_map/ppermute | solution.py:17
  37.8 0.8 %collective-permute-start.19 = (bf16[1,64,512]{2,1,0:T(8,128)(2,1)S(1)}, bf16[1,64,512]{2,1,0:T(8,128)(2,1)S(1)}, u32[]{:S(2)}, u32[]{:S(2)}) collective-permute-start(bf16[1,64,512]{2,1,0:T(8,128)(2,1)S(1)} %get-tuple-element.33), channel_id=1, source_target_pairs={{0,2},{1,3},{2,0},{3,1},{4,6},{5,7},{6,4},{7,5},{8,10},{9,11},{10,... | collective-permute-start | bytes 196616 | tf_op jit(solution)/shard_map/ppermute | solution.py:17
  38.6 0.5 %collective-permute-done.15.refs_1_ = bf16[1,64,512]{2,1,0:T(8,128)(2,1)S(1)} collective-permute-done((bf16[1,64,512]{2,1,0:T(8,128)(2,1)S(1)}, bf16[1,64,512]{2,1,0:T(8,128)(2,1)S(1)}, u32[]{:S(2)}, u32[]{:S(2)}) %collective-permute-start.15) | collective-permute-done | bytes 65568 | tf_op jit(solution)/shard_map/ppermute | solution.py:17
  39.1 1.6 %collective-permute-start.20 = (bf16[1,64,512]{2,1,0:T(8,128)(2,1)S(1)}, bf16[1,64,512]{2,1,0:T(8,128)(2,1)S(1)}, u32[]{:S(2)}, u32[]{:S(2)}) collective-permute-start(bf16[1,64,512]{2,1,0:T(8,128)(2,1)S(1)} %get-tuple-element.34), channel_id=1, source_target_pairs={{0,1},{1,0},{2,3},{3,2},{4,5},{5,4},{6,7},{7,6},{8,9},{9,8},{10,11... | collective-permute-start | bytes 196616 | tf_op jit(solution)/shard_map/ppermute | solution.py:17
  40.7 2.2 %statistics.1 = (f32[1,512,512]{2,1,0:T(8,128)}, f32[1,512,512]{2,1,0:T(8,128)}, f32[1,512,512]{2,1,0:T(8,128)}) custom-call(bf16[512,512]{1,0:T(8,128)(2,1)S(1)} %get-tuple-element.36.block, f32[1,512,512]{2,1,0:T(8,128)S(1)} %copy-done.1, f32[1,512,512]{2,1,0:T(8,128)S(1)} %copy-done.2, f32[1,512,512]{2,1,0:T(8,128)S(1)} %copy-done), custom_call_target="tpu_custom_call" | custom-call | flops 536870912 | bytes 6815744 | tf_op jit(solution)/shard_map/statistics/pallas_call | solution.py:132
  42.9 0.1 collective-permute-done.16.refs_2_
  43.0 0.3 collective-permute-done.19.refs_5_
  43.3 0.3 collective-permute-done.20.refs_6_
  43.6 0.8 %assemble.1 = bf16[2,64,2048]{2,1,0:T(8,128)(2,1)} custom-call(bf16[1,64,512]{2,1,0:T(8,128)(2,1)S(1)} %collective-permute-done.14.refs_0_, bf16[1,64,512]{2,1,0:T(8,128)(2,1)S(1)} %collective-permute-done.15.refs_1_, bf16[1,64,512]{2,1,0:T(8,128)(2,1)S(1)} %collective-permute-done.16.refs_2_, bf16[1,64,512]{2,1,0:T(8,128)(2,1)S(1)} %collective-permute-done.17.refs_3_, ...), custom_call_target="tpu_custom_call" | custom-call | bytes 1048576 | tf_op jit(solution)/shard_map/assemble/pallas_call | solution.py:166
  (22 shorter events, 0.3 us)
Async XLA Ops:
  2.3 1.7 %collective-permute-start.9 = (bf16[1,2,2,64,512]{4,3,1,2,0:T(8,128)(2,1)S(1)}, bf16[1,2,2,64,512]{4,3,1,2,0:T(8,128)(2,1)S(1)}, u32[]{:S(2)}, u32[]{:S(2)}) collective-permute-start(bf16[1,2,2,64,512]{4,3,1,2,0:T(8,128)(2,1)S(1)} %copy.13), channel_id=1, source_target_pairs={{0,8},{8,0},{16,24},{24,16},{1,9},{9,1},{17,25},{25,17},{2,10},{10... | collective-permute-start | bytes 786440 | tf_op jit(solution)/shard_map/ppermute | solution.py:17
  2.8 4.3 %collective-permute-start.5 = (bf16[1,2,2,64,512]{4,3,2,1,0:T(8,128)(2,1)S(1)}, bf16[1,2,2,64,512]{4,3,2,1,0:T(8,128)(2,1)S(1)}, u32[]{:S(2)}, u32[]{:S(2)}) collective-permute-start(bf16[1,2,2,64,512]{4,3,2,1,0:T(8,128)(2,1)S(1)} %get-tuple-element.24), channel_id=1, source_target_pairs={{0,8},{8,0},{16,24},{24,16},{1,9},{9,1},{17,25},{25,17},{2,10},{10... | collective-permute-start | bytes 786440 | tf_op jit(solution)/shard_map/ppermute | solution.py:17
  2.9 9.9 %collective-permute-start = (bf16[2,2,2,64,512]{4,3,2,0,1:T(8,128)(2,1)S(1)}, bf16[2,2,2,64,512]{4,3,2,0,1:T(8,128)(2,1)S(1)}, u32[]{:S(2)}, u32[]{:S(2)}) collective-permute-start(bf16[2,2,2,64,512]{4,3,2,0,1:T(8,128)(2,1)S(1)} %copy.10), channel_id=1, source_target_pairs={{0,8},{8,0},{16,24},{24,16},{1,9},{9,1},{17,25},{25,17},{2,10},{10... | collective-permute-start | bytes 1572872 | tf_op jit(solution)/shard_map/ppermute | solution.py:17
  4.1 5.4 %collective-permute-start.10 = (bf16[1,1,1,64,512]{4,3,2,1,0:T(8,128)(2,1)S(1)}, bf16[1,1,1,64,512]{4,3,2,1,0:T(8,128)(2,1)S(1)}, u32[]{:S(2)}, u32[]{:S(2)}) collective-permute-start(bf16[1,1,1,64,512]{4,3,2,1,0:T(8,128)(2,1)S(1)} %fusion.12), channel_id=1, source_target_pairs={{0,16},{8,24},{16,0},{24,8},{1,17},{9,25},{17,1},{25,9},{2,18},{10... | collective-permute-start | bytes 196616 | tf_op jit(solution)/shard_map/ppermute | solution.py:17
  7.0 7.8 %collective-permute-start.12 = (bf16[1,1,1,64,512]{4,3,2,1,0:T(8,128)(2,1)S(1)}, bf16[1,1,1,64,512]{4,3,2,1,0:T(8,128)(2,1)S(1)}, u32[]{:S(2)}, u32[]{:S(2)}) collective-permute-start(bf16[1,1,1,64,512]{4,3,2,1,0:T(8,128)(2,1)S(1)} %get-tuple-element.50), channel_id=1, source_target_pairs={{0,16},{8,24},{16,0},{24,8},{1,17},{9,25},{17,1},{25,9},{2,18},{10... | collective-permute-start | bytes 196616 | tf_op jit(solution)/shard_map/ppermute | solution.py:17
  7.2 20.3 %copy-start = (f32[1,512,512]{2,1,0:T(8,128)S(1)}, f32[1,512,512]{2,1,0:T(8,128)}, u32[]{:S(2)}) copy-start(f32[1,512,512]{2,1,0:T(8,128)} %accum.1) | copy-start | bytes 3145732
  7.2 20.3 %copy-start.3 = (bf16[1,512,512]{2,1,0:T(8,128)(2,1)S(1)}, bf16[1,512,512]{2,1,0:T(8,128)(2,1)}, u32[]{:S(2)}) copy-start(bf16[1,512,512]{2,1,0:T(8,128)(2,1)} %refs_8_.1) | copy-start | bytes 1572868
  7.2 20.3 %copy-start.4 = (bf16[1,512,512]{2,1,0:T(8,128)(2,1)S(1)}, bf16[1,512,512]{2,1,0:T(8,128)(2,1)}, u32[]{:S(2)}) copy-start(bf16[1,512,512]{2,1,0:T(8,128)(2,1)} %refs_9_.1) | copy-start | bytes 1572868
  7.2 9.0 %collective-permute-start.6 = (bf16[1,1,2,64,512]{4,3,2,1,0:T(8,128)(2,1)S(1)}, bf16[1,1,2,64,512]{4,3,2,1,0:T(8,128)(2,1)S(1)}, u32[]{:S(2)}, u32[]{:S(2)}) collective-permute-start(bf16[1,1,2,64,512]{4,3,2,1,0:T(8,128)(2,1)S(1)} %get-tuple-element.46), channel_id=1, source_target_pairs={{0,16},{8,24},{16,0},{24,8},{1,17},{9,25},{17,1},{25,9},{2,18},{10... | collective-permute-start | bytes 393224 | tf_op jit(solution)/shard_map/ppermute | solution.py:17
  9.5 12.8 %collective-permute-start.11 = (bf16[1,64,512]{2,1,0:T(8,128)(2,1)S(1)}, bf16[1,64,512]{2,1,0:T(8,128)(2,1)S(1)}, u32[]{:S(2)}, u32[]{:S(2)}) collective-permute-start(bf16[1,64,512]{2,1,0:T(8,128)(2,1)S(1)} %fusion.9), channel_id=1, source_target_pairs={{0,4},{1,5},{2,6},{3,7},{4,0},{5,1},{6,2},{7,3},{8,12},{9,13},{10,... | collective-permute-start | bytes 196616 | tf_op jit(solution)/shard_map/ppermute | solution.py:17
  13.0 7.1 %collective-permute-start.1 = (bf16[2,1,2,64,512]{4,3,2,1,0:T(8,128)(2,1)S(1)}, bf16[2,1,2,64,512]{4,3,2,1,0:T(8,128)(2,1)S(1)}, u32[]{:S(2)}, u32[]{:S(2)}) collective-permute-start(bf16[2,1,2,64,512]{4,3,2,1,0:T(8,128)(2,1)S(1)} %get-tuple-element.40), channel_id=1, source_target_pairs={{0,16},{8,24},{16,0},{24,8},{1,17},{9,25},{17,1},{25,9},{2,18},{10... | collective-permute-start | bytes 786440 | tf_op jit(solution)/shard_map/ppermute | solution.py:17
  14.9 25.8 %copy-start.1 = (f32[1,512,512]{2,1,0:T(8,128)S(1)}, f32[1,512,512]{2,1,0:T(8,128)}, u32[]{:S(2)}) copy-start(f32[1,512,512]{2,1,0:T(8,128)} %left.1) | copy-start | bytes 3145732
  14.9 25.8 %copy-start.2 = (f32[1,512,512]{2,1,0:T(8,128)S(1)}, f32[1,512,512]{2,1,0:T(8,128)}, u32[]{:S(2)}) copy-start(f32[1,512,512]{2,1,0:T(8,128)} %right.1) | copy-start | bytes 3145732
  14.9 8.3 %collective-permute-start.13 = (bf16[1,64,512]{2,1,0:T(8,128)(2,1)S(1)}, bf16[1,64,512]{2,1,0:T(8,128)(2,1)S(1)}, u32[]{:S(2)}, u32[]{:S(2)}) collective-permute-start(bf16[1,64,512]{2,1,0:T(8,128)(2,1)S(1)} %fusion.11), channel_id=1, source_target_pairs={{0,5},{1,4},{2,7},{3,6},{4,1},{5,0},{6,3},{7,2},{8,13},{9,12},{10,... | collective-permute-start | bytes 196616 | tf_op jit(solution)/shard_map/ppermute | solution.py:17
  16.3 7.6 %collective-permute-start.8 = (bf16[1,64,512]{2,1,0:T(8,128)(2,1)S(1)}, bf16[1,64,512]{2,1,0:T(8,128)(2,1)S(1)}, u32[]{:S(2)}, u32[]{:S(2)}) collective-permute-start(bf16[1,64,512]{2,1,0:T(8,128)(2,1)S(1)} %get-tuple-element.48), channel_id=1, source_target_pairs={{0,7},{1,6},{2,5},{3,4},{4,3},{5,2},{6,1},{7,0},{8,15},{9,14},{10,... | collective-permute-start | bytes 196616 | tf_op jit(solution)/shard_map/ppermute | solution.py:17
  19.9 6.2 %collective-permute-start.7 = (bf16[1,64,512]{2,1,0:T(8,128)(2,1)S(1)}, bf16[1,64,512]{2,1,0:T(8,128)(2,1)S(1)}, u32[]{:S(2)}, u32[]{:S(2)}) collective-permute-start(bf16[1,64,512]{2,1,0:T(8,128)(2,1)S(1)} %get-tuple-element.49), channel_id=1, source_target_pairs={{0,6},{1,7},{2,4},{3,5},{4,2},{5,3},{6,0},{7,1},{8,14},{9,15},{10,... | collective-permute-start | bytes 196616 | tf_op jit(solution)/shard_map/ppermute | solution.py:17
  20.2 6.0 %collective-permute-start.4 = (bf16[1,64,512]{2,1,0:T(8,128)(2,1)S(1)}, bf16[1,64,512]{2,1,0:T(8,128)(2,1)S(1)}, u32[]{:S(2)}, u32[]{:S(2)}) collective-permute-start(bf16[1,64,512]{2,1,0:T(8,128)(2,1)S(1)} %get-tuple-element.42), channel_id=1, source_target_pairs={{0,3},{1,2},{2,1},{3,0},{4,7},{5,6},{6,5},{7,4},{8,11},{9,10},{10,... | collective-permute-start | bytes 196616 | tf_op jit(solution)/shard_map/ppermute | solution.py:17
  22.3 4.6 %collective-permute-start.3 = (bf16[1,64,512]{2,1,0:T(8,128)(2,1)S(1)}, bf16[1,64,512]{2,1,0:T(8,128)(2,1)S(1)}, u32[]{:S(2)}, u32[]{:S(2)}) collective-permute-start(bf16[1,64,512]{2,1,0:T(8,128)(2,1)S(1)} %get-tuple-element.43), channel_id=1, source_target_pairs={{0,2},{1,3},{2,0},{3,1},{4,6},{5,7},{6,4},{7,5},{8,10},{9,11},{10,... | collective-permute-start | bytes 196616 | tf_op jit(solution)/shard_map/ppermute | solution.py:17
  23.2 4.3 %collective-permute-start.2 = (bf16[1,64,512]{2,1,0:T(8,128)(2,1)S(1)}, bf16[1,64,512]{2,1,0:T(8,128)(2,1)S(1)}, u32[]{:S(2)}, u32[]{:S(2)}) collective-permute-start(bf16[1,64,512]{2,1,0:T(8,128)(2,1)S(1)} %get-tuple-element.44), channel_id=1, source_target_pairs={{0,1},{1,0},{2,3},{3,2},{4,5},{5,4},{6,7},{7,6},{8,9},{9,8},{10,11... | collective-permute-start | bytes 196616 | tf_op jit(solution)/shard_map/ppermute | solution.py:17
  28.8 9.0 %collective-permute-start.14 = (bf16[1,64,512]{2,1,0:T(8,128)(2,1)S(1)}, bf16[1,64,512]{2,1,0:T(8,128)(2,1)S(1)}, u32[]{:S(2)}, u32[]{:S(2)}) collective-permute-start(bf16[1,64,512]{2,1,0:T(8,128)(2,1)S(1)} %get-tuple-element.28), channel_id=1, source_target_pairs={{0,7},{1,6},{2,5},{3,4},{4,3},{5,2},{6,1},{7,0},{8,15},{9,14},{10,... | collective-permute-start | bytes 196616 | tf_op jit(solution)/shard_map/ppermute | solution.py:17
  32.5 6.6 %collective-permute-start.15 = (bf16[1,64,512]{2,1,0:T(8,128)(2,1)S(1)}, bf16[1,64,512]{2,1,0:T(8,128)(2,1)S(1)}, u32[]{:S(2)}, u32[]{:S(2)}) collective-permute-start(bf16[1,64,512]{2,1,0:T(8,128)(2,1)S(1)} %get-tuple-element.29), channel_id=1, source_target_pairs={{0,6},{1,7},{2,4},{3,5},{4,2},{5,3},{6,0},{7,1},{8,14},{9,15},{10,... | collective-permute-start | bytes 196616 | tf_op jit(solution)/shard_map/ppermute | solution.py:17
  32.8 10.2 %collective-permute-start.16 = (bf16[1,64,512]{2,1,0:T(8,128)(2,1)S(1)}, bf16[1,64,512]{2,1,0:T(8,128)(2,1)S(1)}, u32[]{:S(2)}, u32[]{:S(2)}) collective-permute-start(bf16[1,64,512]{2,1,0:T(8,128)(2,1)S(1)} %get-tuple-element.30), channel_id=1, source_target_pairs={{0,5},{1,4},{2,7},{3,6},{4,1},{5,0},{6,3},{7,2},{8,13},{9,12},{10,... | collective-permute-start | bytes 196616 | tf_op jit(solution)/shard_map/ppermute | solution.py:17
  34.0 8.9 %collective-permute-start.17 = (bf16[1,64,512]{2,1,0:T(8,128)(2,1)S(1)}, bf16[1,64,512]{2,1,0:T(8,128)(2,1)S(1)}, u32[]{:S(2)}, u32[]{:S(2)}) collective-permute-start(bf16[1,64,512]{2,1,0:T(8,128)(2,1)S(1)} %get-tuple-element.31), channel_id=1, source_target_pairs={{0,4},{1,5},{2,6},{3,7},{4,0},{5,1},{6,2},{7,3},{8,12},{9,13},{10,... | collective-permute-start | bytes 196616 | tf_op jit(solution)/shard_map/ppermute | solution.py:17
  36.6 6.4 %collective-permute-start.18 = (bf16[1,64,512]{2,1,0:T(8,128)(2,1)S(1)}, bf16[1,64,512]{2,1,0:T(8,128)(2,1)S(1)}, u32[]{:S(2)}, u32[]{:S(2)}) collective-permute-start(bf16[1,64,512]{2,1,0:T(8,128)(2,1)S(1)} %get-tuple-element.32), channel_id=1, source_target_pairs={{0,3},{1,2},{2,1},{3,0},{4,7},{5,6},{6,5},{7,4},{8,11},{9,10},{10,... | collective-permute-start | bytes 196616 | tf_op jit(solution)/shard_map/ppermute | solution.py:17
  37.8 5.5 %collective-permute-start.19 = (bf16[1,64,512]{2,1,0:T(8,128)(2,1)S(1)}, bf16[1,64,512]{2,1,0:T(8,128)(2,1)S(1)}, u32[]{:S(2)}, u32[]{:S(2)}) collective-permute-start(bf16[1,64,512]{2,1,0:T(8,128)(2,1)S(1)} %get-tuple-element.33), channel_id=1, source_target_pairs={{0,2},{1,3},{2,0},{3,1},{4,6},{5,7},{6,4},{7,5},{8,10},{9,11},{10,... | collective-permute-start | bytes 196616 | tf_op jit(solution)/shard_map/ppermute | solution.py:17
  39.1 4.5 %collective-permute-start.20 = (bf16[1,64,512]{2,1,0:T(8,128)(2,1)S(1)}, bf16[1,64,512]{2,1,0:T(8,128)(2,1)S(1)}, u32[]{:S(2)}, u32[]{:S(2)}) collective-permute-start(bf16[1,64,512]{2,1,0:T(8,128)(2,1)S(1)} %get-tuple-element.34), channel_id=1, source_target_pairs={{0,1},{1,0},{2,3},{3,2},{4,5},{5,4},{6,7},{7,6},{8,9},{9,8},{10,11... | collective-permute-start | bytes 196616 | tf_op jit(solution)/shard_map/ppermute | solution.py:17

commit v6 on v5

--- a/solution.py
+++ b/solution.py
@@ -19,6 +19,11 @@
 
 def peer(k, e):
     return jnp.bitwise_xor(lax.axis_index("fsdp"), 2 * k + e)
+
+
+def further(d):
+    n = lax.axis_size("fsdp")
+    return lax.rem(lax.axis_index("fsdp") + (d + n), n)
 
 
 def pick_kernel(groups, grads, *refs):
@@ -66,19 +71,17 @@
     return outs[: len(groups)], outs[len(groups) :]
 
 
-def place(k, e, rows):
-    return pl.ds(pl.multiple_of(peer(k, e) * rows, rows), rows)
+def rows_of(device, rows):
+    return pl.ds(pl.multiple_of(device * rows, rows), rows)
 
 
 def main_kernel(spots, *refs):
-    ins, refs = refs[: len(spots)], refs[len(spots) :]
-    left_root, right_root, accum = refs[:3]
-    outs, (block_out, scaled) = refs[3:-2], refs[-2:]
+    ins, (left_root, right_root, accum) = refs[: len(spots)], refs[len(spots) : len(spots) + 3]
+    outs, (block_out, scaled) = refs[len(spots) + 3 : -2], refs[-2:]
     rows = ins[0].shape[-2]
 
-    for ref, spot in zip(ins, spots):
-        for i, (k, e) in enumerate(spot):
-            block_out[place(k, e, rows)] = ref[i]
+    for ref, (k, e) in zip(ins, spots):
+        block_out[rows_of(peer(k, e), rows)] = ref[0]
     b = block_out[...]
     half = jnp.dot(left_root[0], b, preferred_element_type=jnp.float32).astype(jnp.bfloat16)
     precond = jnp.dot(half, right_root[0], preferred_element_type=jnp.float32)
@@ -88,22 +91,18 @@
     pre_sq = jnp.sum(precond * precond)
     ratio = jnp.sqrt(ada_sq) / jnp.sqrt(pre_sq + 1e-06)
     scaled[...] = (ratio * precond).astype(jnp.bfloat16)
-    for ref, spot in zip(outs, spots):
-        for i, (k, e) in enumerate(spot):
-            ref[i] = scaled[place(k, e, rows)]
+    for d, ref in enumerate(outs):
+        ref[0] = scaled[rows_of(further(d), rows)]
 
 
 def precondition(pieces, spots, left_root, right_root, accum):
     side = left_root.shape[1]
-    rows = pieces[0].shape[-2]
+    piece = jax.ShapeDtypeStruct(pieces[0].shape, jnp.bfloat16)
     outs = pl.pallas_call(
         functools.partial(main_kernel, spots),
-        out_shape=[
-            jax.ShapeDtypeStruct((len(s), rows, side), jnp.bfloat16) for s in spots
-        ]
-        + [jax.ShapeDtypeStruct((side, side), jnp.bfloat16)],
-        in_specs=[VMEM] * (len(spots) + 3),
-        out_specs=[VMEM] * (len(spots) + 1),
+        out_shape=[piece] * len(pieces) + [jax.ShapeDtypeStruct((side, side), jnp.bfloat16)],
+        in_specs=[VMEM] * (len(pieces) + 3),
+        out_specs=[VMEM] * (len(pieces) + 1),
         scratch_shapes=[pltpu.VMEM((side, side), jnp.bfloat16)],
         compiler_params=pltpu.CompilerParams(vmem_limit_bytes=16 * MIB),
         cost_estimate=pl.CostEstimate(
@@ -111,7 +110,7 @@
         ),
         name="precondition",
     )(*pieces, left_root, right_root, accum)
-    return dict(zip(spots, outs)), outs[-1]
+    return outs[:-1], outs[-1]
 
 
 def stats_kernel(block, left, right, accum, left_out, right_out, accum_out):
@@ -142,29 +141,28 @@
     )(block, left, right, accum)
 
 
-def assemble_kernel(spots, *refs):
-    ins, (update, sem) = refs[: len(spots)], refs[len(spots) :]
+def assemble_kernel(*refs):
+    pieces, (update, sem) = refs[:-2], refs[-2:]
     slabs = update.shape[0]
-    block = ins[0].shape[-1]
+    block = pieces[0].shape[-1]
     copies = []
-    for ref, spot in zip(ins, spots):
-        for i, (k, e) in enumerate(spot):
-            owner = peer(k, e)
-            start = pl.multiple_of(owner // slabs * block, block)
-            copies.append(
-                pltpu.make_async_copy(
-                    ref.at[i], update.at[lax.rem(owner, slabs), :, pl.ds(start, block)], sem
-                )
+    for d, ref in enumerate(pieces):
+        owner = further(-d)
+        start = pl.multiple_of(owner // slabs * block, block)
+        copies.append(
+            pltpu.make_async_copy(
+                ref.at[0], update.at[lax.rem(owner, slabs), :, pl.ds(start, block)], sem
             )
+        )
     for copy in copies:
         copy.start()
     for copy in copies:
         copy.wait()
 
 
-def assemble(pieces, spots, shape):
+def assemble(pieces, shape):
     return pl.pallas_call(
-        functools.partial(assemble_kernel, spots),
+        assemble_kernel,
         out_shape=jax.ShapeDtypeStruct(shape, jnp.bfloat16),
         in_specs=[ANY] * len(pieces),
         out_specs=ANY,
@@ -173,13 +171,6 @@
         cost_estimate=pl.CostEstimate(flops=0, bytes_accessed=MIB, transcendentals=0),
         name="assemble",
     )(*pieces)
-
-
-def exchange(get, peers, far_last):
-    ks = [0, 1, *range(peers - 1, 1, -1)] if far_last else range(peers - 1, -1, -1)
-    spots = [(k, e) for k in ks for e in ((0, 1) if far_last else (1, 0))]
-    pieces = [swap(get(k, e), "fsdp", 2 * k + e) if k + e else get(k, e) for k, e in spots]
-    return pieces, tuple((spot,) for spot in spots)
 
 
 def wide(terms):
@@ -215,12 +206,19 @@
     def summed_piece(k, e):
         return total(summed[k, e])
 
-    pieces, spots = exchange(summed_piece, peers, True)
-
+    spots = [(k, e) for k in (0, 1, *range(peers - 1, 1, -1)) for e in range(2)]
+    pieces = [
+        swap(summed_piece(k, e), "fsdp", 2 * k + e) if k + e else summed_piece(k, e)
+        for k, e in spots
+    ]
     scaled, block = precondition(pieces, spots, left_root, right_root, accum)
-    pieces, spots = exchange(lambda k, e: scaled[((k, e),)], peers, False)
+    returned = [
+        lax.ppermute(a, "fsdp", [(i, (i + d) % fsdp_count) for i in range(fsdp_count)])
+        for d, a in enumerate(scaled)
+        if d > 0
+    ]
     left_new, right_new, accum_new = statistics(block, left_stat, right_stat, accum)
-    update = assemble(pieces, spots, (slabs, rows, width // rep_count))
+    update = assemble([scaled[0], *returned], (slabs, rows, width // rep_count))
     return (update, left_new, right_new, accum_new)
 
 

time: 44.6 us -> 44 us (0.987)
  waiting for transfers between devices: 5.68 us -> 4.53 us
  starting transfers between devices: 31.5 us -> 32 us
    ppermute x0 -> x7, starting transfers between devices: none -> 11.9 us  [body(): lax.ppermute(a, 'fsdp', [(i, (i + d) % fsdp_count) for i in range(fsdp_co...]
    ppermute x21 -> x14, starting transfers between devices: 31.5 us -> 20.1 us  [swap(): return lax.ppermute(x, axis, [(i, i ^ bit) for i in range(n)])]
    ppermute x21 -> x14, waiting for transfers between devices: 5.68 us -> 4.51 us  [swap(): return lax.ppermute(x, axis, [(i, i ^ bit) for i in range(n)])]
  transfers between devices with their start and end apart: 21 -> 21, of which waited for: 10 -> 6; matrix products, arithmetic and copies ran while one was open for 1% -> 1% of each run, Pallas kernels for 5% -> 5%
where the time goes in v6:
time: 44 us; the launch traced here: 43.8 us
  starting transfers between devices  32 us (73%)
  Pallas kernels  5.87 us (13%)
  waiting for transfers between devices  4.53 us (10%)
  between operations  0.81 us (2%)
    ppermute x14, starting transfers between devices, swap(): return lax.ppermute(x, axis, [(i, i ^ bit) for i in range(n)])  20.1 us
    ppermute x7, starting transfers between devices, body(): lax.ppermute(a, 'fsdp', [(i, (i + d) % fsdp_count) for i in range(fsdp_co...  11.9 us
    ppermute x14, waiting for transfers between devices, swap(): return lax.ppermute(x, axis, [(i, i ^ bit) for i in range(n)])  4.51 us
    pallas_call x1, Pallas kernels, statistics(): pl.pallas_call(stats_kernel, out_shape=(shape,) * 3, in_specs=[VMEM] * 4,...  2.15 us
    pallas_call x1, Pallas kernels, pick(): pl.pallas_call(functools.partial(pick_kernel, groups), out_shape=shapes *...  1.61 us
    pallas_call x1, Pallas kernels, precondition(): pl.pallas_call(functools.partial(main_kernel, spots), out_shape=[piece] *...  1.31 us
  transfers between devices with their start and end apart: 21, of which 6 were waited for; matrix products, arithmetic and copies ran while one was open for 1% of the time, Pallas kernels for 5%

profile of v6, /device:TPU:0, one launch (start us, length us, event | category | flops | bytes accessed | tf_op | source)
XLA Modules:
  0.0 43.8 jit_solution(3536462971191220314)
XLA Ops:
  0.6 1.6 %pick.1 = (bf16[2,2,2,64,512]{4,3,2,1,0:T(8,128)(2,1)S(1)}, bf16[1,2,2,64,512]{4,3,2,1,0:T(8,128)(2,1)S(1)}, bf16[1,2,2,64,512]{4,3,2,1,0:T(8,128)(2,1)S(1)}, bf...) custom-call(bf16[1,2,64,8192]{3,2,1,0:T(8,128)(2,1)} %grads.1), custom_call_target="tpu_custom_call" | custom-call | bytes 4194304 | tf_op jit(solution)/shard_map/pick/pallas_call | solution.py:61
  2.3 0.5 %collective-permute-start.9 = (bf16[1,2,2,64,512]{4,3,1,2,0:T(8,128)(2,1)S(1)}, bf16[1,2,2,64,512]{4,3,1,2,0:T(8,128)(2,1)S(1)}, u32[]{:S(2)}, u32[]{:S(2)}) collective-permute-start(bf16[1,2,2,64,512]{4,3,1,2,0:T(8,128)(2,1)S(1)} %copy.13), channel_id=1, source_target_pairs={{0,8},{8,0},{16,24},{24,16},{1,9},{9,1},{17,25},{25,17},{2,10},{10... | collective-permute-start | bytes 786440 | tf_op jit(solution)/shard_map/ppermute | solution.py:17
  2.8 0.1 collective-permute-start.5
  2.9 0.5 %collective-permute-start = (bf16[2,2,2,64,512]{4,3,2,0,1:T(8,128)(2,1)S(1)}, bf16[2,2,2,64,512]{4,3,2,0,1:T(8,128)(2,1)S(1)}, u32[]{:S(2)}, u32[]{:S(2)}) collective-permute-start(bf16[2,2,2,64,512]{4,3,2,0,1:T(8,128)(2,1)S(1)} %copy.10), channel_id=1, source_target_pairs={{0,8},{8,0},{16,24},{24,16},{1,9},{9,1},{17,25},{25,17},{2,10},{10... | collective-permute-start | bytes 1572872 | tf_op jit(solution)/shard_map/ppermute | solution.py:17
  3.5 0.5 %collective-permute-done.9 = bf16[1,2,2,64,512]{4,3,1,2,0:T(8,128)(2,1)S(1)} collective-permute-done((bf16[1,2,2,64,512]{4,3,1,2,0:T(8,128)(2,1)S(1)}, bf16[1,2,2,64,512]{4,3,1,2,0:T(8,128)(2,1)S(1)}, u32[]{:S(2)}, u32[]{:S(2)}) %collective-permute-start.9) | collective-permute-done | bytes 262176 | tf_op jit(solution)/shard_map/ppermute | solution.py:17
  4.1 3.0 %collective-permute-start.10 = (bf16[1,1,1,64,512]{4,3,2,1,0:T(8,128)(2,1)S(1)}, bf16[1,1,1,64,512]{4,3,2,1,0:T(8,128)(2,1)S(1)}, u32[]{:S(2)}, u32[]{:S(2)}) collective-permute-start(bf16[1,1,1,64,512]{4,3,2,1,0:T(8,128)(2,1)S(1)} %fusion.12), channel_id=1, source_target_pairs={{0,16},{8,24},{16,0},{24,8},{1,17},{9,25},{17,1},{25,9},{2,18},{10... | collective-permute-start | bytes 196616 | tf_op jit(solution)/shard_map/ppermute | solution.py:17
  7.0 0.1 collective-permute-start.12
  7.1 0.0 collective-permute-done.5
  7.1 0.1 fusion.1
  7.2 0.0 copy-start
  7.2 0.0 copy-start.3
  7.2 0.0 copy-start.4
  7.2 2.0 %collective-permute-start.6 = (bf16[1,1,2,64,512]{4,3,2,1,0:T(8,128)(2,1)S(1)}, bf16[1,1,2,64,512]{4,3,2,1,0:T(8,128)(2,1)S(1)}, u32[]{:S(2)}, u32[]{:S(2)}) collective-permute-start(bf16[1,1,2,64,512]{4,3,2,1,0:T(8,128)(2,1)S(1)} %get-tuple-element.46), channel_id=1, source_target_pairs={{0,16},{8,24},{16,0},{24,8},{1,17},{9,25},{17,1},{25,9},{2,18},{10... | collective-permute-start | bytes 393224 | tf_op jit(solution)/shard_map/ppermute | solution.py:17
  9.2 0.3 collective-permute-done.10
  9.5 3.3 %collective-permute-start.11 = (bf16[1,64,512]{2,1,0:T(8,128)(2,1)S(1)}, bf16[1,64,512]{2,1,0:T(8,128)(2,1)S(1)}, u32[]{:S(2)}, u32[]{:S(2)}) collective-permute-start(bf16[1,64,512]{2,1,0:T(8,128)(2,1)S(1)} %fusion.9), channel_id=1, source_target_pairs={{0,4},{1,5},{2,6},{3,7},{4,0},{5,1},{6,2},{7,3},{8,12},{9,13},{10,... | collective-permute-start | bytes 196616 | tf_op jit(solution)/shard_map/ppermute | solution.py:17
  12.8 0.1 fusion
  13.0 1.9 %collective-permute-start.1 = (bf16[2,1,2,64,512]{4,3,2,1,0:T(8,128)(2,1)S(1)}, bf16[2,1,2,64,512]{4,3,2,1,0:T(8,128)(2,1)S(1)}, u32[]{:S(2)}, u32[]{:S(2)}) collective-permute-start(bf16[2,1,2,64,512]{4,3,2,1,0:T(8,128)(2,1)S(1)} %get-tuple-element.40), channel_id=1, source_target_pairs={{0,16},{8,24},{16,0},{24,8},{1,17},{9,25},{17,1},{25,9},{2,18},{10... | collective-permute-start | bytes 786440 | tf_op jit(solution)/shard_map/ppermute | solution.py:17
  14.9 0.0 copy-start.1
  14.9 0.0 copy-start.2
  14.9 1.3 %collective-permute-start.13 = (bf16[1,64,512]{2,1,0:T(8,128)(2,1)S(1)}, bf16[1,64,512]{2,1,0:T(8,128)(2,1)S(1)}, u32[]{:S(2)}, u32[]{:S(2)}) collective-permute-start(bf16[1,64,512]{2,1,0:T(8,128)(2,1)S(1)} %fusion.11), channel_id=1, source_target_pairs={{0,5},{1,4},{2,7},{3,6},{4,1},{5,0},{6,3},{7,2},{8,13},{9,12},{10,... | collective-permute-start | bytes 196616 | tf_op jit(solution)/shard_map/ppermute | solution.py:17
  16.2 0.0 collective-permute-done.6
  16.3 3.6 %collective-permute-start.8 = (bf16[1,64,512]{2,1,0:T(8,128)(2,1)S(1)}, bf16[1,64,512]{2,1,0:T(8,128)(2,1)S(1)}, u32[]{:S(2)}, u32[]{:S(2)}) collective-permute-start(bf16[1,64,512]{2,1,0:T(8,128)(2,1)S(1)} %get-tuple-element.48), channel_id=1, source_target_pairs={{0,7},{1,6},{2,5},{3,4},{4,3},{5,2},{6,1},{7,0},{8,15},{9,14},{10,... | collective-permute-start | bytes 196616 | tf_op jit(solution)/shard_map/ppermute | solution.py:17
  19.9 0.2 collective-permute-start.7
  20.1 0.1 fusion.16
  20.2 2.1 %collective-permute-start.4 = (bf16[1,64,512]{2,1,0:T(8,128)(2,1)S(1)}, bf16[1,64,512]{2,1,0:T(8,128)(2,1)S(1)}, u32[]{:S(2)}, u32[]{:S(2)}) collective-permute-start(bf16[1,64,512]{2,1,0:T(8,128)(2,1)S(1)} %get-tuple-element.42), channel_id=1, source_target_pairs={{0,3},{1,2},{2,1},{3,0},{4,7},{5,6},{6,5},{7,4},{8,11},{9,10},{10,... | collective-permute-start | bytes 196616 | tf_op jit(solution)/shard_map/ppermute | solution.py:17
  22.3 1.0 %collective-permute-start.3 = (bf16[1,64,512]{2,1,0:T(8,128)(2,1)S(1)}, bf16[1,64,512]{2,1,0:T(8,128)(2,1)S(1)}, u32[]{:S(2)}, u32[]{:S(2)}) collective-permute-start(bf16[1,64,512]{2,1,0:T(8,128)(2,1)S(1)} %get-tuple-element.43), channel_id=1, source_target_pairs={{0,2},{1,3},{2,0},{3,1},{4,6},{5,7},{6,4},{7,5},{8,10},{9,11},{10,... | collective-permute-start | bytes 196616 | tf_op jit(solution)/shard_map/ppermute | solution.py:17
  23.2 0.0 collective-permute-done.13.refs_7_
  23.2 0.5 %collective-permute-start.2 = (bf16[1,64,512]{2,1,0:T(8,128)(2,1)S(1)}, bf16[1,64,512]{2,1,0:T(8,128)(2,1)S(1)}, u32[]{:S(2)}, u32[]{:S(2)}) collective-permute-start(bf16[1,64,512]{2,1,0:T(8,128)(2,1)S(1)} %get-tuple-element.44), channel_id=1, source_target_pairs={{0,1},{1,0},{2,3},{3,2},{4,5},{5,4},{6,7},{7,6},{8,9},{9,8},{10,11... | collective-permute-start | bytes 196616 | tf_op jit(solution)/shard_map/ppermute | solution.py:17
  23.8 0.1 collective-permute-done.8.refs_5_
  23.9 2.3 %collective-permute-done.7.refs_4_ = bf16[1,64,512]{2,1,0:T(8,128)(2,1)S(1)} collective-permute-done((bf16[1,64,512]{2,1,0:T(8,128)(2,1)S(1)}, bf16[1,64,512]{2,1,0:T(8,128)(2,1)S(1)}, u32[]{:S(2)}, u32[]{:S(2)}) %collective-permute-start.7) | collective-permute-done | bytes 65568 | tf_op jit(solution)/shard_map/ppermute | solution.py:17
  26.2 0.0 collective-permute-done.4.refs_3_
  26.2 0.7 %collective-permute-done.3.refs_2_ = bf16[1,64,512]{2,1,0:T(8,128)(2,1)S(1)} collective-permute-done((bf16[1,64,512]{2,1,0:T(8,128)(2,1)S(1)}, bf16[1,64,512]{2,1,0:T(8,128)(2,1)S(1)}, u32[]{:S(2)}, u32[]{:S(2)}) %collective-permute-start.3) | collective-permute-done | bytes 65568 | tf_op jit(solution)/shard_map/ppermute | solution.py:17
  26.9 0.6 %collective-permute-done.2.refs_1_ = bf16[1,64,512]{2,1,0:T(8,128)(2,1)S(1)} collective-permute-done((bf16[1,64,512]{2,1,0:T(8,128)(2,1)S(1)}, bf16[1,64,512]{2,1,0:T(8,128)(2,1)S(1)}, u32[]{:S(2)}, u32[]{:S(2)}) %collective-permute-start.2) | collective-permute-done | bytes 65568 | tf_op jit(solution)/shard_map/ppermute | solution.py:17
  27.5 1.3 %precondition.1 = (bf16[1,64,512]{2,1,0:T(8,128)(2,1)S(1)}, bf16[1,64,512]{2,1,0:T(8,128)(2,1)S(1)}, bf16[1,64,512]{2,1,0:T(8,128)(2,1)S(1)}, bf16[1,64,512]{2,1...) custom-call(bf16[1,64,512]{2,1,0:T(8,128)(2,1)S(1)} %get-tuple-eleme, ...), custom_call_target="tpu_custom_call" | custom-call | flops 536870912 | bytes 3145728 | tf_op jit(solution)/shard_map/precondition/pallas_call | solution.py:101
  28.8 0.7 %collective-permute-start.14 = (bf16[1,64,512]{2,1,0:T(8,128)(2,1)S(1)}, bf16[1,64,512]{2,1,0:T(8,128)(2,1)S(1)}, u32[]{:S(2)}, u32[]{:S(2)}) collective-permute-start(bf16[1,64,512]{2,1,0:T(8,128)(2,1)S(1)} %get-tuple-element.29), channel_id=1, source_target_pairs={{0,1},{1,2},{2,3},{3,4},{4,5},{5,6},{6,7},{7,0},{8,9},{9,10},{10,1... | collective-permute-start | bytes 196616 | tf_op jit(solution)/shard_map/ppermute | solution.py:216
  29.5 1.0 %collective-permute-start.15 = (bf16[1,64,512]{2,1,0:T(8,128)(2,1)S(1)}, bf16[1,64,512]{2,1,0:T(8,128)(2,1)S(1)}, u32[]{:S(2)}, u32[]{:S(2)}) collective-permute-start(bf16[1,64,512]{2,1,0:T(8,128)(2,1)S(1)} %get-tuple-element.30), channel_id=1, source_target_pairs={{0,2},{1,3},{2,4},{3,5},{4,6},{5,7},{6,0},{7,1},{8,10},{9,11},{10,... | collective-permute-start | bytes 196616 | tf_op jit(solution)/shard_map/ppermute | solution.py:216
  30.5 4.1 %collective-permute-start.16 = (bf16[1,64,512]{2,1,0:T(8,128)(2,1)S(1)}, bf16[1,64,512]{2,1,0:T(8,128)(2,1)S(1)}, u32[]{:S(2)}, u32[]{:S(2)}) collective-permute-start(bf16[1,64,512]{2,1,0:T(8,128)(2,1)S(1)} %get-tuple-element.31), channel_id=1, source_target_pairs={{0,3},{1,4},{2,5},{3,6},{4,7},{5,0},{6,1},{7,2},{8,11},{9,12},{10,... | collective-permute-start | bytes 196616 | tf_op jit(solution)/shard_map/ppermute | solution.py:216
  34.5 0.7 %collective-permute-start.17 = (bf16[1,64,512]{2,1,0:T(8,128)(2,1)S(1)}, bf16[1,64,512]{2,1,0:T(8,128)(2,1)S(1)}, u32[]{:S(2)}, u32[]{:S(2)}) collective-permute-start(bf16[1,64,512]{2,1,0:T(8,128)(2,1)S(1)} %get-tuple-element.32), channel_id=1, source_target_pairs={{0,4},{1,5},{2,6},{3,7},{4,0},{5,1},{6,2},{7,3},{8,12},{9,13},{10,... | collective-permute-start | bytes 196616 | tf_op jit(solution)/shard_map/ppermute | solution.py:216
  35.2 2.2 %collective-permute-start.18 = (bf16[1,64,512]{2,1,0:T(8,128)(2,1)S(1)}, bf16[1,64,512]{2,1,0:T(8,128)(2,1)S(1)}, u32[]{:S(2)}, u32[]{:S(2)}) collective-permute-start(bf16[1,64,512]{2,1,0:T(8,128)(2,1)S(1)} %get-tuple-element.33), channel_id=1, source_target_pairs={{0,5},{1,6},{2,7},{3,0},{4,1},{5,2},{6,3},{7,4},{8,13},{9,14},{10,... | collective-permute-start | bytes 196616 | tf_op jit(solution)/shard_map/ppermute | solution.py:216
  37.4 1.0 %collective-permute-start.19 = (bf16[1,64,512]{2,1,0:T(8,128)(2,1)S(1)}, bf16[1,64,512]{2,1,0:T(8,128)(2,1)S(1)}, u32[]{:S(2)}, u32[]{:S(2)}) collective-permute-start(bf16[1,64,512]{2,1,0:T(8,128)(2,1)S(1)} %get-tuple-element.34), channel_id=1, source_target_pairs={{0,6},{1,7},{2,0},{3,1},{4,2},{5,3},{6,4},{7,5},{8,14},{9,15},{10,... | collective-permute-start | bytes 196616 | tf_op jit(solution)/shard_map/ppermute | solution.py:216
  38.4 0.0 collective-permute-done.15.refs_2_
  38.4 2.3 %collective-permute-start.20 = (bf16[1,64,512]{2,1,0:T(8,128)(2,1)S(1)}, bf16[1,64,512]{2,1,0:T(8,128)(2,1)S(1)}, u32[]{:S(2)}, u32[]{:S(2)}) collective-permute-start(bf16[1,64,512]{2,1,0:T(8,128)(2,1)S(1)} %get-tuple-element.35), channel_id=1, source_target_pairs={{0,7},{1,0},{2,1},{3,2},{4,3},{5,4},{6,5},{7,6},{8,15},{9,8},{10,9... | collective-permute-start | bytes 196616 | tf_op jit(solution)/shard_map/ppermute | solution.py:216
  40.8 2.1 %statistics.1 = (f32[1,512,512]{2,1,0:T(8,128)}, f32[1,512,512]{2,1,0:T(8,128)}, f32[1,512,512]{2,1,0:T(8,128)}) custom-call(bf16[512,512]{1,0:T(8,128)(2,1)S(1)} %get-tuple-element.36.block, f32[1,512,512]{2,1,0:T(8,128)S(1)} %copy-done.1, f32[1,512,512]{2,1,0:T(8,128)S(1)} %copy-done.2, f32[1,512,512]{2,1,0:T(8,128)S(1)} %copy-done), custom_call_target="tpu_custom_call" | custom-call | flops 536870912 | bytes 6815744 | tf_op jit(solution)/shard_map/statistics/pallas_call | solution.py:131
  42.9 0.0 collective-permute-done.16.refs_3_
  42.9 0.0 collective-permute-done.17.refs_4_
  43.0 0.0 collective-permute-done.18.refs_5_
  43.0 0.0 collective-permute-done.19.refs_6_
  43.0 0.8 %assemble.1 = bf16[2,64,2048]{2,1,0:T(8,128)(2,1)} custom-call(bf16[1,64,512]{2,1,0:T(8,128)(2,1)S(1)} %get-tuple-element.28.refs_0_, bf16[1,64,512]{2,1,0:T(8,128)(2,1)S(1)} %collective-permute-done.14.refs_1_, bf16[1,64,512]{2,1,0:T(8,128)(2,1)S(1)} %collective-permute-done.15.refs_2_, bf16[1,64,512]{2,1,0:T(8,128)(2,1)S(1)} %collective-permute-done.16.refs_3_, ...), custom_call_target="tpu_custom_call" | custom-call | bytes 1048576 | tf_op jit(solution)/shard_map/assemble/pallas_call | solution.py:164
  (22 shorter events, 0.3 us)
Async XLA Ops:
  2.3 1.7 %collective-permute-start.9 = (bf16[1,2,2,64,512]{4,3,1,2,0:T(8,128)(2,1)S(1)}, bf16[1,2,2,64,512]{4,3,1,2,0:T(8,128)(2,1)S(1)}, u32[]{:S(2)}, u32[]{:S(2)}) collective-permute-start(bf16[1,2,2,64,512]{4,3,1,2,0:T(8,128)(2,1)S(1)} %copy.13), channel_id=1, source_target_pairs={{0,8},{8,0},{16,24},{24,16},{1,9},{9,1},{17,25},{25,17},{2,10},{10... | collective-permute-start | bytes 786440 | tf_op jit(solution)/shard_map/ppermute | solution.py:17
  2.8 4.3 %collective-permute-start.5 = (bf16[1,2,2,64,512]{4,3,2,1,0:T(8,128)(2,1)S(1)}, bf16[1,2,2,64,512]{4,3,2,1,0:T(8,128)(2,1)S(1)}, u32[]{:S(2)}, u32[]{:S(2)}) collective-permute-start(bf16[1,2,2,64,512]{4,3,2,1,0:T(8,128)(2,1)S(1)} %get-tuple-element.24), channel_id=1, source_target_pairs={{0,8},{8,0},{16,24},{24,16},{1,9},{9,1},{17,25},{25,17},{2,10},{10... | collective-permute-start | bytes 786440 | tf_op jit(solution)/shard_map/ppermute | solution.py:17
  2.9 9.9 %collective-permute-start = (bf16[2,2,2,64,512]{4,3,2,0,1:T(8,128)(2,1)S(1)}, bf16[2,2,2,64,512]{4,3,2,0,1:T(8,128)(2,1)S(1)}, u32[]{:S(2)}, u32[]{:S(2)}) collective-permute-start(bf16[2,2,2,64,512]{4,3,2,0,1:T(8,128)(2,1)S(1)} %copy.10), channel_id=1, source_target_pairs={{0,8},{8,0},{16,24},{24,16},{1,9},{9,1},{17,25},{25,17},{2,10},{10... | collective-permute-start | bytes 1572872 | tf_op jit(solution)/shard_map/ppermute | solution.py:17
  4.1 5.4 %collective-permute-start.10 = (bf16[1,1,1,64,512]{4,3,2,1,0:T(8,128)(2,1)S(1)}, bf16[1,1,1,64,512]{4,3,2,1,0:T(8,128)(2,1)S(1)}, u32[]{:S(2)}, u32[]{:S(2)}) collective-permute-start(bf16[1,1,1,64,512]{4,3,2,1,0:T(8,128)(2,1)S(1)} %fusion.12), channel_id=1, source_target_pairs={{0,16},{8,24},{16,0},{24,8},{1,17},{9,25},{17,1},{25,9},{2,18},{10... | collective-permute-start | bytes 196616 | tf_op jit(solution)/shard_map/ppermute | solution.py:17
  7.0 7.8 %collective-permute-start.12 = (bf16[1,1,1,64,512]{4,3,2,1,0:T(8,128)(2,1)S(1)}, bf16[1,1,1,64,512]{4,3,2,1,0:T(8,128)(2,1)S(1)}, u32[]{:S(2)}, u32[]{:S(2)}) collective-permute-start(bf16[1,1,1,64,512]{4,3,2,1,0:T(8,128)(2,1)S(1)} %get-tuple-element.50), channel_id=1, source_target_pairs={{0,16},{8,24},{16,0},{24,8},{1,17},{9,25},{17,1},{25,9},{2,18},{10... | collective-permute-start | bytes 196616 | tf_op jit(solution)/shard_map/ppermute | solution.py:17
  7.2 20.3 %copy-start = (f32[1,512,512]{2,1,0:T(8,128)S(1)}, f32[1,512,512]{2,1,0:T(8,128)}, u32[]{:S(2)}) copy-start(f32[1,512,512]{2,1,0:T(8,128)} %accum.1) | copy-start | bytes 3145732
  7.2 20.3 %copy-start.3 = (bf16[1,512,512]{2,1,0:T(8,128)(2,1)S(1)}, bf16[1,512,512]{2,1,0:T(8,128)(2,1)}, u32[]{:S(2)}) copy-start(bf16[1,512,512]{2,1,0:T(8,128)(2,1)} %refs_8_.1) | copy-start | bytes 1572868
  7.2 20.3 %copy-start.4 = (bf16[1,512,512]{2,1,0:T(8,128)(2,1)S(1)}, bf16[1,512,512]{2,1,0:T(8,128)(2,1)}, u32[]{:S(2)}) copy-start(bf16[1,512,512]{2,1,0:T(8,128)(2,1)} %refs_9_.1) | copy-start | bytes 1572868
  7.2 9.0 %collective-permute-start.6 = (bf16[1,1,2,64,512]{4,3,2,1,0:T(8,128)(2,1)S(1)}, bf16[1,1,2,64,512]{4,3,2,1,0:T(8,128)(2,1)S(1)}, u32[]{:S(2)}, u32[]{:S(2)}) collective-permute-start(bf16[1,1,2,64,512]{4,3,2,1,0:T(8,128)(2,1)S(1)} %get-tuple-element.46), channel_id=1, source_target_pairs={{0,16},{8,24},{16,0},{24,8},{1,17},{9,25},{17,1},{25,9},{2,18},{10... | collective-permute-start | bytes 393224 | tf_op jit(solution)/shard_map/ppermute | solution.py:17
  9.5 12.8 %collective-permute-start.11 = (bf16[1,64,512]{2,1,0:T(8,128)(2,1)S(1)}, bf16[1,64,512]{2,1,0:T(8,128)(2,1)S(1)}, u32[]{:S(2)}, u32[]{:S(2)}) collective-permute-start(bf16[1,64,512]{2,1,0:T(8,128)(2,1)S(1)} %fusion.9), channel_id=1, source_target_pairs={{0,4},{1,5},{2,6},{3,7},{4,0},{5,1},{6,2},{7,3},{8,12},{9,13},{10,... | collective-permute-start | bytes 196616 | tf_op jit(solution)/shard_map/ppermute | solution.py:17
  13.0 7.1 %collective-permute-start.1 = (bf16[2,1,2,64,512]{4,3,2,1,0:T(8,128)(2,1)S(1)}, bf16[2,1,2,64,512]{4,3,2,1,0:T(8,128)(2,1)S(1)}, u32[]{:S(2)}, u32[]{:S(2)}) collective-permute-start(bf16[2,1,2,64,512]{4,3,2,1,0:T(8,128)(2,1)S(1)} %get-tuple-element.40), channel_id=1, source_target_pairs={{0,16},{8,24},{16,0},{24,8},{1,17},{9,25},{17,1},{25,9},{2,18},{10... | collective-permute-start | bytes 786440 | tf_op jit(solution)/shard_map/ppermute | solution.py:17
  14.9 25.9 %copy-start.1 = (f32[1,512,512]{2,1,0:T(8,128)S(1)}, f32[1,512,512]{2,1,0:T(8,128)}, u32[]{:S(2)}) copy-start(f32[1,512,512]{2,1,0:T(8,128)} %left.1) | copy-start | bytes 3145732
  14.9 25.9 %copy-start.2 = (f32[1,512,512]{2,1,0:T(8,128)S(1)}, f32[1,512,512]{2,1,0:T(8,128)}, u32[]{:S(2)}) copy-start(f32[1,512,512]{2,1,0:T(8,128)} %right.1) | copy-start | bytes 3145732
  14.9 8.3 %collective-permute-start.13 = (bf16[1,64,512]{2,1,0:T(8,128)(2,1)S(1)}, bf16[1,64,512]{2,1,0:T(8,128)(2,1)S(1)}, u32[]{:S(2)}, u32[]{:S(2)}) collective-permute-start(bf16[1,64,512]{2,1,0:T(8,128)(2,1)S(1)} %fusion.11), channel_id=1, source_target_pairs={{0,5},{1,4},{2,7},{3,6},{4,1},{5,0},{6,3},{7,2},{8,13},{9,12},{10,... | collective-permute-start | bytes 196616 | tf_op jit(solution)/shard_map/ppermute | solution.py:17
  16.3 7.6 %collective-permute-start.8 = (bf16[1,64,512]{2,1,0:T(8,128)(2,1)S(1)}, bf16[1,64,512]{2,1,0:T(8,128)(2,1)S(1)}, u32[]{:S(2)}, u32[]{:S(2)}) collective-permute-start(bf16[1,64,512]{2,1,0:T(8,128)(2,1)S(1)} %get-tuple-element.48), channel_id=1, source_target_pairs={{0,7},{1,6},{2,5},{3,4},{4,3},{5,2},{6,1},{7,0},{8,15},{9,14},{10,... | collective-permute-start | bytes 196616 | tf_op jit(solution)/shard_map/ppermute | solution.py:17
  19.9 6.2 %collective-permute-start.7 = (bf16[1,64,512]{2,1,0:T(8,128)(2,1)S(1)}, bf16[1,64,512]{2,1,0:T(8,128)(2,1)S(1)}, u32[]{:S(2)}, u32[]{:S(2)}) collective-permute-start(bf16[1,64,512]{2,1,0:T(8,128)(2,1)S(1)} %get-tuple-element.49), channel_id=1, source_target_pairs={{0,6},{1,7},{2,4},{3,5},{4,2},{5,3},{6,0},{7,1},{8,14},{9,15},{10,... | collective-permute-start | bytes 196616 | tf_op jit(solution)/shard_map/ppermute | solution.py:17
  20.2 6.0 %collective-permute-start.4 = (bf16[1,64,512]{2,1,0:T(8,128)(2,1)S(1)}, bf16[1,64,512]{2,1,0:T(8,128)(2,1)S(1)}, u32[]{:S(2)}, u32[]{:S(2)}) collective-permute-start(bf16[1,64,512]{2,1,0:T(8,128)(2,1)S(1)} %get-tuple-element.42), channel_id=1, source_target_pairs={{0,3},{1,2},{2,1},{3,0},{4,7},{5,6},{6,5},{7,4},{8,11},{9,10},{10,... | collective-permute-start | bytes 196616 | tf_op jit(solution)/shard_map/ppermute | solution.py:17
  22.3 4.6 %collective-permute-start.3 = (bf16[1,64,512]{2,1,0:T(8,128)(2,1)S(1)}, bf16[1,64,512]{2,1,0:T(8,128)(2,1)S(1)}, u32[]{:S(2)}, u32[]{:S(2)}) collective-permute-start(bf16[1,64,512]{2,1,0:T(8,128)(2,1)S(1)} %get-tuple-element.43), channel_id=1, source_target_pairs={{0,2},{1,3},{2,0},{3,1},{4,6},{5,7},{6,4},{7,5},{8,10},{9,11},{10,... | collective-permute-start | bytes 196616 | tf_op jit(solution)/shard_map/ppermute | solution.py:17
  23.2 4.3 %collective-permute-start.2 = (bf16[1,64,512]{2,1,0:T(8,128)(2,1)S(1)}, bf16[1,64,512]{2,1,0:T(8,128)(2,1)S(1)}, u32[]{:S(2)}, u32[]{:S(2)}) collective-permute-start(bf16[1,64,512]{2,1,0:T(8,128)(2,1)S(1)} %get-tuple-element.44), channel_id=1, source_target_pairs={{0,1},{1,0},{2,3},{3,2},{4,5},{5,4},{6,7},{7,6},{8,9},{9,8},{10,11... | collective-permute-start | bytes 196616 | tf_op jit(solution)/shard_map/ppermute | solution.py:17
  28.8 8.6 %collective-permute-start.14 = (bf16[1,64,512]{2,1,0:T(8,128)(2,1)S(1)}, bf16[1,64,512]{2,1,0:T(8,128)(2,1)S(1)}, u32[]{:S(2)}, u32[]{:S(2)}) collective-permute-start(bf16[1,64,512]{2,1,0:T(8,128)(2,1)S(1)} %get-tuple-element.29), channel_id=1, source_target_pairs={{0,1},{1,2},{2,3},{3,4},{4,5},{5,6},{6,7},{7,0},{8,9},{9,10},{10,1... | collective-permute-start | bytes 196616 | tf_op jit(solution)/shard_map/ppermute | solution.py:216
  29.5 8.9 %collective-permute-start.15 = (bf16[1,64,512]{2,1,0:T(8,128)(2,1)S(1)}, bf16[1,64,512]{2,1,0:T(8,128)(2,1)S(1)}, u32[]{:S(2)}, u32[]{:S(2)}) collective-permute-start(bf16[1,64,512]{2,1,0:T(8,128)(2,1)S(1)} %get-tuple-element.30), channel_id=1, source_target_pairs={{0,2},{1,3},{2,4},{3,5},{4,6},{5,7},{6,0},{7,1},{8,10},{9,11},{10,... | collective-permute-start | bytes 196616 | tf_op jit(solution)/shard_map/ppermute | solution.py:216
  30.5 12.5 %collective-permute-start.16 = (bf16[1,64,512]{2,1,0:T(8,128)(2,1)S(1)}, bf16[1,64,512]{2,1,0:T(8,128)(2,1)S(1)}, u32[]{:S(2)}, u32[]{:S(2)}) collective-permute-start(bf16[1,64,512]{2,1,0:T(8,128)(2,1)S(1)} %get-tuple-element.31), channel_id=1, source_target_pairs={{0,3},{1,4},{2,5},{3,6},{4,7},{5,0},{6,1},{7,2},{8,11},{9,12},{10,... | collective-permute-start | bytes 196616 | tf_op jit(solution)/shard_map/ppermute | solution.py:216
  34.5 8.4 %collective-permute-start.17 = (bf16[1,64,512]{2,1,0:T(8,128)(2,1)S(1)}, bf16[1,64,512]{2,1,0:T(8,128)(2,1)S(1)}, u32[]{:S(2)}, u32[]{:S(2)}) collective-permute-start(bf16[1,64,512]{2,1,0:T(8,128)(2,1)S(1)} %get-tuple-element.32), channel_id=1, source_target_pairs={{0,4},{1,5},{2,6},{3,7},{4,0},{5,1},{6,2},{7,3},{8,12},{9,13},{10,... | collective-permute-start | bytes 196616 | tf_op jit(solution)/shard_map/ppermute | solution.py:216
  35.2 7.7 %collective-permute-start.18 = (bf16[1,64,512]{2,1,0:T(8,128)(2,1)S(1)}, bf16[1,64,512]{2,1,0:T(8,128)(2,1)S(1)}, u32[]{:S(2)}, u32[]{:S(2)}) collective-permute-start(bf16[1,64,512]{2,1,0:T(8,128)(2,1)S(1)} %get-tuple-element.33), channel_id=1, source_target_pairs={{0,5},{1,6},{2,7},{3,0},{4,1},{5,2},{6,3},{7,4},{8,13},{9,14},{10,... | collective-permute-start | bytes 196616 | tf_op jit(solution)/shard_map/ppermute | solution.py:216
  37.4 5.5 %collective-permute-start.19 = (bf16[1,64,512]{2,1,0:T(8,128)(2,1)S(1)}, bf16[1,64,512]{2,1,0:T(8,128)(2,1)S(1)}, u32[]{:S(2)}, u32[]{:S(2)}) collective-permute-start(bf16[1,64,512]{2,1,0:T(8,128)(2,1)S(1)} %get-tuple-element.34), channel_id=1, source_target_pairs={{0,6},{1,7},{2,0},{3,1},{4,2},{5,3},{6,4},{7,5},{8,14},{9,15},{10,... | collective-permute-start | bytes 196616 | tf_op jit(solution)/shard_map/ppermute | solution.py:216
  38.4 4.5 %collective-permute-start.20 = (bf16[1,64,512]{2,1,0:T(8,128)(2,1)S(1)}, bf16[1,64,512]{2,1,0:T(8,128)(2,1)S(1)}, u32[]{:S(2)}, u32[]{:S(2)}) collective-permute-start(bf16[1,64,512]{2,1,0:T(8,128)(2,1)S(1)} %get-tuple-element.35), channel_id=1, source_target_pairs={{0,7},{1,0},{2,1},{3,2},{4,3},{5,4},{6,5},{7,6},{8,15},{9,8},{10,9... | collective-permute-start | bytes 196616 | tf_op jit(solution)/shard_map/ppermute | solution.py:216

commit v7 on v6

--- a/solution.py
+++ b/solution.py
@@ -113,16 +113,23 @@
     return outs[:-1], outs[-1]
 
 
-def stats_kernel(block, left, right, accum, left_out, right_out, accum_out):
+def stats_kernel(block, left, right, accum, *refs):
+    outs, news, sems = refs[:3], refs[3:6], refs[6]
+    copies = [pltpu.make_async_copy(news[i], outs[i].at[0], sems.at[i]) for i in range(3)]
     b = block[...]
     wide = b.astype(jnp.float32)
-    accum_out[0] = accum[0] + wide * wide
-    left_out[0] = left[0] + lax.dot_general(
+    news[2][...] = accum[0] + wide * wide
+    copies[2].start()
+    news[0][...] = left[0] + lax.dot_general(
         b, b, (((1,), (1,)), ((), ())), preferred_element_type=jnp.float32
     )
-    right_out[0] = right[0] + lax.dot_general(
+    copies[0].start()
+    news[1][...] = right[0] + lax.dot_general(
         b, b, (((0,), (0,)), ((), ())), preferred_element_type=jnp.float32
     )
+    copies[1].start()
+    for copy in copies:
+        copy.wait()
 
 
 def statistics(block, left, right, accum):
@@ -132,7 +139,9 @@
         stats_kernel,
         out_shape=(shape,) * 3,
         in_specs=[VMEM] * 4,
-        out_specs=(VMEM,) * 3,
+        out_specs=(ANY,) * 3,
+        scratch_shapes=[pltpu.VMEM((side, side), jnp.float32)] * 3
+        + [pltpu.SemaphoreType.DMA((3,))],
         compiler_params=pltpu.CompilerParams(vmem_limit_bytes=20 * MIB),
         cost_estimate=pl.CostEstimate(
             flops=4 * side**3, bytes_accessed=26 * side * side, transcendentals=0

time: 44 us -> 43.7 us (level)
  transfers between devices with their start and end apart: 21 -> 21, of which waited for: 6 -> 6; matrix products, arithmetic and copies ran while one was open for 1% -> 1% of each run, Pallas kernels for 5% -> 4%
where the time goes in v7:
time: 43.7 us; the launch traced here: 43.5 us
  starting transfers between devices  32 us (73%)
  Pallas kernels  5.58 us (13%)
  waiting for transfers between devices  4.54 us (10%)
  between operations  0.83 us (2%)
    ppermute x14, starting transfers between devices, swap(): return lax.ppermute(x, axis, [(i, i ^ bit) for i in range(n)])  20.1 us
    ppermute x7, starting transfers between devices, body(): lax.ppermute(a, 'fsdp', [(i, (i + d) % fsdp_count) for i in range(fsdp_co...  11.9 us
    ppermute x14, waiting for transfers between devices, swap(): return lax.ppermute(x, axis, [(i, i ^ bit) for i in range(n)])  4.51 us
    pallas_call x1, Pallas kernels, statistics(): pl.pallas_call(stats_kernel, out_shape=(shape,) * 3, in_specs=[VMEM] * 4,...  1.85 us
    pallas_call x1, Pallas kernels, pick(): pl.pallas_call(functools.partial(pick_kernel, groups), out_shape=shapes *...  1.61 us
    pallas_call x1, Pallas kernels, precondition(): pl.pallas_call(functools.partial(main_kernel, spots), out_shape=[piece] *...  1.31 us
  transfers between devices with their start and end apart: 21, of which 6 were waited for; matrix products, arithmetic and copies ran while one was open for 1% of the time, Pallas kernels for 4%

profile of v7, /device:TPU:0, one launch (start us, length us, event | category | flops | bytes accessed | tf_op | source)
XLA Modules:
  0.0 43.5 jit_solution(11107604643975470482)
XLA Ops:
  0.6 1.6 %pick.1 = (bf16[2,2,2,64,512]{4,3,2,1,0:T(8,128)(2,1)S(1)}, bf16[1,2,2,64,512]{4,3,2,1,0:T(8,128)(2,1)S(1)}, bf16[1,2,2,64,512]{4,3,2,1,0:T(8,128)(2,1)S(1)}, bf...) custom-call(bf16[1,2,64,8192]{3,2,1,0:T(8,128)(2,1)} %grads.1), custom_call_target="tpu_custom_call" | custom-call | bytes 4194304 | tf_op jit(solution)/shard_map/pick/pallas_call | solution.py:61
  2.3 0.5 %collective-permute-start.9 = (bf16[1,2,2,64,512]{4,3,1,2,0:T(8,128)(2,1)S(1)}, bf16[1,2,2,64,512]{4,3,1,2,0:T(8,128)(2,1)S(1)}, u32[]{:S(2)}, u32[]{:S(2)}) collective-permute-start(bf16[1,2,2,64,512]{4,3,1,2,0:T(8,128)(2,1)S(1)} %copy.13), channel_id=1, source_target_pairs={{0,8},{8,0},{16,24},{24,16},{1,9},{9,1},{17,25},{25,17},{2,10},{10... | collective-permute-start | bytes 786440 | tf_op jit(solution)/shard_map/ppermute | solution.py:17
  2.8 0.1 collective-permute-start.5
  2.9 0.5 %collective-permute-start = (bf16[2,2,2,64,512]{4,3,2,0,1:T(8,128)(2,1)S(1)}, bf16[2,2,2,64,512]{4,3,2,0,1:T(8,128)(2,1)S(1)}, u32[]{:S(2)}, u32[]{:S(2)}) collective-permute-start(bf16[2,2,2,64,512]{4,3,2,0,1:T(8,128)(2,1)S(1)} %copy.10), channel_id=1, source_target_pairs={{0,8},{8,0},{16,24},{24,16},{1,9},{9,1},{17,25},{25,17},{2,10},{10... | collective-permute-start | bytes 1572872 | tf_op jit(solution)/shard_map/ppermute | solution.py:17
  3.5 0.5 %collective-permute-done.9 = bf16[1,2,2,64,512]{4,3,1,2,0:T(8,128)(2,1)S(1)} collective-permute-done((bf16[1,2,2,64,512]{4,3,1,2,0:T(8,128)(2,1)S(1)}, bf16[1,2,2,64,512]{4,3,1,2,0:T(8,128)(2,1)S(1)}, u32[]{:S(2)}, u32[]{:S(2)}) %collective-permute-start.9) | collective-permute-done | bytes 262176 | tf_op jit(solution)/shard_map/ppermute | solution.py:17
  4.1 3.0 %collective-permute-start.10 = (bf16[1,1,1,64,512]{4,3,2,1,0:T(8,128)(2,1)S(1)}, bf16[1,1,1,64,512]{4,3,2,1,0:T(8,128)(2,1)S(1)}, u32[]{:S(2)}, u32[]{:S(2)}) collective-permute-start(bf16[1,1,1,64,512]{4,3,2,1,0:T(8,128)(2,1)S(1)} %fusion.12), channel_id=1, source_target_pairs={{0,16},{8,24},{16,0},{24,8},{1,17},{9,25},{17,1},{25,9},{2,18},{10... | collective-permute-start | bytes 196616 | tf_op jit(solution)/shard_map/ppermute | solution.py:17
  7.0 0.1 collective-permute-start.12
  7.1 0.0 collective-permute-done.5
  7.1 0.1 fusion.1
  7.2 0.0 copy-start
  7.2 0.0 copy-start.3
  7.2 0.0 copy-start.4
  7.2 2.0 %collective-permute-start.6 = (bf16[1,1,2,64,512]{4,3,2,1,0:T(8,128)(2,1)S(1)}, bf16[1,1,2,64,512]{4,3,2,1,0:T(8,128)(2,1)S(1)}, u32[]{:S(2)}, u32[]{:S(2)}) collective-permute-start(bf16[1,1,2,64,512]{4,3,2,1,0:T(8,128)(2,1)S(1)} %get-tuple-element.46), channel_id=1, source_target_pairs={{0,16},{8,24},{16,0},{24,8},{1,17},{9,25},{17,1},{25,9},{2,18},{10... | collective-permute-start | bytes 393224 | tf_op jit(solution)/shard_map/ppermute | solution.py:17
  9.2 0.3 collective-permute-done.10
  9.5 3.3 %collective-permute-start.11 = (bf16[1,64,512]{2,1,0:T(8,128)(2,1)S(1)}, bf16[1,64,512]{2,1,0:T(8,128)(2,1)S(1)}, u32[]{:S(2)}, u32[]{:S(2)}) collective-permute-start(bf16[1,64,512]{2,1,0:T(8,128)(2,1)S(1)} %fusion.9), channel_id=1, source_target_pairs={{0,4},{1,5},{2,6},{3,7},{4,0},{5,1},{6,2},{7,3},{8,12},{9,13},{10,... | collective-permute-start | bytes 196616 | tf_op jit(solution)/shard_map/ppermute | solution.py:17
  12.8 0.1 fusion
  13.0 1.9 %collective-permute-start.1 = (bf16[2,1,2,64,512]{4,3,2,1,0:T(8,128)(2,1)S(1)}, bf16[2,1,2,64,512]{4,3,2,1,0:T(8,128)(2,1)S(1)}, u32[]{:S(2)}, u32[]{:S(2)}) collective-permute-start(bf16[2,1,2,64,512]{4,3,2,1,0:T(8,128)(2,1)S(1)} %get-tuple-element.40), channel_id=1, source_target_pairs={{0,16},{8,24},{16,0},{24,8},{1,17},{9,25},{17,1},{25,9},{2,18},{10... | collective-permute-start | bytes 786440 | tf_op jit(solution)/shard_map/ppermute | solution.py:17
  14.9 0.0 copy-start.1
  14.9 0.0 copy-start.2
  14.9 1.3 %collective-permute-start.13 = (bf16[1,64,512]{2,1,0:T(8,128)(2,1)S(1)}, bf16[1,64,512]{2,1,0:T(8,128)(2,1)S(1)}, u32[]{:S(2)}, u32[]{:S(2)}) collective-permute-start(bf16[1,64,512]{2,1,0:T(8,128)(2,1)S(1)} %fusion.11), channel_id=1, source_target_pairs={{0,5},{1,4},{2,7},{3,6},{4,1},{5,0},{6,3},{7,2},{8,13},{9,12},{10,... | collective-permute-start | bytes 196616 | tf_op jit(solution)/shard_map/ppermute | solution.py:17
  16.2 0.0 collective-permute-done.6
  16.3 3.6 %collective-permute-start.8 = (bf16[1,64,512]{2,1,0:T(8,128)(2,1)S(1)}, bf16[1,64,512]{2,1,0:T(8,128)(2,1)S(1)}, u32[]{:S(2)}, u32[]{:S(2)}) collective-permute-start(bf16[1,64,512]{2,1,0:T(8,128)(2,1)S(1)} %get-tuple-element.48), channel_id=1, source_target_pairs={{0,7},{1,6},{2,5},{3,4},{4,3},{5,2},{6,1},{7,0},{8,15},{9,14},{10,... | collective-permute-start | bytes 196616 | tf_op jit(solution)/shard_map/ppermute | solution.py:17
  19.9 0.2 collective-permute-start.7
  20.1 0.1 fusion.16
  20.2 2.1 %collective-permute-start.4 = (bf16[1,64,512]{2,1,0:T(8,128)(2,1)S(1)}, bf16[1,64,512]{2,1,0:T(8,128)(2,1)S(1)}, u32[]{:S(2)}, u32[]{:S(2)}) collective-permute-start(bf16[1,64,512]{2,1,0:T(8,128)(2,1)S(1)} %get-tuple-element.42), channel_id=1, source_target_pairs={{0,3},{1,2},{2,1},{3,0},{4,7},{5,6},{6,5},{7,4},{8,11},{9,10},{10,... | collective-permute-start | bytes 196616 | tf_op jit(solution)/shard_map/ppermute | solution.py:17
  22.3 1.0 %collective-permute-start.3 = (bf16[1,64,512]{2,1,0:T(8,128)(2,1)S(1)}, bf16[1,64,512]{2,1,0:T(8,128)(2,1)S(1)}, u32[]{:S(2)}, u32[]{:S(2)}) collective-permute-start(bf16[1,64,512]{2,1,0:T(8,128)(2,1)S(1)} %get-tuple-element.43), channel_id=1, source_target_pairs={{0,2},{1,3},{2,0},{3,1},{4,6},{5,7},{6,4},{7,5},{8,10},{9,11},{10,... | collective-permute-start | bytes 196616 | tf_op jit(solution)/shard_map/ppermute | solution.py:17
  23.2 0.0 collective-permute-done.13.refs_7_
  23.2 0.5 %collective-permute-start.2 = (bf16[1,64,512]{2,1,0:T(8,128)(2,1)S(1)}, bf16[1,64,512]{2,1,0:T(8,128)(2,1)S(1)}, u32[]{:S(2)}, u32[]{:S(2)}) collective-permute-start(bf16[1,64,512]{2,1,0:T(8,128)(2,1)S(1)} %get-tuple-element.44), channel_id=1, source_target_pairs={{0,1},{1,0},{2,3},{3,2},{4,5},{5,4},{6,7},{7,6},{8,9},{9,8},{10,11... | collective-permute-start | bytes 196616 | tf_op jit(solution)/shard_map/ppermute | solution.py:17
  23.8 0.1 collective-permute-done.8.refs_5_
  23.9 2.3 %collective-permute-done.7.refs_4_ = bf16[1,64,512]{2,1,0:T(8,128)(2,1)S(1)} collective-permute-done((bf16[1,64,512]{2,1,0:T(8,128)(2,1)S(1)}, bf16[1,64,512]{2,1,0:T(8,128)(2,1)S(1)}, u32[]{:S(2)}, u32[]{:S(2)}) %collective-permute-start.7) | collective-permute-done | bytes 65568 | tf_op jit(solution)/shard_map/ppermute | solution.py:17
  26.2 0.0 collective-permute-done.4.refs_3_
  26.2 0.7 %collective-permute-done.3.refs_2_ = bf16[1,64,512]{2,1,0:T(8,128)(2,1)S(1)} collective-permute-done((bf16[1,64,512]{2,1,0:T(8,128)(2,1)S(1)}, bf16[1,64,512]{2,1,0:T(8,128)(2,1)S(1)}, u32[]{:S(2)}, u32[]{:S(2)}) %collective-permute-start.3) | collective-permute-done | bytes 65568 | tf_op jit(solution)/shard_map/ppermute | solution.py:17
  26.9 0.6 %collective-permute-done.2.refs_1_ = bf16[1,64,512]{2,1,0:T(8,128)(2,1)S(1)} collective-permute-done((bf16[1,64,512]{2,1,0:T(8,128)(2,1)S(1)}, bf16[1,64,512]{2,1,0:T(8,128)(2,1)S(1)}, u32[]{:S(2)}, u32[]{:S(2)}) %collective-permute-start.2) | collective-permute-done | bytes 65568 | tf_op jit(solution)/shard_map/ppermute | solution.py:17
  27.5 1.3 %precondition.1 = (bf16[1,64,512]{2,1,0:T(8,128)(2,1)S(1)}, bf16[1,64,512]{2,1,0:T(8,128)(2,1)S(1)}, bf16[1,64,512]{2,1,0:T(8,128)(2,1)S(1)}, bf16[1,64,512]{2,1...) custom-call(bf16[1,64,512]{2,1,0:T(8,128)(2,1)S(1)} %get-tuple-eleme, ...), custom_call_target="tpu_custom_call" | custom-call | flops 536870912 | bytes 3145728 | tf_op jit(solution)/shard_map/precondition/pallas_call | solution.py:101
  28.8 0.7 %collective-permute-start.14 = (bf16[1,64,512]{2,1,0:T(8,128)(2,1)S(1)}, bf16[1,64,512]{2,1,0:T(8,128)(2,1)S(1)}, u32[]{:S(2)}, u32[]{:S(2)}) collective-permute-start(bf16[1,64,512]{2,1,0:T(8,128)(2,1)S(1)} %get-tuple-element.29), channel_id=1, source_target_pairs={{0,1},{1,2},{2,3},{3,4},{4,5},{5,6},{6,7},{7,0},{8,9},{9,10},{10,1... | collective-permute-start | bytes 196616 | tf_op jit(solution)/shard_map/ppermute | solution.py:225
  29.5 1.0 %collective-permute-start.15 = (bf16[1,64,512]{2,1,0:T(8,128)(2,1)S(1)}, bf16[1,64,512]{2,1,0:T(8,128)(2,1)S(1)}, u32[]{:S(2)}, u32[]{:S(2)}) collective-permute-start(bf16[1,64,512]{2,1,0:T(8,128)(2,1)S(1)} %get-tuple-element.30), channel_id=1, source_target_pairs={{0,2},{1,3},{2,4},{3,5},{4,6},{5,7},{6,0},{7,1},{8,10},{9,11},{10,... | collective-permute-start | bytes 196616 | tf_op jit(solution)/shard_map/ppermute | solution.py:225
  30.5 4.1 %collective-permute-start.16 = (bf16[1,64,512]{2,1,0:T(8,128)(2,1)S(1)}, bf16[1,64,512]{2,1,0:T(8,128)(2,1)S(1)}, u32[]{:S(2)}, u32[]{:S(2)}) collective-permute-start(bf16[1,64,512]{2,1,0:T(8,128)(2,1)S(1)} %get-tuple-element.31), channel_id=1, source_target_pairs={{0,3},{1,4},{2,5},{3,6},{4,7},{5,0},{6,1},{7,2},{8,11},{9,12},{10,... | collective-permute-start | bytes 196616 | tf_op jit(solution)/shard_map/ppermute | solution.py:225
  34.5 0.7 %collective-permute-start.17 = (bf16[1,64,512]{2,1,0:T(8,128)(2,1)S(1)}, bf16[1,64,512]{2,1,0:T(8,128)(2,1)S(1)}, u32[]{:S(2)}, u32[]{:S(2)}) collective-permute-start(bf16[1,64,512]{2,1,0:T(8,128)(2,1)S(1)} %get-tuple-element.32), channel_id=1, source_target_pairs={{0,4},{1,5},{2,6},{3,7},{4,0},{5,1},{6,2},{7,3},{8,12},{9,13},{10,... | collective-permute-start | bytes 196616 | tf_op jit(solution)/shard_map/ppermute | solution.py:225
  35.2 2.2 %collective-permute-start.18 = (bf16[1,64,512]{2,1,0:T(8,128)(2,1)S(1)}, bf16[1,64,512]{2,1,0:T(8,128)(2,1)S(1)}, u32[]{:S(2)}, u32[]{:S(2)}) collective-permute-start(bf16[1,64,512]{2,1,0:T(8,128)(2,1)S(1)} %get-tuple-element.33), channel_id=1, source_target_pairs={{0,5},{1,6},{2,7},{3,0},{4,1},{5,2},{6,3},{7,4},{8,13},{9,14},{10,... | collective-permute-start | bytes 196616 | tf_op jit(solution)/shard_map/ppermute | solution.py:225
  37.4 1.0 %collective-permute-start.19 = (bf16[1,64,512]{2,1,0:T(8,128)(2,1)S(1)}, bf16[1,64,512]{2,1,0:T(8,128)(2,1)S(1)}, u32[]{:S(2)}, u32[]{:S(2)}) collective-permute-start(bf16[1,64,512]{2,1,0:T(8,128)(2,1)S(1)} %get-tuple-element.34), channel_id=1, source_target_pairs={{0,6},{1,7},{2,0},{3,1},{4,2},{5,3},{6,4},{7,5},{8,14},{9,15},{10,... | collective-permute-start | bytes 196616 | tf_op jit(solution)/shard_map/ppermute | solution.py:225
  38.4 0.0 collective-permute-done.15.refs_2_
  38.4 2.3 %collective-permute-start.20 = (bf16[1,64,512]{2,1,0:T(8,128)(2,1)S(1)}, bf16[1,64,512]{2,1,0:T(8,128)(2,1)S(1)}, u32[]{:S(2)}, u32[]{:S(2)}) collective-permute-start(bf16[1,64,512]{2,1,0:T(8,128)(2,1)S(1)} %get-tuple-element.35), channel_id=1, source_target_pairs={{0,7},{1,0},{2,1},{3,2},{4,3},{5,4},{6,5},{7,6},{8,15},{9,8},{10,9... | collective-permute-start | bytes 196616 | tf_op jit(solution)/shard_map/ppermute | solution.py:225
  40.8 1.9 %statistics.1 = (f32[1,512,512]{2,1,0:T(8,128)}, f32[1,512,512]{2,1,0:T(8,128)}, f32[1,512,512]{2,1,0:T(8,128)}) custom-call(bf16[512,512]{1,0:T(8,128)(2,1)S(1)} %get-tuple-element.36.block, f32[1,512,512]{2,1,0:T(8,128)S(1)} %copy-done.1, f32[1,512,512]{2,1,0:T(8,128)S(1)} %copy-done.2, f32[1,512,512]{2,1,0:T(8,128)S(1)} %copy-done), custom_call_target="tpu_custom_call" | custom-call | flops 536870912 | bytes 6815744 | tf_op jit(solution)/shard_map/statistics/pallas_call | solution.py:138
  42.7 0.0 collective-permute-done.16.refs_3_
  42.7 0.0 collective-permute-done.18.refs_5_
  42.7 0.0 collective-permute-done.19.refs_6_
  42.7 0.0 collective-permute-done.20.refs_7_
  42.7 0.8 %assemble.1 = bf16[2,64,2048]{2,1,0:T(8,128)(2,1)} custom-call(bf16[1,64,512]{2,1,0:T(8,128)(2,1)S(1)} %get-tuple-element.28.refs_0_, bf16[1,64,512]{2,1,0:T(8,128)(2,1)S(1)} %collective-permute-done.14.refs_1_, bf16[1,64,512]{2,1,0:T(8,128)(2,1)S(1)} %collective-permute-done.15.refs_2_, bf16[1,64,512]{2,1,0:T(8,128)(2,1)S(1)} %collective-permute-done.16.refs_3_, ...), custom_call_target="tpu_custom_call" | custom-call | bytes 1048576 | tf_op jit(solution)/shard_map/assemble/pallas_call | solution.py:173
  (22 shorter events, 0.3 us)
Async XLA Ops:
  2.3 1.7 %collective-permute-start.9 = (bf16[1,2,2,64,512]{4,3,1,2,0:T(8,128)(2,1)S(1)}, bf16[1,2,2,64,512]{4,3,1,2,0:T(8,128)(2,1)S(1)}, u32[]{:S(2)}, u32[]{:S(2)}) collective-permute-start(bf16[1,2,2,64,512]{4,3,1,2,0:T(8,128)(2,1)S(1)} %copy.13), channel_id=1, source_target_pairs={{0,8},{8,0},{16,24},{24,16},{1,9},{9,1},{17,25},{25,17},{2,10},{10... | collective-permute-start | bytes 786440 | tf_op jit(solution)/shard_map/ppermute | solution.py:17
  2.8 4.3 %collective-permute-start.5 = (bf16[1,2,2,64,512]{4,3,2,1,0:T(8,128)(2,1)S(1)}, bf16[1,2,2,64,512]{4,3,2,1,0:T(8,128)(2,1)S(1)}, u32[]{:S(2)}, u32[]{:S(2)}) collective-permute-start(bf16[1,2,2,64,512]{4,3,2,1,0:T(8,128)(2,1)S(1)} %get-tuple-element.24), channel_id=1, source_target_pairs={{0,8},{8,0},{16,24},{24,16},{1,9},{9,1},{17,25},{25,17},{2,10},{10... | collective-permute-start | bytes 786440 | tf_op jit(solution)/shard_map/ppermute | solution.py:17
  2.9 9.9 %collective-permute-start = (bf16[2,2,2,64,512]{4,3,2,0,1:T(8,128)(2,1)S(1)}, bf16[2,2,2,64,512]{4,3,2,0,1:T(8,128)(2,1)S(1)}, u32[]{:S(2)}, u32[]{:S(2)}) collective-permute-start(bf16[2,2,2,64,512]{4,3,2,0,1:T(8,128)(2,1)S(1)} %copy.10), channel_id=1, source_target_pairs={{0,8},{8,0},{16,24},{24,16},{1,9},{9,1},{17,25},{25,17},{2,10},{10... | collective-permute-start | bytes 1572872 | tf_op jit(solution)/shard_map/ppermute | solution.py:17
  4.1 5.4 %collective-permute-start.10 = (bf16[1,1,1,64,512]{4,3,2,1,0:T(8,128)(2,1)S(1)}, bf16[1,1,1,64,512]{4,3,2,1,0:T(8,128)(2,1)S(1)}, u32[]{:S(2)}, u32[]{:S(2)}) collective-permute-start(bf16[1,1,1,64,512]{4,3,2,1,0:T(8,128)(2,1)S(1)} %fusion.12), channel_id=1, source_target_pairs={{0,16},{8,24},{16,0},{24,8},{1,17},{9,25},{17,1},{25,9},{2,18},{10... | collective-permute-start | bytes 196616 | tf_op jit(solution)/shard_map/ppermute | solution.py:17
  7.0 7.8 %collective-permute-start.12 = (bf16[1,1,1,64,512]{4,3,2,1,0:T(8,128)(2,1)S(1)}, bf16[1,1,1,64,512]{4,3,2,1,0:T(8,128)(2,1)S(1)}, u32[]{:S(2)}, u32[]{:S(2)}) collective-permute-start(bf16[1,1,1,64,512]{4,3,2,1,0:T(8,128)(2,1)S(1)} %get-tuple-element.50), channel_id=1, source_target_pairs={{0,16},{8,24},{16,0},{24,8},{1,17},{9,25},{17,1},{25,9},{2,18},{10... | collective-permute-start | bytes 196616 | tf_op jit(solution)/shard_map/ppermute | solution.py:17
  7.2 20.3 %copy-start = (f32[1,512,512]{2,1,0:T(8,128)S(1)}, f32[1,512,512]{2,1,0:T(8,128)}, u32[]{:S(2)}) copy-start(f32[1,512,512]{2,1,0:T(8,128)} %accum.1) | copy-start | bytes 3145732
  7.2 20.3 %copy-start.3 = (bf16[1,512,512]{2,1,0:T(8,128)(2,1)S(1)}, bf16[1,512,512]{2,1,0:T(8,128)(2,1)}, u32[]{:S(2)}) copy-start(bf16[1,512,512]{2,1,0:T(8,128)(2,1)} %refs_8_.1) | copy-start | bytes 1572868
  7.2 20.3 %copy-start.4 = (bf16[1,512,512]{2,1,0:T(8,128)(2,1)S(1)}, bf16[1,512,512]{2,1,0:T(8,128)(2,1)}, u32[]{:S(2)}) copy-start(bf16[1,512,512]{2,1,0:T(8,128)(2,1)} %refs_9_.1) | copy-start | bytes 1572868
  7.2 9.0 %collective-permute-start.6 = (bf16[1,1,2,64,512]{4,3,2,1,0:T(8,128)(2,1)S(1)}, bf16[1,1,2,64,512]{4,3,2,1,0:T(8,128)(2,1)S(1)}, u32[]{:S(2)}, u32[]{:S(2)}) collective-permute-start(bf16[1,1,2,64,512]{4,3,2,1,0:T(8,128)(2,1)S(1)} %get-tuple-element.46), channel_id=1, source_target_pairs={{0,16},{8,24},{16,0},{24,8},{1,17},{9,25},{17,1},{25,9},{2,18},{10... | collective-permute-start | bytes 393224 | tf_op jit(solution)/shard_map/ppermute | solution.py:17
  9.5 12.8 %collective-permute-start.11 = (bf16[1,64,512]{2,1,0:T(8,128)(2,1)S(1)}, bf16[1,64,512]{2,1,0:T(8,128)(2,1)S(1)}, u32[]{:S(2)}, u32[]{:S(2)}) collective-permute-start(bf16[1,64,512]{2,1,0:T(8,128)(2,1)S(1)} %fusion.9), channel_id=1, source_target_pairs={{0,4},{1,5},{2,6},{3,7},{4,0},{5,1},{6,2},{7,3},{8,12},{9,13},{10,... | collective-permute-start | bytes 196616 | tf_op jit(solution)/shard_map/ppermute | solution.py:17
  13.0 7.1 %collective-permute-start.1 = (bf16[2,1,2,64,512]{4,3,2,1,0:T(8,128)(2,1)S(1)}, bf16[2,1,2,64,512]{4,3,2,1,0:T(8,128)(2,1)S(1)}, u32[]{:S(2)}, u32[]{:S(2)}) collective-permute-start(bf16[2,1,2,64,512]{4,3,2,1,0:T(8,128)(2,1)S(1)} %get-tuple-element.40), channel_id=1, source_target_pairs={{0,16},{8,24},{16,0},{24,8},{1,17},{9,25},{17,1},{25,9},{2,18},{10... | collective-permute-start | bytes 786440 | tf_op jit(solution)/shard_map/ppermute | solution.py:17
  14.9 25.9 %copy-start.1 = (f32[1,512,512]{2,1,0:T(8,128)S(1)}, f32[1,512,512]{2,1,0:T(8,128)}, u32[]{:S(2)}) copy-start(f32[1,512,512]{2,1,0:T(8,128)} %left.1) | copy-start | bytes 3145732
  14.9 25.9 %copy-start.2 = (f32[1,512,512]{2,1,0:T(8,128)S(1)}, f32[1,512,512]{2,1,0:T(8,128)}, u32[]{:S(2)}) copy-start(f32[1,512,512]{2,1,0:T(8,128)} %right.1) | copy-start | bytes 3145732
  14.9 8.3 %collective-permute-start.13 = (bf16[1,64,512]{2,1,0:T(8,128)(2,1)S(1)}, bf16[1,64,512]{2,1,0:T(8,128)(2,1)S(1)}, u32[]{:S(2)}, u32[]{:S(2)}) collective-permute-start(bf16[1,64,512]{2,1,0:T(8,128)(2,1)S(1)} %fusion.11), channel_id=1, source_target_pairs={{0,5},{1,4},{2,7},{3,6},{4,1},{5,0},{6,3},{7,2},{8,13},{9,12},{10,... | collective-permute-start | bytes 196616 | tf_op jit(solution)/shard_map/ppermute | solution.py:17
  16.3 7.6 %collective-permute-start.8 = (bf16[1,64,512]{2,1,0:T(8,128)(2,1)S(1)}, bf16[1,64,512]{2,1,0:T(8,128)(2,1)S(1)}, u32[]{:S(2)}, u32[]{:S(2)}) collective-permute-start(bf16[1,64,512]{2,1,0:T(8,128)(2,1)S(1)} %get-tuple-element.48), channel_id=1, source_target_pairs={{0,7},{1,6},{2,5},{3,4},{4,3},{5,2},{6,1},{7,0},{8,15},{9,14},{10,... | collective-permute-start | bytes 196616 | tf_op jit(solution)/shard_map/ppermute | solution.py:17
  19.9 6.2 %collective-permute-start.7 = (bf16[1,64,512]{2,1,0:T(8,128)(2,1)S(1)}, bf16[1,64,512]{2,1,0:T(8,128)(2,1)S(1)}, u32[]{:S(2)}, u32[]{:S(2)}) collective-permute-start(bf16[1,64,512]{2,1,0:T(8,128)(2,1)S(1)} %get-tuple-element.49), channel_id=1, source_target_pairs={{0,6},{1,7},{2,4},{3,5},{4,2},{5,3},{6,0},{7,1},{8,14},{9,15},{10,... | collective-permute-start | bytes 196616 | tf_op jit(solution)/shard_map/ppermute | solution.py:17
  20.2 6.0 %collective-permute-start.4 = (bf16[1,64,512]{2,1,0:T(8,128)(2,1)S(1)}, bf16[1,64,512]{2,1,0:T(8,128)(2,1)S(1)}, u32[]{:S(2)}, u32[]{:S(2)}) collective-permute-start(bf16[1,64,512]{2,1,0:T(8,128)(2,1)S(1)} %get-tuple-element.42), channel_id=1, source_target_pairs={{0,3},{1,2},{2,1},{3,0},{4,7},{5,6},{6,5},{7,4},{8,11},{9,10},{10,... | collective-permute-start | bytes 196616 | tf_op jit(solution)/shard_map/ppermute | solution.py:17
  22.3 4.6 %collective-permute-start.3 = (bf16[1,64,512]{2,1,0:T(8,128)(2,1)S(1)}, bf16[1,64,512]{2,1,0:T(8,128)(2,1)S(1)}, u32[]{:S(2)}, u32[]{:S(2)}) collective-permute-start(bf16[1,64,512]{2,1,0:T(8,128)(2,1)S(1)} %get-tuple-element.43), channel_id=1, source_target_pairs={{0,2},{1,3},{2,0},{3,1},{4,6},{5,7},{6,4},{7,5},{8,10},{9,11},{10,... | collective-permute-start | bytes 196616 | tf_op jit(solution)/shard_map/ppermute | solution.py:17
  23.2 4.3 %collective-permute-start.2 = (bf16[1,64,512]{2,1,0:T(8,128)(2,1)S(1)}, bf16[1,64,512]{2,1,0:T(8,128)(2,1)S(1)}, u32[]{:S(2)}, u32[]{:S(2)}) collective-permute-start(bf16[1,64,512]{2,1,0:T(8,128)(2,1)S(1)} %get-tuple-element.44), channel_id=1, source_target_pairs={{0,1},{1,0},{2,3},{3,2},{4,5},{5,4},{6,7},{7,6},{8,9},{9,8},{10,11... | collective-permute-start | bytes 196616 | tf_op jit(solution)/shard_map/ppermute | solution.py:17
  28.8 8.6 %collective-permute-start.14 = (bf16[1,64,512]{2,1,0:T(8,128)(2,1)S(1)}, bf16[1,64,512]{2,1,0:T(8,128)(2,1)S(1)}, u32[]{:S(2)}, u32[]{:S(2)}) collective-permute-start(bf16[1,64,512]{2,1,0:T(8,128)(2,1)S(1)} %get-tuple-element.29), channel_id=1, source_target_pairs={{0,1},{1,2},{2,3},{3,4},{4,5},{5,6},{6,7},{7,0},{8,9},{9,10},{10,1... | collective-permute-start | bytes 196616 | tf_op jit(solution)/shard_map/ppermute | solution.py:225
  29.5 8.9 %collective-permute-start.15 = (bf16[1,64,512]{2,1,0:T(8,128)(2,1)S(1)}, bf16[1,64,512]{2,1,0:T(8,128)(2,1)S(1)}, u32[]{:S(2)}, u32[]{:S(2)}) collective-permute-start(bf16[1,64,512]{2,1,0:T(8,128)(2,1)S(1)} %get-tuple-element.30), channel_id=1, source_target_pairs={{0,2},{1,3},{2,4},{3,5},{4,6},{5,7},{6,0},{7,1},{8,10},{9,11},{10,... | collective-permute-start | bytes 196616 | tf_op jit(solution)/shard_map/ppermute | solution.py:225
  30.5 12.2 %collective-permute-start.16 = (bf16[1,64,512]{2,1,0:T(8,128)(2,1)S(1)}, bf16[1,64,512]{2,1,0:T(8,128)(2,1)S(1)}, u32[]{:S(2)}, u32[]{:S(2)}) collective-permute-start(bf16[1,64,512]{2,1,0:T(8,128)(2,1)S(1)} %get-tuple-element.31), channel_id=1, source_target_pairs={{0,3},{1,4},{2,5},{3,6},{4,7},{5,0},{6,1},{7,2},{8,11},{9,12},{10,... | collective-permute-start | bytes 196616 | tf_op jit(solution)/shard_map/ppermute | solution.py:225
  34.5 8.1 %collective-permute-start.17 = (bf16[1,64,512]{2,1,0:T(8,128)(2,1)S(1)}, bf16[1,64,512]{2,1,0:T(8,128)(2,1)S(1)}, u32[]{:S(2)}, u32[]{:S(2)}) collective-permute-start(bf16[1,64,512]{2,1,0:T(8,128)(2,1)S(1)} %get-tuple-element.32), channel_id=1, source_target_pairs={{0,4},{1,5},{2,6},{3,7},{4,0},{5,1},{6,2},{7,3},{8,12},{9,13},{10,... | collective-permute-start | bytes 196616 | tf_op jit(solution)/shard_map/ppermute | solution.py:225
  35.2 7.5 %collective-permute-start.18 = (bf16[1,64,512]{2,1,0:T(8,128)(2,1)S(1)}, bf16[1,64,512]{2,1,0:T(8,128)(2,1)S(1)}, u32[]{:S(2)}, u32[]{:S(2)}) collective-permute-start(bf16[1,64,512]{2,1,0:T(8,128)(2,1)S(1)} %get-tuple-element.33), channel_id=1, source_target_pairs={{0,5},{1,6},{2,7},{3,0},{4,1},{5,2},{6,3},{7,4},{8,13},{9,14},{10,... | collective-permute-start | bytes 196616 | tf_op jit(solution)/shard_map/ppermute | solution.py:225
  37.4 5.3 %collective-permute-start.19 = (bf16[1,64,512]{2,1,0:T(8,128)(2,1)S(1)}, bf16[1,64,512]{2,1,0:T(8,128)(2,1)S(1)}, u32[]{:S(2)}, u32[]{:S(2)}) collective-permute-start(bf16[1,64,512]{2,1,0:T(8,128)(2,1)S(1)} %get-tuple-element.34), channel_id=1, source_target_pairs={{0,6},{1,7},{2,0},{3,1},{4,2},{5,3},{6,4},{7,5},{8,14},{9,15},{10,... | collective-permute-start | bytes 196616 | tf_op jit(solution)/shard_map/ppermute | solution.py:225
  38.4 4.3 %collective-permute-start.20 = (bf16[1,64,512]{2,1,0:T(8,128)(2,1)S(1)}, bf16[1,64,512]{2,1,0:T(8,128)(2,1)S(1)}, u32[]{:S(2)}, u32[]{:S(2)}) collective-permute-start(bf16[1,64,512]{2,1,0:T(8,128)(2,1)S(1)} %get-tuple-element.35), channel_id=1, source_target_pairs={{0,7},{1,0},{2,1},{3,2},{4,3},{5,4},{6,5},{7,6},{8,15},{9,8},{10,9... | collective-permute-start | bytes 196616 | tf_op jit(solution)/shard_map/ppermute | solution.py:225

commit v8 on v7

--- a/solution.py
+++ b/solution.py
@@ -77,22 +77,22 @@
 
 def main_kernel(spots, *refs):
     ins, (left_root, right_root, accum) = refs[: len(spots)], refs[len(spots) : len(spots) + 3]
-    outs, (block_out, scaled) = refs[len(spots) + 3 : -2], refs[-2:]
+    outs, block_out = refs[len(spots) + 3 : -1], refs[-1]
     rows = ins[0].shape[-2]
 
     for ref, (k, e) in zip(ins, spots):
         block_out[rows_of(peer(k, e), rows)] = ref[0]
     b = block_out[...]
-    half = jnp.dot(left_root[0], b, preferred_element_type=jnp.float32).astype(jnp.bfloat16)
+    root = jnp.concatenate([left_root[0, rows_of(further(d), rows)] for d in range(len(outs))])
+    half = jnp.dot(root, b, preferred_element_type=jnp.float32).astype(jnp.bfloat16)
     precond = jnp.dot(half, right_root[0], preferred_element_type=jnp.float32)
     wide = b.astype(jnp.float32)
     square = wide * wide
     ada_sq = jnp.sum(square / (accum[0] + square))
     pre_sq = jnp.sum(precond * precond)
     ratio = jnp.sqrt(ada_sq) / jnp.sqrt(pre_sq + 1e-06)
-    scaled[...] = (ratio * precond).astype(jnp.bfloat16)
     for d, ref in enumerate(outs):
-        ref[0] = scaled[rows_of(further(d), rows)]
+        ref[0] = (ratio * precond[d * rows : (d + 1) * rows]).astype(jnp.bfloat16)
 
 
 def precondition(pieces, spots, left_root, right_root, accum):
@@ -103,7 +103,6 @@
         out_shape=[piece] * len(pieces) + [jax.ShapeDtypeStruct((side, side), jnp.bfloat16)],
         in_specs=[VMEM] * (len(pieces) + 3),
         out_specs=[VMEM] * (len(pieces) + 1),
-        scratch_shapes=[pltpu.VMEM((side, side), jnp.bfloat16)],
         compiler_params=pltpu.CompilerParams(vmem_limit_bytes=16 * MIB),
         cost_estimate=pl.CostEstimate(
             flops=4 * side**3, bytes_accessed=12 * side * side, transcendentals=0

time: 43.7 us -> 43.6 us (level)
  no operation moved by 1% of the time
where the time goes in v8:
time: 43.6 us; the launch traced here: 43.4 us
  starting transfers between devices  32 us (73%)
  Pallas kernels  5.51 us (13%)
  waiting for transfers between devices  4.54 us (10%)
  between operations  0.83 us (2%)
    ppermute x14, starting transfers between devices, swap(): return lax.ppermute(x, axis, [(i, i ^ bit) for i in range(n)])  20.1 us
    ppermute x7, starting transfers between devices, body(): lax.ppermute(a, 'fsdp', [(i, (i + d) % fsdp_count) for i in range(fsdp_co...  11.9 us
    ppermute x14, waiting for transfers between devices, swap(): return lax.ppermute(x, axis, [(i, i ^ bit) for i in range(n)])  4.51 us
    pallas_call x1, Pallas kernels, statistics(): pl.pallas_call(stats_kernel, out_shape=(shape,) * 3, in_specs=[VMEM] * 4,...  1.85 us
    pallas_call x1, Pallas kernels, pick(): pl.pallas_call(functools.partial(pick_kernel, groups), out_shape=shapes *...  1.61 us
    pallas_call x1, Pallas kernels, precondition(): pl.pallas_call(functools.partial(main_kernel, spots), out_shape=[piece] *...  1.24 us
  transfers between devices with their start and end apart: 21, of which 6 were waited for; matrix products, arithmetic and copies ran while one was open for 1% of the time, Pallas kernels for 4%

profile of v8, /device:TPU:0, one launch (start us, length us, event | category | flops | bytes accessed | tf_op | source)
XLA Modules:
  0.0 43.4 jit_solution(7603311340466101067)
XLA Ops:
  0.6 1.6 %pick.1 = (bf16[2,2,2,64,512]{4,3,2,1,0:T(8,128)(2,1)S(1)}, bf16[1,2,2,64,512]{4,3,2,1,0:T(8,128)(2,1)S(1)}, bf16[1,2,2,64,512]{4,3,2,1,0:T(8,128)(2,1)S(1)}, bf...) custom-call(bf16[1,2,64,8192]{3,2,1,0:T(8,128)(2,1)} %grads.1), custom_call_target="tpu_custom_call" | custom-call | bytes 4194304 | tf_op jit(solution)/shard_map/pick/pallas_call | solution.py:61
  2.3 0.5 %collective-permute-start.9 = (bf16[1,2,2,64,512]{4,3,1,2,0:T(8,128)(2,1)S(1)}, bf16[1,2,2,64,512]{4,3,1,2,0:T(8,128)(2,1)S(1)}, u32[]{:S(2)}, u32[]{:S(2)}) collective-permute-start(bf16[1,2,2,64,512]{4,3,1,2,0:T(8,128)(2,1)S(1)} %copy.13), channel_id=1, source_target_pairs={{0,8},{8,0},{16,24},{24,16},{1,9},{9,1},{17,25},{25,17},{2,10},{10... | collective-permute-start | bytes 786440 | tf_op jit(solution)/shard_map/ppermute | solution.py:17
  2.8 0.1 collective-permute-start.5
  2.9 0.5 %collective-permute-start = (bf16[2,2,2,64,512]{4,3,2,0,1:T(8,128)(2,1)S(1)}, bf16[2,2,2,64,512]{4,3,2,0,1:T(8,128)(2,1)S(1)}, u32[]{:S(2)}, u32[]{:S(2)}) collective-permute-start(bf16[2,2,2,64,512]{4,3,2,0,1:T(8,128)(2,1)S(1)} %copy.10), channel_id=1, source_target_pairs={{0,8},{8,0},{16,24},{24,16},{1,9},{9,1},{17,25},{25,17},{2,10},{10... | collective-permute-start | bytes 1572872 | tf_op jit(solution)/shard_map/ppermute | solution.py:17
  3.5 0.5 %collective-permute-done.9 = bf16[1,2,2,64,512]{4,3,1,2,0:T(8,128)(2,1)S(1)} collective-permute-done((bf16[1,2,2,64,512]{4,3,1,2,0:T(8,128)(2,1)S(1)}, bf16[1,2,2,64,512]{4,3,1,2,0:T(8,128)(2,1)S(1)}, u32[]{:S(2)}, u32[]{:S(2)}) %collective-permute-start.9) | collective-permute-done | bytes 262176 | tf_op jit(solution)/shard_map/ppermute | solution.py:17
  4.1 3.0 %collective-permute-start.10 = (bf16[1,1,1,64,512]{4,3,2,1,0:T(8,128)(2,1)S(1)}, bf16[1,1,1,64,512]{4,3,2,1,0:T(8,128)(2,1)S(1)}, u32[]{:S(2)}, u32[]{:S(2)}) collective-permute-start(bf16[1,1,1,64,512]{4,3,2,1,0:T(8,128)(2,1)S(1)} %fusion.12), channel_id=1, source_target_pairs={{0,16},{8,24},{16,0},{24,8},{1,17},{9,25},{17,1},{25,9},{2,18},{10... | collective-permute-start | bytes 196616 | tf_op jit(solution)/shard_map/ppermute | solution.py:17
  7.0 0.1 collective-permute-start.12
  7.1 0.0 collective-permute-done.5
  7.1 0.1 fusion.1
  7.2 0.0 copy-start
  7.2 0.0 copy-start.3
  7.2 0.0 copy-start.4
  7.2 2.0 %collective-permute-start.6 = (bf16[1,1,2,64,512]{4,3,2,1,0:T(8,128)(2,1)S(1)}, bf16[1,1,2,64,512]{4,3,2,1,0:T(8,128)(2,1)S(1)}, u32[]{:S(2)}, u32[]{:S(2)}) collective-permute-start(bf16[1,1,2,64,512]{4,3,2,1,0:T(8,128)(2,1)S(1)} %get-tuple-element.46), channel_id=1, source_target_pairs={{0,16},{8,24},{16,0},{24,8},{1,17},{9,25},{17,1},{25,9},{2,18},{10... | collective-permute-start | bytes 393224 | tf_op jit(solution)/shard_map/ppermute | solution.py:17
  9.2 0.3 collective-permute-done.10
  9.5 3.3 %collective-permute-start.11 = (bf16[1,64,512]{2,1,0:T(8,128)(2,1)S(1)}, bf16[1,64,512]{2,1,0:T(8,128)(2,1)S(1)}, u32[]{:S(2)}, u32[]{:S(2)}) collective-permute-start(bf16[1,64,512]{2,1,0:T(8,128)(2,1)S(1)} %fusion.9), channel_id=1, source_target_pairs={{0,4},{1,5},{2,6},{3,7},{4,0},{5,1},{6,2},{7,3},{8,12},{9,13},{10,... | collective-permute-start | bytes 196616 | tf_op jit(solution)/shard_map/ppermute | solution.py:17
  12.8 0.1 fusion
  13.0 1.9 %collective-permute-start.1 = (bf16[2,1,2,64,512]{4,3,2,1,0:T(8,128)(2,1)S(1)}, bf16[2,1,2,64,512]{4,3,2,1,0:T(8,128)(2,1)S(1)}, u32[]{:S(2)}, u32[]{:S(2)}) collective-permute-start(bf16[2,1,2,64,512]{4,3,2,1,0:T(8,128)(2,1)S(1)} %get-tuple-element.40), channel_id=1, source_target_pairs={{0,16},{8,24},{16,0},{24,8},{1,17},{9,25},{17,1},{25,9},{2,18},{10... | collective-permute-start | bytes 786440 | tf_op jit(solution)/shard_map/ppermute | solution.py:17
  14.9 0.0 copy-start.1
  14.9 0.0 copy-start.2
  14.9 1.3 %collective-permute-start.13 = (bf16[1,64,512]{2,1,0:T(8,128)(2,1)S(1)}, bf16[1,64,512]{2,1,0:T(8,128)(2,1)S(1)}, u32[]{:S(2)}, u32[]{:S(2)}) collective-permute-start(bf16[1,64,512]{2,1,0:T(8,128)(2,1)S(1)} %fusion.11), channel_id=1, source_target_pairs={{0,5},{1,4},{2,7},{3,6},{4,1},{5,0},{6,3},{7,2},{8,13},{9,12},{10,... | collective-permute-start | bytes 196616 | tf_op jit(solution)/shard_map/ppermute | solution.py:17
  16.2 0.0 collective-permute-done.6
  16.3 3.6 %collective-permute-start.8 = (bf16[1,64,512]{2,1,0:T(8,128)(2,1)S(1)}, bf16[1,64,512]{2,1,0:T(8,128)(2,1)S(1)}, u32[]{:S(2)}, u32[]{:S(2)}) collective-permute-start(bf16[1,64,512]{2,1,0:T(8,128)(2,1)S(1)} %get-tuple-element.48), channel_id=1, source_target_pairs={{0,7},{1,6},{2,5},{3,4},{4,3},{5,2},{6,1},{7,0},{8,15},{9,14},{10,... | collective-permute-start | bytes 196616 | tf_op jit(solution)/shard_map/ppermute | solution.py:17
  19.9 0.2 collective-permute-start.7
  20.1 0.1 fusion.16
  20.2 2.1 %collective-permute-start.4 = (bf16[1,64,512]{2,1,0:T(8,128)(2,1)S(1)}, bf16[1,64,512]{2,1,0:T(8,128)(2,1)S(1)}, u32[]{:S(2)}, u32[]{:S(2)}) collective-permute-start(bf16[1,64,512]{2,1,0:T(8,128)(2,1)S(1)} %get-tuple-element.42), channel_id=1, source_target_pairs={{0,3},{1,2},{2,1},{3,0},{4,7},{5,6},{6,5},{7,4},{8,11},{9,10},{10,... | collective-permute-start | bytes 196616 | tf_op jit(solution)/shard_map/ppermute | solution.py:17
  22.3 1.0 %collective-permute-start.3 = (bf16[1,64,512]{2,1,0:T(8,128)(2,1)S(1)}, bf16[1,64,512]{2,1,0:T(8,128)(2,1)S(1)}, u32[]{:S(2)}, u32[]{:S(2)}) collective-permute-start(bf16[1,64,512]{2,1,0:T(8,128)(2,1)S(1)} %get-tuple-element.43), channel_id=1, source_target_pairs={{0,2},{1,3},{2,0},{3,1},{4,6},{5,7},{6,4},{7,5},{8,10},{9,11},{10,... | collective-permute-start | bytes 196616 | tf_op jit(solution)/shard_map/ppermute | solution.py:17
  23.2 0.0 collective-permute-done.13.refs_7_
  23.2 0.5 %collective-permute-start.2 = (bf16[1,64,512]{2,1,0:T(8,128)(2,1)S(1)}, bf16[1,64,512]{2,1,0:T(8,128)(2,1)S(1)}, u32[]{:S(2)}, u32[]{:S(2)}) collective-permute-start(bf16[1,64,512]{2,1,0:T(8,128)(2,1)S(1)} %get-tuple-element.44), channel_id=1, source_target_pairs={{0,1},{1,0},{2,3},{3,2},{4,5},{5,4},{6,7},{7,6},{8,9},{9,8},{10,11... | collective-permute-start | bytes 196616 | tf_op jit(solution)/shard_map/ppermute | solution.py:17
  23.8 0.1 collective-permute-done.8.refs_5_
  23.9 2.3 %collective-permute-done.7.refs_4_ = bf16[1,64,512]{2,1,0:T(8,128)(2,1)S(1)} collective-permute-done((bf16[1,64,512]{2,1,0:T(8,128)(2,1)S(1)}, bf16[1,64,512]{2,1,0:T(8,128)(2,1)S(1)}, u32[]{:S(2)}, u32[]{:S(2)}) %collective-permute-start.7) | collective-permute-done | bytes 65568 | tf_op jit(solution)/shard_map/ppermute | solution.py:17
  26.2 0.0 collective-permute-done.4.refs_3_
  26.2 0.7 %collective-permute-done.3.refs_2_ = bf16[1,64,512]{2,1,0:T(8,128)(2,1)S(1)} collective-permute-done((bf16[1,64,512]{2,1,0:T(8,128)(2,1)S(1)}, bf16[1,64,512]{2,1,0:T(8,128)(2,1)S(1)}, u32[]{:S(2)}, u32[]{:S(2)}) %collective-permute-start.3) | collective-permute-done | bytes 65568 | tf_op jit(solution)/shard_map/ppermute | solution.py:17
  26.9 0.6 %collective-permute-done.2.refs_1_ = bf16[1,64,512]{2,1,0:T(8,128)(2,1)S(1)} collective-permute-done((bf16[1,64,512]{2,1,0:T(8,128)(2,1)S(1)}, bf16[1,64,512]{2,1,0:T(8,128)(2,1)S(1)}, u32[]{:S(2)}, u32[]{:S(2)}) %collective-permute-start.2) | collective-permute-done | bytes 65568 | tf_op jit(solution)/shard_map/ppermute | solution.py:17
  27.5 1.2 %precondition.1 = (bf16[1,64,512]{2,1,0:T(8,128)(2,1)S(1)}, bf16[1,64,512]{2,1,0:T(8,128)(2,1)S(1)}, bf16[1,64,512]{2,1,0:T(8,128)(2,1)S(1)}, bf16[1,64,512]{2,1...) custom-call(bf16[1,64,512]{2,1,0:T(8,128)(2,1)S(1)} %get-tuple-eleme, ...), custom_call_target="tpu_custom_call" | custom-call | flops 536870912 | bytes 3145728 | tf_op jit(solution)/shard_map/precondition/pallas_call | solution.py:101
  28.8 0.7 %collective-permute-start.14 = (bf16[1,64,512]{2,1,0:T(8,128)(2,1)S(1)}, bf16[1,64,512]{2,1,0:T(8,128)(2,1)S(1)}, u32[]{:S(2)}, u32[]{:S(2)}) collective-permute-start(bf16[1,64,512]{2,1,0:T(8,128)(2,1)S(1)} %get-tuple-element.29), channel_id=1, source_target_pairs={{0,1},{1,2},{2,3},{3,4},{4,5},{5,6},{6,7},{7,0},{8,9},{9,10},{10,1... | collective-permute-start | bytes 196616 | tf_op jit(solution)/shard_map/ppermute | solution.py:224
  29.4 1.0 %collective-permute-start.15 = (bf16[1,64,512]{2,1,0:T(8,128)(2,1)S(1)}, bf16[1,64,512]{2,1,0:T(8,128)(2,1)S(1)}, u32[]{:S(2)}, u32[]{:S(2)}) collective-permute-start(bf16[1,64,512]{2,1,0:T(8,128)(2,1)S(1)} %get-tuple-element.30), channel_id=1, source_target_pairs={{0,2},{1,3},{2,4},{3,5},{4,6},{5,7},{6,0},{7,1},{8,10},{9,11},{10,... | collective-permute-start | bytes 196616 | tf_op jit(solution)/shard_map/ppermute | solution.py:224
  30.4 4.1 %collective-permute-start.16 = (bf16[1,64,512]{2,1,0:T(8,128)(2,1)S(1)}, bf16[1,64,512]{2,1,0:T(8,128)(2,1)S(1)}, u32[]{:S(2)}, u32[]{:S(2)}) collective-permute-start(bf16[1,64,512]{2,1,0:T(8,128)(2,1)S(1)} %get-tuple-element.31), channel_id=1, source_target_pairs={{0,3},{1,4},{2,5},{3,6},{4,7},{5,0},{6,1},{7,2},{8,11},{9,12},{10,... | collective-permute-start | bytes 196616 | tf_op jit(solution)/shard_map/ppermute | solution.py:224
  34.5 0.7 %collective-permute-start.17 = (bf16[1,64,512]{2,1,0:T(8,128)(2,1)S(1)}, bf16[1,64,512]{2,1,0:T(8,128)(2,1)S(1)}, u32[]{:S(2)}, u32[]{:S(2)}) collective-permute-start(bf16[1,64,512]{2,1,0:T(8,128)(2,1)S(1)} %get-tuple-element.32), channel_id=1, source_target_pairs={{0,4},{1,5},{2,6},{3,7},{4,0},{5,1},{6,2},{7,3},{8,12},{9,13},{10,... | collective-permute-start | bytes 196616 | tf_op jit(solution)/shard_map/ppermute | solution.py:224
  35.2 2.2 %collective-permute-start.18 = (bf16[1,64,512]{2,1,0:T(8,128)(2,1)S(1)}, bf16[1,64,512]{2,1,0:T(8,128)(2,1)S(1)}, u32[]{:S(2)}, u32[]{:S(2)}) collective-permute-start(bf16[1,64,512]{2,1,0:T(8,128)(2,1)S(1)} %get-tuple-element.33), channel_id=1, source_target_pairs={{0,5},{1,6},{2,7},{3,0},{4,1},{5,2},{6,3},{7,4},{8,13},{9,14},{10,... | collective-permute-start | bytes 196616 | tf_op jit(solution)/shard_map/ppermute | solution.py:224
  37.4 0.0 collective-permute-done.14.refs_1_
  37.4 1.0 %collective-permute-start.19 = (bf16[1,64,512]{2,1,0:T(8,128)(2,1)S(1)}, bf16[1,64,512]{2,1,0:T(8,128)(2,1)S(1)}, u32[]{:S(2)}, u32[]{:S(2)}) collective-permute-start(bf16[1,64,512]{2,1,0:T(8,128)(2,1)S(1)} %get-tuple-element.34), channel_id=1, source_target_pairs={{0,6},{1,7},{2,0},{3,1},{4,2},{5,3},{6,4},{7,5},{8,14},{9,15},{10,... | collective-permute-start | bytes 196616 | tf_op jit(solution)/shard_map/ppermute | solution.py:224
  38.4 0.0 collective-permute-done.15.refs_2_
  38.4 2.3 %collective-permute-start.20 = (bf16[1,64,512]{2,1,0:T(8,128)(2,1)S(1)}, bf16[1,64,512]{2,1,0:T(8,128)(2,1)S(1)}, u32[]{:S(2)}, u32[]{:S(2)}) collective-permute-start(bf16[1,64,512]{2,1,0:T(8,128)(2,1)S(1)} %get-tuple-element.35), channel_id=1, source_target_pairs={{0,7},{1,0},{2,1},{3,2},{4,3},{5,4},{6,5},{7,6},{8,15},{9,8},{10,9... | collective-permute-start | bytes 196616 | tf_op jit(solution)/shard_map/ppermute | solution.py:224
  40.7 1.9 %statistics.1 = (f32[1,512,512]{2,1,0:T(8,128)}, f32[1,512,512]{2,1,0:T(8,128)}, f32[1,512,512]{2,1,0:T(8,128)}) custom-call(bf16[512,512]{1,0:T(8,128)(2,1)S(1)} %get-tuple-element.36.block, f32[1,512,512]{2,1,0:T(8,128)S(1)} %copy-done.1, f32[1,512,512]{2,1,0:T(8,128)S(1)} %copy-done.2, f32[1,512,512]{2,1,0:T(8,128)S(1)} %copy-done), custom_call_target="tpu_custom_call" | custom-call | flops 536870912 | bytes 6815744 | tf_op jit(solution)/shard_map/statistics/pallas_call | solution.py:137
  42.6 0.0 collective-permute-done.17.refs_4_
  42.6 0.0 collective-permute-done.18.refs_5_
  42.6 0.0 collective-permute-done.20.refs_7_
  42.6 0.8 %assemble.1 = bf16[2,64,2048]{2,1,0:T(8,128)(2,1)} custom-call(bf16[1,64,512]{2,1,0:T(8,128)(2,1)S(1)} %get-tuple-element.28.refs_0_, bf16[1,64,512]{2,1,0:T(8,128)(2,1)S(1)} %collective-permute-done.14.refs_1_, bf16[1,64,512]{2,1,0:T(8,128)(2,1)S(1)} %collective-permute-done.15.refs_2_, bf16[1,64,512]{2,1,0:T(8,128)(2,1)S(1)} %collective-permute-done.16.refs_3_, ...), custom_call_target="tpu_custom_call" | custom-call | bytes 1048576 | tf_op jit(solution)/shard_map/assemble/pallas_call | solution.py:172
  (22 shorter events, 0.3 us)
Async XLA Ops:
  2.3 1.7 %collective-permute-start.9 = (bf16[1,2,2,64,512]{4,3,1,2,0:T(8,128)(2,1)S(1)}, bf16[1,2,2,64,512]{4,3,1,2,0:T(8,128)(2,1)S(1)}, u32[]{:S(2)}, u32[]{:S(2)}) collective-permute-start(bf16[1,2,2,64,512]{4,3,1,2,0:T(8,128)(2,1)S(1)} %copy.13), channel_id=1, source_target_pairs={{0,8},{8,0},{16,24},{24,16},{1,9},{9,1},{17,25},{25,17},{2,10},{10... | collective-permute-start | bytes 786440 | tf_op jit(solution)/shard_map/ppermute | solution.py:17
  2.8 4.3 %collective-permute-start.5 = (bf16[1,2,2,64,512]{4,3,2,1,0:T(8,128)(2,1)S(1)}, bf16[1,2,2,64,512]{4,3,2,1,0:T(8,128)(2,1)S(1)}, u32[]{:S(2)}, u32[]{:S(2)}) collective-permute-start(bf16[1,2,2,64,512]{4,3,2,1,0:T(8,128)(2,1)S(1)} %get-tuple-element.24), channel_id=1, source_target_pairs={{0,8},{8,0},{16,24},{24,16},{1,9},{9,1},{17,25},{25,17},{2,10},{10... | collective-permute-start | bytes 786440 | tf_op jit(solution)/shard_map/ppermute | solution.py:17
  2.9 9.9 %collective-permute-start = (bf16[2,2,2,64,512]{4,3,2,0,1:T(8,128)(2,1)S(1)}, bf16[2,2,2,64,512]{4,3,2,0,1:T(8,128)(2,1)S(1)}, u32[]{:S(2)}, u32[]{:S(2)}) collective-permute-start(bf16[2,2,2,64,512]{4,3,2,0,1:T(8,128)(2,1)S(1)} %copy.10), channel_id=1, source_target_pairs={{0,8},{8,0},{16,24},{24,16},{1,9},{9,1},{17,25},{25,17},{2,10},{10... | collective-permute-start | bytes 1572872 | tf_op jit(solution)/shard_map/ppermute | solution.py:17
  4.1 5.4 %collective-permute-start.10 = (bf16[1,1,1,64,512]{4,3,2,1,0:T(8,128)(2,1)S(1)}, bf16[1,1,1,64,512]{4,3,2,1,0:T(8,128)(2,1)S(1)}, u32[]{:S(2)}, u32[]{:S(2)}) collective-permute-start(bf16[1,1,1,64,512]{4,3,2,1,0:T(8,128)(2,1)S(1)} %fusion.12), channel_id=1, source_target_pairs={{0,16},{8,24},{16,0},{24,8},{1,17},{9,25},{17,1},{25,9},{2,18},{10... | collective-permute-start | bytes 196616 | tf_op jit(solution)/shard_map/ppermute | solution.py:17
  7.0 7.8 %collective-permute-start.12 = (bf16[1,1,1,64,512]{4,3,2,1,0:T(8,128)(2,1)S(1)}, bf16[1,1,1,64,512]{4,3,2,1,0:T(8,128)(2,1)S(1)}, u32[]{:S(2)}, u32[]{:S(2)}) collective-permute-start(bf16[1,1,1,64,512]{4,3,2,1,0:T(8,128)(2,1)S(1)} %get-tuple-element.50), channel_id=1, source_target_pairs={{0,16},{8,24},{16,0},{24,8},{1,17},{9,25},{17,1},{25,9},{2,18},{10... | collective-permute-start | bytes 196616 | tf_op jit(solution)/shard_map/ppermute | solution.py:17
  7.2 20.3 %copy-start = (f32[1,512,512]{2,1,0:T(8,128)S(1)}, f32[1,512,512]{2,1,0:T(8,128)}, u32[]{:S(2)}) copy-start(f32[1,512,512]{2,1,0:T(8,128)} %accum.1) | copy-start | bytes 3145732
  7.2 20.3 %copy-start.3 = (bf16[1,512,512]{2,1,0:T(8,128)(2,1)S(1)}, bf16[1,512,512]{2,1,0:T(8,128)(2,1)}, u32[]{:S(2)}) copy-start(bf16[1,512,512]{2,1,0:T(8,128)(2,1)} %refs_8_.1) | copy-start | bytes 1572868
  7.2 20.3 %copy-start.4 = (bf16[1,512,512]{2,1,0:T(8,128)(2,1)S(1)}, bf16[1,512,512]{2,1,0:T(8,128)(2,1)}, u32[]{:S(2)}) copy-start(bf16[1,512,512]{2,1,0:T(8,128)(2,1)} %refs_9_.1) | copy-start | bytes 1572868
  7.2 9.0 %collective-permute-start.6 = (bf16[1,1,2,64,512]{4,3,2,1,0:T(8,128)(2,1)S(1)}, bf16[1,1,2,64,512]{4,3,2,1,0:T(8,128)(2,1)S(1)}, u32[]{:S(2)}, u32[]{:S(2)}) collective-permute-start(bf16[1,1,2,64,512]{4,3,2,1,0:T(8,128)(2,1)S(1)} %get-tuple-element.46), channel_id=1, source_target_pairs={{0,16},{8,24},{16,0},{24,8},{1,17},{9,25},{17,1},{25,9},{2,18},{10... | collective-permute-start | bytes 393224 | tf_op jit(solution)/shard_map/ppermute | solution.py:17
  9.5 12.8 %collective-permute-start.11 = (bf16[1,64,512]{2,1,0:T(8,128)(2,1)S(1)}, bf16[1,64,512]{2,1,0:T(8,128)(2,1)S(1)}, u32[]{:S(2)}, u32[]{:S(2)}) collective-permute-start(bf16[1,64,512]{2,1,0:T(8,128)(2,1)S(1)} %fusion.9), channel_id=1, source_target_pairs={{0,4},{1,5},{2,6},{3,7},{4,0},{5,1},{6,2},{7,3},{8,12},{9,13},{10,... | collective-permute-start | bytes 196616 | tf_op jit(solution)/shard_map/ppermute | solution.py:17
  13.0 7.1 %collective-permute-start.1 = (bf16[2,1,2,64,512]{4,3,2,1,0:T(8,128)(2,1)S(1)}, bf16[2,1,2,64,512]{4,3,2,1,0:T(8,128)(2,1)S(1)}, u32[]{:S(2)}, u32[]{:S(2)}) collective-permute-start(bf16[2,1,2,64,512]{4,3,2,1,0:T(8,128)(2,1)S(1)} %get-tuple-element.40), channel_id=1, source_target_pairs={{0,16},{8,24},{16,0},{24,8},{1,17},{9,25},{17,1},{25,9},{2,18},{10... | collective-permute-start | bytes 786440 | tf_op jit(solution)/shard_map/ppermute | solution.py:17
  14.9 25.8 %copy-start.1 = (f32[1,512,512]{2,1,0:T(8,128)S(1)}, f32[1,512,512]{2,1,0:T(8,128)}, u32[]{:S(2)}) copy-start(f32[1,512,512]{2,1,0:T(8,128)} %left.1) | copy-start | bytes 3145732
  14.9 25.8 %copy-start.2 = (f32[1,512,512]{2,1,0:T(8,128)S(1)}, f32[1,512,512]{2,1,0:T(8,128)}, u32[]{:S(2)}) copy-start(f32[1,512,512]{2,1,0:T(8,128)} %right.1) | copy-start | bytes 3145732
  14.9 8.3 %collective-permute-start.13 = (bf16[1,64,512]{2,1,0:T(8,128)(2,1)S(1)}, bf16[1,64,512]{2,1,0:T(8,128)(2,1)S(1)}, u32[]{:S(2)}, u32[]{:S(2)}) collective-permute-start(bf16[1,64,512]{2,1,0:T(8,128)(2,1)S(1)} %fusion.11), channel_id=1, source_target_pairs={{0,5},{1,4},{2,7},{3,6},{4,1},{5,0},{6,3},{7,2},{8,13},{9,12},{10,... | collective-permute-start | bytes 196616 | tf_op jit(solution)/shard_map/ppermute | solution.py:17
  16.3 7.6 %collective-permute-start.8 = (bf16[1,64,512]{2,1,0:T(8,128)(2,1)S(1)}, bf16[1,64,512]{2,1,0:T(8,128)(2,1)S(1)}, u32[]{:S(2)}, u32[]{:S(2)}) collective-permute-start(bf16[1,64,512]{2,1,0:T(8,128)(2,1)S(1)} %get-tuple-element.48), channel_id=1, source_target_pairs={{0,7},{1,6},{2,5},{3,4},{4,3},{5,2},{6,1},{7,0},{8,15},{9,14},{10,... | collective-permute-start | bytes 196616 | tf_op jit(solution)/shard_map/ppermute | solution.py:17
  19.9 6.2 %collective-permute-start.7 = (bf16[1,64,512]{2,1,0:T(8,128)(2,1)S(1)}, bf16[1,64,512]{2,1,0:T(8,128)(2,1)S(1)}, u32[]{:S(2)}, u32[]{:S(2)}) collective-permute-start(bf16[1,64,512]{2,1,0:T(8,128)(2,1)S(1)} %get-tuple-element.49), channel_id=1, source_target_pairs={{0,6},{1,7},{2,4},{3,5},{4,2},{5,3},{6,0},{7,1},{8,14},{9,15},{10,... | collective-permute-start | bytes 196616 | tf_op jit(solution)/shard_map/ppermute | solution.py:17
  20.2 6.0 %collective-permute-start.4 = (bf16[1,64,512]{2,1,0:T(8,128)(2,1)S(1)}, bf16[1,64,512]{2,1,0:T(8,128)(2,1)S(1)}, u32[]{:S(2)}, u32[]{:S(2)}) collective-permute-start(bf16[1,64,512]{2,1,0:T(8,128)(2,1)S(1)} %get-tuple-element.42), channel_id=1, source_target_pairs={{0,3},{1,2},{2,1},{3,0},{4,7},{5,6},{6,5},{7,4},{8,11},{9,10},{10,... | collective-permute-start | bytes 196616 | tf_op jit(solution)/shard_map/ppermute | solution.py:17
  22.3 4.6 %collective-permute-start.3 = (bf16[1,64,512]{2,1,0:T(8,128)(2,1)S(1)}, bf16[1,64,512]{2,1,0:T(8,128)(2,1)S(1)}, u32[]{:S(2)}, u32[]{:S(2)}) collective-permute-start(bf16[1,64,512]{2,1,0:T(8,128)(2,1)S(1)} %get-tuple-element.43), channel_id=1, source_target_pairs={{0,2},{1,3},{2,0},{3,1},{4,6},{5,7},{6,4},{7,5},{8,10},{9,11},{10,... | collective-permute-start | bytes 196616 | tf_op jit(solution)/shard_map/ppermute | solution.py:17
  23.2 4.3 %collective-permute-start.2 = (bf16[1,64,512]{2,1,0:T(8,128)(2,1)S(1)}, bf16[1,64,512]{2,1,0:T(8,128)(2,1)S(1)}, u32[]{:S(2)}, u32[]{:S(2)}) collective-permute-start(bf16[1,64,512]{2,1,0:T(8,128)(2,1)S(1)} %get-tuple-element.44), channel_id=1, source_target_pairs={{0,1},{1,0},{2,3},{3,2},{4,5},{5,4},{6,7},{7,6},{8,9},{9,8},{10,11... | collective-permute-start | bytes 196616 | tf_op jit(solution)/shard_map/ppermute | solution.py:17
  28.8 8.6 %collective-permute-start.14 = (bf16[1,64,512]{2,1,0:T(8,128)(2,1)S(1)}, bf16[1,64,512]{2,1,0:T(8,128)(2,1)S(1)}, u32[]{:S(2)}, u32[]{:S(2)}) collective-permute-start(bf16[1,64,512]{2,1,0:T(8,128)(2,1)S(1)} %get-tuple-element.29), channel_id=1, source_target_pairs={{0,1},{1,2},{2,3},{3,4},{4,5},{5,6},{6,7},{7,0},{8,9},{9,10},{10,1... | collective-permute-start | bytes 196616 | tf_op jit(solution)/shard_map/ppermute | solution.py:224
  29.4 8.9 %collective-permute-start.15 = (bf16[1,64,512]{2,1,0:T(8,128)(2,1)S(1)}, bf16[1,64,512]{2,1,0:T(8,128)(2,1)S(1)}, u32[]{:S(2)}, u32[]{:S(2)}) collective-permute-start(bf16[1,64,512]{2,1,0:T(8,128)(2,1)S(1)} %get-tuple-element.30), channel_id=1, source_target_pairs={{0,2},{1,3},{2,4},{3,5},{4,6},{5,7},{6,0},{7,1},{8,10},{9,11},{10,... | collective-permute-start | bytes 196616 | tf_op jit(solution)/shard_map/ppermute | solution.py:224
  30.4 12.2 %collective-permute-start.16 = (bf16[1,64,512]{2,1,0:T(8,128)(2,1)S(1)}, bf16[1,64,512]{2,1,0:T(8,128)(2,1)S(1)}, u32[]{:S(2)}, u32[]{:S(2)}) collective-permute-start(bf16[1,64,512]{2,1,0:T(8,128)(2,1)S(1)} %get-tuple-element.31), channel_id=1, source_target_pairs={{0,3},{1,4},{2,5},{3,6},{4,7},{5,0},{6,1},{7,2},{8,11},{9,12},{10,... | collective-permute-start | bytes 196616 | tf_op jit(solution)/shard_map/ppermute | solution.py:224
  34.5 8.1 %collective-permute-start.17 = (bf16[1,64,512]{2,1,0:T(8,128)(2,1)S(1)}, bf16[1,64,512]{2,1,0:T(8,128)(2,1)S(1)}, u32[]{:S(2)}, u32[]{:S(2)}) collective-permute-start(bf16[1,64,512]{2,1,0:T(8,128)(2,1)S(1)} %get-tuple-element.32), channel_id=1, source_target_pairs={{0,4},{1,5},{2,6},{3,7},{4,0},{5,1},{6,2},{7,3},{8,12},{9,13},{10,... | collective-permute-start | bytes 196616 | tf_op jit(solution)/shard_map/ppermute | solution.py:224
  35.2 7.5 %collective-permute-start.18 = (bf16[1,64,512]{2,1,0:T(8,128)(2,1)S(1)}, bf16[1,64,512]{2,1,0:T(8,128)(2,1)S(1)}, u32[]{:S(2)}, u32[]{:S(2)}) collective-permute-start(bf16[1,64,512]{2,1,0:T(8,128)(2,1)S(1)} %get-tuple-element.33), channel_id=1, source_target_pairs={{0,5},{1,6},{2,7},{3,0},{4,1},{5,2},{6,3},{7,4},{8,13},{9,14},{10,... | collective-permute-start | bytes 196616 | tf_op jit(solution)/shard_map/ppermute | solution.py:224
  37.4 5.3 %collective-permute-start.19 = (bf16[1,64,512]{2,1,0:T(8,128)(2,1)S(1)}, bf16[1,64,512]{2,1,0:T(8,128)(2,1)S(1)}, u32[]{:S(2)}, u32[]{:S(2)}) collective-permute-start(bf16[1,64,512]{2,1,0:T(8,128)(2,1)S(1)} %get-tuple-element.34), channel_id=1, source_target_pairs={{0,6},{1,7},{2,0},{3,1},{4,2},{5,3},{6,4},{7,5},{8,14},{9,15},{10,... | collective-permute-start | bytes 196616 | tf_op jit(solution)/shard_map/ppermute | solution.py:224
  38.4 4.3 %collective-permute-start.20 = (bf16[1,64,512]{2,1,0:T(8,128)(2,1)S(1)}, bf16[1,64,512]{2,1,0:T(8,128)(2,1)S(1)}, u32[]{:S(2)}, u32[]{:S(2)}) collective-permute-start(bf16[1,64,512]{2,1,0:T(8,128)(2,1)S(1)} %get-tuple-element.35), channel_id=1, source_target_pairs={{0,7},{1,0},{2,1},{3,2},{4,3},{5,4},{6,5},{7,6},{8,15},{9,8},{10,9... | collective-permute-start | bytes 196616 | tf_op jit(solution)/shard_map/ppermute | solution.py:224
